TPU v7x, 256 devices: a whole 4x4x8 slice. The times are simulated.
256 devices in a mesh: ka: 16 (over x_lo, z), ga: 16 (over x_hi, y, core).
Axes of the slice: x: 4 (x_hi: 2, x_lo: 2; x = x_hi * 2 + x_lo), y: 4, z: 8, core: 2. Of those that a mesh axis runs over, the one named last changes fastest.
Arguments:
- initial_packet: float32 [32, 256, 64, 256], P('ka', 'ga'), may hold values from -6 to 6
- extents: int32 [32, 256], P('ka'), may hold values from 8 to 64, as said below
- potential: float32 [256, 64, 256], P('ga'), may hold values from 0 to 2
- coriolis_weight: float32 [256], P('ga'), may hold values from 0.005 to 0.03
- radial_kinetic: float32 [256, 256], replicated, as said below
- bond_kinetic: float32 [64, 64], replicated, as said below
- angle_kinetic: float32 [256, 256], replicated, as said below
Outputs:
- newest_packet: float32 [32, 256, 64, 256], P('ka', 'ga')
- former_packet: float32 [32, 256, 64, 256], P('ka', 'ga')
Inputs may be any that keep to these rules, and one draw needn't show every extreme that they name: Grid points with bond index below extents[K, R] are live; extents[K, R] ≤ 64 − floor(3K/2) for every K and R, and some slab of block 0 is live over all 64 points. `radial_kinetic`: symmetric. `bond_kinetic`: symmetric. `angle_kinetic`: symmetric.
All inputs are finite; a program needn't handle non-finite values.
Results may differ from a plain program's by a relative error of at most 0.0001.
Values sent between devices are 32-bit elements; how exact they have to be, the bound alone decides.
No kernel may reach another device: no remote copies, remote signals or barrier semaphores. Data moves between devices by JAX's collectives and lax.ppermute only.
A program may use at most 128 MiB of HBM per device.

v0:
```python
import jax
import jax.numpy as jnp
from jax import lax
from jax.sharding import PartitionSpec as P

ITERS = 3


energy_shift = 4.0
energy_spread = 7.0


def with_halo(block, sides, width):
    for axis, dim in sides:
        count = lax.axis_size(axis)
        forward = [(i, i + 1) for i in range(count - 1)]
        backward = [(target, source) for source, target in forward]
        low = lax.ppermute(
            lax.slice_in_dim(block, block.shape[dim] - width, None, axis=dim), axis, forward
        )
        high = lax.ppermute(lax.slice_in_dim(block, 0, width, axis=dim), axis, backward)
        block = jnp.concatenate([low, block, high], axis=dim)
    return block


def shards(
    initial_packet, extents, potential, coriolis_weight, radial_kinetic, bond_kinetic, angle_kinetic
):
    highest = lax.Precision.HIGHEST
    blocks = initial_packet.shape[0]
    slab_rows = initial_packet.shape[1]
    bonds = initial_packet.shape[2]
    total_blocks = blocks * lax.axis_size("ka")
    top_value = total_blocks - 1
    own_extents = lax.dynamic_slice_in_dim(extents, lax.axis_index("ga") * slab_rows, slab_rows, 1)
    bond_rows = jnp.arange(bonds, dtype=jnp.int32)
    live_mask = (bond_rows[None, None, :] < own_extents[:, :, None]).astype(jnp.float32)[..., None]
    kvalues = (lax.axis_index("ka") * blocks + jnp.arange(blocks, dtype=jnp.int32)).astype(
        jnp.float32
    )
    total = jnp.float32(top_value * (top_value + 1))
    ladder_upper = jnp.sqrt(total - kvalues * (kvalues + 1.0))[:, None, None, None]
    ladder_lower = jnp.sqrt(total - kvalues * (kvalues - 1.0))[:, None, None, None]
    weight_column = coriolis_weight[None, :, None, None]

    def radial_pass(packet):
        applied = jnp.einsum(
            "rs,ksqa->krqa",
            radial_kinetic,
            lax.all_to_all(packet, "ga", split_axis=2, concat_axis=1, tiled=True),
            precision=highest,
        )
        return lax.all_to_all(applied, "ga", split_axis=1, concat_axis=2, tiled=True)

    def local_terms(packet):
        return radial_pass(packet) + jnp.einsum(
            "qp,kspa->ksqa", bond_kinetic, packet, precision=highest
        )

    def apply_scaled(packet):
        padded = with_halo(packet, (("ka", 0),), 1)
        lower_block = padded[:-2]
        upper_block = padded[2:]
        result = local_terms(packet)
        result = result + jnp.einsum("ab,ksqb->ksqa", angle_kinetic, packet, precision=highest)
        coupling = ladder_upper * upper_block + ladder_lower * lower_block
        result = result + potential[None] * packet - weight_column * coupling
        return live_mask * (result - energy_shift * packet) / energy_spread

    start = live_mask * initial_packet
    previous = start
    current = apply_scaled(start)
    for count in range(ITERS - 1):
        nextone = 2.0 * apply_scaled(current) - previous
        previous = current
        current = nextone
    return (current, previous)


def solution(mesh):
    return jax.shard_map(
        shards,
        mesh=mesh,
        in_specs=(
            P("ka", "ga", None, None),
            P("ka", None),
            P("ga", None, None),
            P("ga"),
            P(),
            P(),
            P(),
        ),
        out_specs=(P("ka", "ga", None, None), P("ka", "ga", None, None)),
        check_vma=False,
    )
```

profile of v0, /device:TPU:1, one launch (start us, length us, event | category | flops | bytes accessed | tf_op | source)
XLA Modules:
  0.0 342.8 jit_solution(5725819781561364458)
XLA Ops:
  0.7 0.8 constant_dynamic-slice_fusion
  1.5 1.9 broadcast_multiply_fusion.1
  3.5 1.2 copy.42
  4.7 36.4 %all_to_all.108 = f32[2,16,64,256]{3,1,0,2:T(8,128)S(1)} all-to-all(f32[2,16,64,256]{3,1,0,2:T(8,128)S(1)} %copy.42), channel_id=1, replica_groups=mesh['ka'=16,'ga'=16] {'ga'}, dimensions={2} | all-to-all | bytes 4194304 | tf_op jit(solution)/shard_map/all_to_all | solution.py:50
  41.1 0.2 copy.44
  41.3 4.9 %convolution_bitcast_fusion.2 = f32[2,256,4,256]{1,3,2,0:T(8,128)} fusion(f32[2,256,4,256]{3,1,2,0:T(8,128)S(1)} %bitcast.89, f32[256,256]{1,0:T(8,128)S(1)} %copy-done), kind=kOutput, calls=%fused_computation.42 | convolution fusion | flops 1610612736 | bytes 4456448 | tf_op jit(solution)/shard_map/rs,ksqa->krqa/dot_general | solution.py:47
  46.3 3.0 copy.46
  49.3 5.3 %all-to-all-start.1 = ((f32[2,256,4,256]{3,2,0,1:T(4,128)}), f32[2,256,4,256]{3,2,0,1:T(4,128)}, u32[]{:S(2)}, u32[]{:S(2)}) async-start(f32[2,256,4,256]{3,2,0,1:T(4,128)} %copy.46), calls=%async_computation.1 | async-start | bytes 4194304 | tf_op jit(solution)/shard_map/all_to_all | solution.py:53
  54.6 1.5 fusion.50
  56.2 1.3 collective-permute-start
  57.4 5.6 %collective-permute-start.1 = (f32[1,16,64,256]{3,2,1,0:T(8,128)}, f32[1,16,64,256]{3,2,1,0:T(8,128)}, u32[]{:S(2)}, u32[]{:S(2)}) collective-permute-start(f32[1,16,64,256]{3,2,1,0:T(8,128)} %get-tuple-element.7), channel_id=1, source_target_pairs={{0,16},{16,32},{32,48},{48,64},{64,80},{80,96},{96,112},{112,128},... | collective-permute-start | bytes 3145736 | tf_op jit(solution)/shard_map/ppermute | solution.py:18
  63.1 3.2 fusion.36
  66.3 39.5 %all-to-all-done.1 = f32[2,256,4,256]{3,2,0,1:T(4,128)} async-done(((f32[2,256,4,256]{3,2,0,1:T(4,128)}), f32[2,256,4,256]{3,2,0,1:T(4,128)}, u32[]{:S(2)}, u32[]{:S(2)}) %all-to-all-start.1) | async-done | bytes 2097184 | tf_op jit(solution)/shard_map/all_to_all | solution.py:53
  105.7 2.3 copy.47
  108.0 2.7 copy.48
  110.7 3.0 all_to_all.85
  113.7 6.2 %broadcast_multiply_fusion = (f32[2,16,64,256]{3,2,1,0:T(8,128)S(1)}, f32[2,16,64,256]{3,2,1,0:T(8,128)}) fusion(f32[2,16,64,256]{3,2,1,0:T(8,128)S(1)} %broadcast_multiply_fusion.1, f32[1,16,64,256]{3,2,1,0:T(8,128)} %collective-permute-done.1, f32[2]{0:T(128)S(1)} %get-tuple-element.11, f32[1,16,64,256]{3,2,1,0:T(8,128)} %collective-permute-done, ...), kind=kOutput, calls=%fused_computation.43 | convolution fusion | flops 410517504 | bytes 13656144 | tf_op jit(solution)/shard_map/qp,kspa->ksqa/dot_general | solution.py:56
  119.9 1.2 copy.49
  121.2 34.3 %all_to_all.109 = f32[2,16,64,256]{3,1,0,2:T(8,128)S(1)} all-to-all(f32[2,16,64,256]{3,1,0,2:T(8,128)S(1)} %copy.49), channel_id=1, replica_groups=mesh['ka'=16,'ga'=16] {'ga'}, dimensions={2} | all-to-all | bytes 4194304 | tf_op jit(solution)/shard_map/all_to_all | solution.py:50
  155.5 0.2 copy.51
  155.7 5.0 %convolution_bitcast_fusion.1 = f32[2,256,4,256]{1,3,2,0:T(8,128)} fusion(f32[2,256,4,256]{3,1,2,0:T(8,128)S(1)} %bitcast.92, f32[256,256]{1,0:T(8,128)S(1)} %copy-done), kind=kOutput, calls=%fused_computation.41 | convolution fusion | flops 1610612736 | bytes 4456448 | tf_op jit(solution)/shard_map/rs,ksqa->krqa/dot_general | solution.py:47
  160.7 3.0 copy.53
  163.7 5.7 %all-to-all-start.3 = ((f32[2,256,4,256]{3,2,0,1:T(4,128)}), f32[2,256,4,256]{3,2,0,1:T(4,128)}, u32[]{:S(2)}, u32[]{:S(2)}) async-start(f32[2,256,4,256]{3,2,0,1:T(4,128)} %copy.53), calls=%async_computation.3 | async-start | bytes 4194304 | tf_op jit(solution)/shard_map/all_to_all | solution.py:53
  169.4 3.1 fusion.49
  172.5 1.4 collective-permute-start.2
  173.9 5.1 %collective-permute-start.3 = (f32[1,16,64,256]{3,2,1,0:T(8,128)}, f32[1,16,64,256]{3,2,1,0:T(8,128)}, u32[]{:S(2)}, u32[]{:S(2)}) collective-permute-start(f32[1,16,64,256]{3,2,1,0:T(8,128)} %get-tuple-element.5), channel_id=1, source_target_pairs={{0,16},{16,32},{32,48},{48,64},{64,80},{80,96},{96,112},{112,128},... | collective-permute-start | bytes 3145736 | tf_op jit(solution)/shard_map/ppermute | solution.py:18
  179.0 1.1 broadcast_multiply_fusion.2
  180.1 3.4 fusion.40
  183.5 31.5 %all-to-all-done.3 = f32[2,256,4,256]{3,2,0,1:T(4,128)} async-done(((f32[2,256,4,256]{3,2,0,1:T(4,128)}), f32[2,256,4,256]{3,2,0,1:T(4,128)}, u32[]{:S(2)}, u32[]{:S(2)}) %all-to-all-start.3) | async-done | bytes 2097184 | tf_op jit(solution)/shard_map/all_to_all | solution.py:53
  215.0 2.3 copy.54
  217.3 2.7 copy.55
  220.0 2.9 all_to_all.93
  222.9 7.7 %fusion.16 = f32[2,16,64,256]{3,2,1,0:T(8,128)S(1)} fusion(f32[2,16,64,256]{3,2,1,0:T(8,128)S(1)} %broadcast_multiply_fusion.1, f32[2,16,64,256]{3,2,1,0:T(8,128)} %copy-done.4, f32[1,16,64,256]{3,2,1,0:T(8,128)} %collective-permute-done.3, f32[1,16,64,256]{3,2,1,0:T(8,128)} %collective-permute-done.2, f32[2,16,64,256]{3,2,1,0:T(8,128)} %all_to_all.93, ...), kind=kOutput, calls=%fused_computation.19 | convolution fusion | flops 1619001344 | bytes 15999056 | tf_op jit(solution)/shard_map/ab,ksqb->ksqa/dot_general | solution.py:65
  230.7 1.2 copy.56
  232.0 56.8 %all_to_all.110 = f32[2,16,64,256]{3,1,0,2:T(8,128)S(1)} all-to-all(f32[2,16,64,256]{3,1,0,2:T(8,128)S(1)} %copy.56), channel_id=1, replica_groups=mesh['ka'=16,'ga'=16] {'ga'}, dimensions={2} | all-to-all | bytes 4194304 | tf_op jit(solution)/shard_map/all_to_all | solution.py:50
  288.7 0.2 copy.58
  288.9 3.6 %convolution_bitcast_fusion = f32[2,256,4,256]{1,3,2,0:T(8,128)S(1)} fusion(f32[2,256,4,256]{3,1,2,0:T(8,128)S(1)} %bitcast.95, f32[256,256]{1,0:T(8,128)S(1)} %copy-done), kind=kOutput, calls=%fused_computation.40 | convolution fusion | flops 1610612736 | bytes 4456448 | tf_op jit(solution)/shard_map/rs,ksqa->krqa/dot_general | solution.py:47
  292.6 2.0 copy.60
  294.5 5.5 %all-to-all-start.5 = ((f32[2,256,4,256]{3,2,0,1:T(4,128)}), f32[2,256,4,256]{3,2,0,1:T(4,128)}, u32[]{:S(2)}, u32[]{:S(2)}) async-start(f32[2,256,4,256]{3,2,0,1:T(4,128)} %copy.60), calls=%async_computation.5 | async-start | bytes 4194304 | tf_op jit(solution)/shard_map/all_to_all | solution.py:53
  300.0 1.6 fusion.48
  301.6 1.3 collective-permute-start.4
  302.9 5.1 %collective-permute-start.5 = (f32[1,16,64,256]{3,2,1,0:T(8,128)}, f32[1,16,64,256]{3,2,1,0:T(8,128)}, u32[]{:S(2)}, u32[]{:S(2)}) collective-permute-start(f32[1,16,64,256]{3,2,1,0:T(8,128)} %get-tuple-element.3), channel_id=1, source_target_pairs={{0,16},{16,32},{32,48},{48,64},{64,80},{80,96},{96,112},{112,128},... | collective-permute-start | bytes 3145736 | tf_op jit(solution)/shard_map/ppermute | solution.py:18
  308.0 3.4 fusion.38
  311.3 17.3 %all-to-all-done.5 = f32[2,256,4,256]{3,2,0,1:T(4,128)} async-done(((f32[2,256,4,256]{3,2,0,1:T(4,128)}), f32[2,256,4,256]{3,2,0,1:T(4,128)}, u32[]{:S(2)}, u32[]{:S(2)}) %all-to-all-start.5) | async-done | bytes 2097184 | tf_op jit(solution)/shard_map/all_to_all | solution.py:53
  328.7 2.3 copy.61
  330.9 2.7 copy.62
  333.6 2.9 all_to_all.101
  336.6 6.0 %fusion.7 = f32[2,16,64,256]{3,2,1,0:T(8,128)} fusion(f32[2,16,64,256]{3,2,1,0:T(8,128)S(1)} %copy-done.2, f32[1,16,64,256]{3,2,1,0:T(8,128)} %collective-permute-done.5, f32[1,16,64,256]{3,2,1,0:T(8,128)} %collective-permute-done.4, f32[2,16,64,256]{3,2,1,0:T(8,128)} %all_to_all.101, f32[2,16,256,64]{2,3,1,0:T(8,128)} %fusion.38, ...), kind=kOutput, calls=%fused_computation.8 | convolution fusion | flops 1619525632 | bytes 13901904 | tf_op jit(solution)/shard_map/ab,ksqb->ksqa/dot_general | solution.py:65
  (26 shorter events, 0.3 us)
Async XLA Ops:
  0.6 40.7 %copy-start = (f32[256,256]{1,0:T(8,128)S(1)}, f32[256,256]{1,0:T(8,128)}, u32[]{:S(2)}) copy-start(f32[256,256]{1,0:T(8,128)} %param.11) | copy-start | bytes 786436
  49.3 56.4 %all-to-all-start.1 = ((f32[2,256,4,256]{3,2,0,1:T(4,128)}), f32[2,256,4,256]{3,2,0,1:T(4,128)}, u32[]{:S(2)}, u32[]{:S(2)}) async-start(f32[2,256,4,256]{3,2,0,1:T(4,128)} %copy.46), calls=%async_computation.1 | async-start | bytes 4194304 | tf_op jit(solution)/shard_map/all_to_all | solution.py:53
  54.6 8.5 %copy-start.6 = (f32[256,256]{1,0:T(8,128)S(1)}, f32[256,256]{1,0:T(8,128)}, u32[]{:S(2)}) copy-start(f32[256,256]{1,0:T(8,128)} %param.13) | copy-start | bytes 786436
  56.2 57.5 %collective-permute-start = (f32[1,16,64,256]{3,2,1,0:T(8,128)}, f32[1,16,64,256]{3,2,1,0:T(8,128)}, u32[]{:S(2)}, u32[]{:S(2)}) collective-permute-start(f32[1,16,64,256]{3,2,1,0:T(8,128)} %get-tuple-element.6), channel_id=1, source_target_pairs={{16,0},{32,16},{48,32},{64,48},{80,64},{96,80},{112,96},{128,112},... | collective-permute-start | bytes 3145736 | tf_op jit(solution)/shard_map/ppermute | solution.py:21
  57.4 56.2 %collective-permute-start.1 = (f32[1,16,64,256]{3,2,1,0:T(8,128)}, f32[1,16,64,256]{3,2,1,0:T(8,128)}, u32[]{:S(2)}, u32[]{:S(2)}) collective-permute-start(f32[1,16,64,256]{3,2,1,0:T(8,128)} %get-tuple-element.7), channel_id=1, source_target_pairs={{0,16},{16,32},{32,48},{48,64},{64,80},{80,96},{96,112},{112,128},... | collective-permute-start | bytes 3145736 | tf_op jit(solution)/shard_map/ppermute | solution.py:18
  110.7 3.0 copy-start.5
  110.7 3.0 copy-start.7
  110.7 3.0 copy-start.8
  119.9 1.3 copy-start.4
  163.7 51.3 %all-to-all-start.3 = ((f32[2,256,4,256]{3,2,0,1:T(4,128)}), f32[2,256,4,256]{3,2,0,1:T(4,128)}, u32[]{:S(2)}, u32[]{:S(2)}) async-start(f32[2,256,4,256]{3,2,0,1:T(4,128)} %copy.53), calls=%async_computation.3 | async-start | bytes 4194304 | tf_op jit(solution)/shard_map/all_to_all | solution.py:53
  172.5 7.6 %copy-start.3 = (f32[2,16,64,256]{3,2,1,0:T(8,128)S(1)}, f32[2,16,64,256]{3,2,1,0:T(8,128)}, u32[]{:S(2)}) copy-start(f32[2,16,64,256]{3,2,1,0:T(8,128)} %get-tuple-element.9) | copy-start | bytes 6291460
  172.5 50.4 %collective-permute-start.2 = (f32[1,16,64,256]{3,2,1,0:T(8,128)}, f32[1,16,64,256]{3,2,1,0:T(8,128)}, u32[]{:S(2)}, u32[]{:S(2)}) collective-permute-start(f32[1,16,64,256]{3,2,1,0:T(8,128)} %get-tuple-element.4), channel_id=1, source_target_pairs={{16,0},{32,16},{48,32},{64,48},{80,64},{96,80},{112,96},{128,112},... | collective-permute-start | bytes 3145736 | tf_op jit(solution)/shard_map/ppermute | solution.py:21
  173.9 49.0 %collective-permute-start.3 = (f32[1,16,64,256]{3,2,1,0:T(8,128)}, f32[1,16,64,256]{3,2,1,0:T(8,128)}, u32[]{:S(2)}, u32[]{:S(2)}) collective-permute-start(f32[1,16,64,256]{3,2,1,0:T(8,128)} %get-tuple-element.5), channel_id=1, source_target_pairs={{0,16},{16,32},{32,48},{48,64},{64,80},{80,96},{96,112},{112,128},... | collective-permute-start | bytes 3145736 | tf_op jit(solution)/shard_map/ppermute | solution.py:18
  230.6 1.3 copy-start.1
  294.5 5.5 %copy-start.2 = (f32[2,16,64,256]{3,2,1,0:T(8,128)S(1)}, f32[2,16,64,256]{3,2,1,0:T(8,128)}, u32[]{:S(2)}) copy-start(f32[2,16,64,256]{3,2,1,0:T(8,128)} %copy-done.1) | copy-start | bytes 6291460
  294.5 34.1 %all-to-all-start.5 = ((f32[2,256,4,256]{3,2,0,1:T(4,128)}), f32[2,256,4,256]{3,2,0,1:T(4,128)}, u32[]{:S(2)}, u32[]{:S(2)}) async-start(f32[2,256,4,256]{3,2,0,1:T(4,128)} %copy.60), calls=%async_computation.5 | async-start | bytes 4194304 | tf_op jit(solution)/shard_map/all_to_all | solution.py:53
  301.6 34.9 %collective-permute-start.4 = (f32[1,16,64,256]{3,2,1,0:T(8,128)}, f32[1,16,64,256]{3,2,1,0:T(8,128)}, u32[]{:S(2)}, u32[]{:S(2)}) collective-permute-start(f32[1,16,64,256]{3,2,1,0:T(8,128)} %get-tuple-element.2), channel_id=1, source_target_pairs={{16,0},{32,16},{48,32},{64,48},{80,64},{96,80},{112,96},{128,112},... | collective-permute-start | bytes 3145736 | tf_op jit(solution)/shard_map/ppermute | solution.py:21
  302.9 33.7 %collective-permute-start.5 = (f32[1,16,64,256]{3,2,1,0:T(8,128)}, f32[1,16,64,256]{3,2,1,0:T(8,128)}, u32[]{:S(2)}, u32[]{:S(2)}) collective-permute-start(f32[1,16,64,256]{3,2,1,0:T(8,128)} %get-tuple-element.3), channel_id=1, source_target_pairs={{0,16},{16,32},{32,48},{48,64},{64,80},{80,96},{96,112},{112,128},... | collective-permute-start | bytes 3145736 | tf_op jit(solution)/shard_map/ppermute | solution.py:18
where the time goes:
time: 349 us; the launch traced here: 343 us
  blocking collectives  127 us (36%)
  waiting for transfers between devices  88.3 us (25%)
  local copies, waits for them, and re-layouts  43.4 us (12%)
  matrix products  43.4 us (12%)
  starting transfers between devices  36.2 us (10%)
    all_to_all x3, blocking collectives, radial_pass(): lax.all_to_all(packet, 'ga', split_axis=2, concat_axis=1, tiled=True)  127 us
    all_to_all x3, waiting for transfers between devices, radial_pass(): lax.all_to_all(applied, 'ga', split_axis=1, concat_axis=2, tiled=True)  88.3 us
    all_to_all x9, local copies, waits for them, and re-layouts, radial_pass(): lax.all_to_all(applied, 'ga', split_axis=1, concat_axis=2, tiled=True)  23.7 us
    dot_general x3, matrix products, apply_scaled(): jnp.einsum('ab,ksqb->ksqa', angle_kinetic, packet, precision=highest)  16.9 us
    all_to_all x3, starting transfers between devices, radial_pass(): lax.all_to_all(applied, 'ga', split_axis=1, concat_axis=2, tiled=True)  16.5 us
    ppermute x3, starting transfers between devices, with_halo(): lax.ppermute(lax.slice_in_dim(block, block.shape[dim] - width, None, axis...  15.8 us
    dot_general x3, matrix products, radial_pass(): jnp.einsum('rs,ksqa->krqa', radial_kinetic, lax.all_to_all(packet, 'ga',...  13.5 us
    dot_general x3, matrix products, local_terms(): jnp.einsum('qp,kspa->ksqa', bond_kinetic, packet, precision=highest)  13 us
  transfers between devices with their start and end apart: 9, of which 3 were waited for; matrix products, arithmetic and copies ran while one was open for 9% of the time, Pallas kernels for 0%

commit v1 on v0

v1 whole, which is shorter than its diff:
```python
import functools

import jax
import jax.numpy as jnp
from jax import lax
from jax.experimental import pallas as pl
from jax.experimental.pallas import tpu as pltpu
from jax.sharding import PartitionSpec as P

SHIFT = 4.0
SPREAD = 7.0
CHIPS = 8
OCT = 8
F32 = jnp.float32
BF16 = jnp.bfloat16


def split(x):
    high = x.astype(BF16)
    return high, (x - high.astype(F32)).astype(BF16)


def mm(a, b):
    return jnp.dot(a, b, preferred_element_type=F32)


def params():
    return pltpu.CompilerParams(vmem_limit_bytes=32 * 1024 * 1024)


def prep(ids, radial, bond, angle):
    def kernel(ids, radial, bond, angle, rad_h, rad_l, bond_cat, ang_h, ang_l, tmp, tmpb):
        ga = ids[0]
        chip = ids[1]

        def rows(ref, count, size, own):
            return jnp.concatenate(
                [ref[pl.ds(pl.multiple_of((i ^ own) * size, size), size), :] for i in range(count)], 0
            )

        tmp[...] = rows(radial, 16, 16, ga).T
        high, low = split(rows(tmp, 16, 16, ga) / SPREAD)
        rad_h[...] = high
        rad_l[...] = low
        tmpb[...] = rows(bond, 8, 8, chip).T
        high, low = split(rows(tmpb, 8, 8, chip) / SPREAD)
        bond_cat[...] = jnp.concatenate([high, high, low], 1)
        high, low = split(angle[...].T / SPREAD)
        ang_h[...] = high
        ang_l[...] = low

    big = jax.ShapeDtypeStruct((256, 256), BF16)
    vm = pl.BlockSpec(memory_space=pltpu.VMEM)
    return pl.pallas_call(
        kernel,
        out_shape=(big, big, jax.ShapeDtypeStruct((64, 192), BF16), big, big),
        in_specs=[pl.BlockSpec(memory_space=pltpu.SMEM), vm, vm, vm],
        out_specs=(vm,) * 5,
        scratch_shapes=[pltpu.VMEM((256, 256), F32), pltpu.VMEM((128, 64), F32)],
        compiler_params=params(),
        name="prep",
    )(ids, radial, jnp.pad(bond, ((0, 64), (0, 64))), angle)


def start(ids, ext, own, other):
    def kernel(ids, ext, own, other, whole, *pieces):
        j = pl.program_id(0)
        row = (j ^ ids[1]) * OCT + lax.broadcasted_iota(jnp.int32, (OCT, 256), 0)
        for r in range(32):
            x = own[0, r] if r < 16 else other[r - 16]
            x = jnp.where(row < ext[r], x, 0.0)
            whole[0, r] = x
            for i in range(1, CHIPS):
                @pl.when(j == i)
                def _(i=i, r=r, x=x):
                    pieces[i - 1][r] = x

    piece = pl.BlockSpec((32, OCT, 256), lambda j, ids, ext: (0, 0, 0))
    return pl.pallas_call(
        kernel,
        grid_spec=pltpu.PrefetchScalarGridSpec(
            num_scalar_prefetch=2,
            grid=(CHIPS,),
            in_specs=[
                pl.BlockSpec((1, 16, OCT, 256), lambda j, ids, ext: (ids[2], 0, j ^ ids[1], 0)),
                pl.BlockSpec((16, OCT, 256), lambda j, ids, ext: (0, j ^ ids[1], 0)),
            ],
            out_specs=[pl.BlockSpec((1, 32, OCT, 256), lambda j, ids, ext: (j, 0, 0, 0))] + [piece] * 7,
        ),
        out_shape=[jax.ShapeDtypeStruct((CHIPS, 32, OCT, 256), F32)]
        + [jax.ShapeDtypeStruct((32, OCT, 256), F32)] * 7,
        compiler_params=params(),
        name="start",
    )(ids, ext, own, other)


def local_terms(ids, ext, coef, cur, near, far, pot, bond_cat, ang_h, ang_l, prev):
    step = 4

    def kernel(ids, ext, coef, cur, near, far, pot, bond_cat, ang_h, ang_l, *rest):
        prev, outs = (rest[0], rest[1:]) if len(rest) > CHIPS else (None, rest)
        first = pl.program_id(0) * step
        line = lax.broadcasted_iota(jnp.int32, (64, 256), 0)
        row = ((line >> 3) ^ ids[1]) * OCT + (line & 7)
        xs = [cur[:, r].reshape(64, 256) for r in range(step)]
        high, low = split(jnp.concatenate(xs, 0))
        angle = mm(high, ang_h[...]) + mm(low, ang_h[...]) + mm(high, ang_l[...])
        for r in range(step):
            part = slice(r * 64, r * 64 + 64)
            stack = jnp.concatenate([high[part], low[part], high[part]], 0)
            total = angle[part] + mm(bond_cat[...], stack)
            values = jnp.concatenate(
                [pot[r, pl.ds(pl.multiple_of((o ^ ids[1]) * OCT, OCT), OCT), :] for o in range(CHIPS)], 0
            )
            total = total + (values - SHIFT) * (1.0 / SPREAD) * xs[r]
            weight = coef[2 + first + r] * (1.0 / SPREAD)
            total = total - (weight * coef[0]) * near[:, r].reshape(64, 256)
            total = total - (weight * coef[1]) * far[:, r].reshape(64, 256)
            total = jnp.where(row < ext[first + r], total, 0.0)
            if prev is not None:
                total = 2.0 * total - prev[:, r].reshape(64, 256)
            for o in range(CHIPS):
                outs[o][r] = total[o * OCT : (o + 1) * OCT]

    whole = pl.BlockSpec((CHIPS, step, OCT, 256), lambda i: (0, i, 0, 0))
    crossed = pl.BlockSpec((CHIPS, step, OCT, 256), lambda i: (0, (i + 16 // step) % (32 // step), 0, 0))
    smem = pl.BlockSpec(memory_space=pltpu.SMEM)
    args = [ids, ext, coef, cur, near, far, pot, bond_cat, ang_h, ang_l]
    specs = [smem, smem, smem, whole, crossed, crossed, pl.BlockSpec((step, 64, 256), lambda i: (i, 0, 0))]
    specs += [
        pl.BlockSpec((64, 192), lambda i: (0, 0)),
        pl.BlockSpec((256, 256), lambda i: (0, 0)),
        pl.BlockSpec((256, 256), lambda i: (0, 0)),
    ]
    if prev is not None:
        args.append(prev)
        specs.append(whole)
    return pl.pallas_call(
        kernel,
        grid=(32 // step,),
        in_specs=specs,
        out_specs=[pl.BlockSpec((step, OCT, 256), lambda i: (i, 0, 0))] * CHIPS,
        out_shape=[jax.ShapeDtypeStruct((32, OCT, 256), F32)] * CHIPS,
        compiler_params=params(),
        cost_estimate=pl.CostEstimate(flops=2_000_000_000, bytes_accessed=14_000_000, transcendentals=0),
        name="local_terms",
    )(*args)


def radial_term(ids, ext_col, rad_h, rad_l, pieces, scale, more=None):
    flat = [p.reshape(256, 256) for p in pieces]
    if more is not None:
        flat += [p.reshape(256, 256) for p in more]
    count = len(flat)

    def kernel(ids, ext_col, rad_h, rad_l, *refs):
        ins, outs = refs[:count], refs[count:]

        def column(q):
            at = pl.ds(q, 32, stride=OCT)
            x = [ins[j][at, :] for j in range(CHIPS)]
            if count > CHIPS:
                x = [x[j] + ins[CHIPS + j][at, :] for j in range(CHIPS)]
            return jnp.concatenate(x, 0)

        for q in range(0, OCT, 2):
            high, low = split(jnp.concatenate([column(q), column(q + 1)], 1))
            total = mm(rad_h[...], high) + mm(rad_h[...], low) + mm(rad_l[...], high)
            for i in range(2):
                half = total[:, i * 128 : i * 128 + 128]
                half = jnp.where(ext_col[...] > ids[1] * OCT + q + i, half * scale, 0.0)
                for j in range(CHIPS):
                    outs[j][pl.ds(q + i, 32, stride=OCT), :] = half[j * 32 : j * 32 + 32]

    lanes = pl.BlockSpec((256, 128), lambda i: (0, i))
    full = pl.BlockSpec((256, 256), lambda i: (0, 0))
    out = pl.pallas_call(
        kernel,
        grid=(2,),
        in_specs=[
            pl.BlockSpec(memory_space=pltpu.SMEM), pl.BlockSpec((256, 1), lambda i: (0, 0)), full, full
        ] + [lanes] * count,
        out_specs=[lanes] * CHIPS,
        out_shape=[jax.ShapeDtypeStruct((256, 256), F32)] * CHIPS,
        compiler_params=params(),
        cost_estimate=pl.CostEstimate(flops=2_000_000_000, bytes_accessed=5_000_000, transcendentals=0),
        name="radial_term",
    )(ids, ext_col, rad_h, rad_l, *flat)
    return [o.reshape(32, OCT, 256) for o in out]


def finish(ids, own, other):
    def kernel(ids, own, other, out):
        out[ids[2]] = own[0]
        out[1 - ids[2]] = other[0]

    return pl.pallas_call(
        kernel,
        grid_spec=pltpu.PrefetchScalarGridSpec(
            num_scalar_prefetch=1,
            grid=(CHIPS,),
            in_specs=[
                pl.BlockSpec((1, 16, OCT, 256), lambda j, ids: (j, 0, 0, 0)),
                pl.BlockSpec((1, 16, OCT, 256), lambda j, ids: (j, 0, 0, 0)),
            ],
            out_specs=pl.BlockSpec((2, 16, OCT, 256), lambda j, ids: (0, 0, j ^ ids[1], 0)),
        ),
        out_shape=jax.ShapeDtypeStruct((2, 16, 64, 256), F32),
        compiler_params=params(),
        name="finish",
    )(ids, own, other)


def shards(initial_packet, extents, potential, coriolis_weight, radial_kinetic, bond_kinetic, angle_kinetic):
    ka, ga = lax.axis_index("ka"), lax.axis_index("ga")
    chip, core = ga // 2, ga % 2
    ids = jnp.stack([ga, chip, core]).astype(jnp.int32)
    groups = lax.axis_size("ka")
    members = lax.axis_size("ga")
    top = jnp.float32((2 * groups - 1) * (2 * groups))

    def swap_core(x):
        return lax.ppermute(x, "ga", [(g, g ^ 1) for g in range(members)])

    def swap_chip(x, j):
        return lax.ppermute(x, "ga", [(g, g ^ (2 * j)) for g in range(members)])

    far_pairs = []
    for i in range(groups):
        for g in range(members):
            target = i + 1 if g % 2 else i - 1
            if 0 <= target < groups:
                far_pairs.append((i * members + g, target * members + (g ^ 1)))

    def halo(x):
        return swap_core(x), lax.ppermute(x, ("ka", "ga"), far_pairs)

    def exchange(pieces):
        return [pieces[0]] + [swap_chip(pieces[j], j) for j in range(1, CHIPS)]

    other = swap_core(lax.dynamic_index_in_dim(initial_packet, 1 - core, 0, keepdims=False))
    pot = jnp.concatenate([potential, swap_core(potential)], 0)
    weight = jnp.concatenate([coriolis_weight, swap_core(coriolis_weight)])
    kvalue = (2 * ka + core).astype(F32)
    upper = jnp.sqrt(top - kvalue * (kvalue + 1.0))
    lower = jnp.sqrt(top - kvalue * (kvalue - 1.0))
    coef = jnp.concatenate(
        [jnp.stack([jnp.where(core == 0, upper, lower), jnp.where(core == 0, lower, upper)]), weight]
    )
    ext = lax.dynamic_index_in_dim(extents, core, 0, keepdims=False).reshape(16, 16)
    ext = ext[jnp.arange(16) ^ ga].reshape(256)
    ext_col = ext[:, None]
    ext = ext[:32]

    rad_h, rad_l, bond_cat, ang_h, ang_l = prep(ids, radial_kinetic, bond_kinetic, angle_kinetic)

    def local(cur, halos, prev=None):
        return local_terms(ids, ext, coef, cur, *halos, pot, bond_cat, ang_h, ang_l, prev)

    def radial(pieces, scale, more=None):
        return radial_term(ids, ext_col, rad_h, rad_l, pieces, scale, more)

    def add(a, b):
        return [x + y for x, y in zip(a, b)]

    def outputs(whole):
        return finish(ids, whole, swap_core(whole[:, 16:]))

    t0, *p0 = start(ids, ext, initial_packet, other)
    p0 = [t0[0]] + p0
    p0_far = exchange(p0)
    a0 = local(t0, halo(t0))
    b0 = radial(p0_far, 1.0)
    a0_far = exchange(a0)
    t1 = jnp.stack(add(a0, exchange(b0)))
    b1 = radial(a0_far, 2.0, b0)
    c1 = local(t1, halo(t1), t0)
    p2 = add(c1, exchange(b1))
    t2 = jnp.stack(p2)
    p2_far = exchange(p2)
    c2 = local(t2, halo(t2), t1)
    b2 = radial(p2_far, 2.0)
    t3 = jnp.stack(add(c2, exchange(b2)))
    return outputs(t3), outputs(t2)


def solution(mesh):
    return jax.shard_map(
        shards,
        mesh=mesh,
        in_specs=(
            P("ka", "ga", None, None),
            P("ka", None),
            P("ga", None, None),
            P("ga"),
            P(),
            P(),
            P(),
        ),
        out_specs=(P("ka", "ga", None, None), P("ka", "ga", None, None)),
        check_vma=False,
    )
```

time: 349 us -> 323 us (0.926)
  blocking collectives: 127 us -> 0 us
  waiting for transfers between devices: 88.3 us -> 176 us
  starting transfers between devices: 36.2 us -> 93 us
  matrix products: 43.4 us -> 0 us
  Pallas kernels: 0 us -> 38.9 us
  local copies, waits for them, and re-layouts: 43.4 us -> 9.62 us
    ppermute x6 -> x53, waiting for transfers between devices: 0.02 us -> 176 us  [the longest x42 172 us: swap_chip(): return lax.ppermute(x, 'ga', [(g, g ^ 2 * j) for g in range(members)])]
    all_to_all x3 -> x0, blocking collectives: 127 us -> none  [radial_pass(): lax.all_to_all(packet, 'ga', split_axis=2, concat_axis=1, tiled=True)]
    all_to_all x3 -> x0, waiting for transfers between devices: 88.3 us -> none  [radial_pass(): lax.all_to_all(applied, 'ga', split_axis=1, concat_axis=2, tiled=True)]
    ppermute x6 -> x53, starting transfers between devices: 19.7 us -> 93 us  [the longest x42 68.9 us: swap_chip(): return lax.ppermute(x, 'ga', [(g, g ^ 2 * j) for g in range(members)])]
    dot_general x9 -> x0, matrix products: 43.4 us -> none  [the longest x3 16.9 us: apply_scaled(): jnp.einsum('ab,ksqb->ksqa', angle_kinetic, packet, precision=highest)]
    pallas_call x0 -> x10, Pallas kernels: none -> 38.9 us  [the longest x3 14.5 us: local_terms(): pl.pallas_call(kernel, grid=(32 // step,), in_specs=specs, out_specs=[pl....]
    all_to_all x12 -> x0, local copies, waits for them, and re-layouts: 24.4 us -> none  [the longest x9 23.7 us: radial_pass(): lax.all_to_all(applied, 'ga', split_axis=1, concat_axis=2, tiled=True)]
    all_to_all x3 -> x0, starting transfers between devices: 16.5 us -> none  [radial_pass(): lax.all_to_all(applied, 'ga', split_axis=1, concat_axis=2, tiled=True)]
  transfers between devices with their start and end apart: 9 -> 53, of which waited for: 3 -> 30; matrix products, arithmetic and copies ran while one was open for 9% -> 1% of each run, Pallas kernels for 0% -> 9%
where the time goes in v1:
time: 323 us; the launch traced here: 320 us
  waiting for transfers between devices  176 us (54%)
  starting transfers between devices  93 us (29%)
  Pallas kernels  38.9 us (12%)
  local copies, waits for them, and re-layouts  9.62 us (3%)
    ppermute x42, waiting for transfers between devices, swap_chip(): return lax.ppermute(x, 'ga', [(g, g ^ 2 * j) for g in range(members)])  172 us
    ppermute x42, starting transfers between devices, swap_chip(): return lax.ppermute(x, 'ga', [(g, g ^ 2 * j) for g in range(members)])  68.9 us
    ppermute x8, starting transfers between devices, swap_core(): return lax.ppermute(x, 'ga', [(g, g ^ 1) for g in range(members)])  18.1 us
    pallas_call x3, Pallas kernels, local_terms(): pl.pallas_call(kernel, grid=(32 // step,), in_specs=specs, out_specs=[pl....  14.5 us
    pallas_call x3, Pallas kernels, radial_term(): pl.pallas_call(kernel, grid=(2,), in_specs=[pl.BlockSpec(memory_space=plt...  8.31 us
    pallas_call x1, Pallas kernels, start(): pl.pallas_call(kernel, grid_spec=pltpu.PrefetchScalarGridSpec(num_scalar_...  8.18 us
    unnamed x33, local copies, waits for them, and re-layouts  7.15 us
    pallas_call x2, Pallas kernels, finish(): pl.pallas_call(kernel, grid_spec=pltpu.PrefetchScalarGridSpec(num_scalar_...  7.06 us
  transfers between devices with their start and end apart: 53, of which 30 were waited for; matrix products, arithmetic and copies ran while one was open for 1% of the time, Pallas kernels for 9%

profile of v1, /device:TPU:1, one launch (start us, length us, event | category | flops | bytes accessed | tf_op | source)
XLA Modules:
  0.0 320.1 jit_solution(4999358749795045441)
XLA Ops:
  2.0 3.3 %collective-permute-start.1 = (f32[16,64,256]{2,1,0:T(8,128)S(1)}, f32[16,64,256]{2,1,0:T(8,128)S(1)}, u32[]{:S(2)}, u32[]{:S(2)}) collective-permute-start(f32[16,64,256]{2,1,0:T(8,128)S(1)} %dynamic-slice_bitcast_fusion), channel_id=1, source_target_pairs={{0,1},{1,0},{2,3},{3,2},{4,5},{5,4},{6,7},{7,6},{8,9},{9,8},{10,11... | collective-permute-start | bytes 3145736 | tf_op jit(solution)/shard_map/ppermute | solution.py:223
  9.3 8.2 %start.1 = (f32[8,32,8,256]{3,2,1,0:T(8,128)S(1)}, f32[32,8,256]{2,1,0:T(8,128)S(1)}, f32[32,8,256]{2,1,0:T(8,128)}, f32[32,8,256]{2,1,0:T(8,128)}, f32[32,8,256...) custom-call(s32[3]{0:T(128)S(1)} %pad_add_fusion.ids, ...), custom_call_target="tpu_custom_call" | custom-call | tf_op jit(solution)/shard_map/start/pallas_call | solution.py:79
  24.0 2.6 collective-permute-done
  26.6 3.3 %collective-permute-start.6 = (f32[32,8,256]{2,1,0:T(8,128)}, f32[32,8,256]{2,1,0:T(8,128)}, u32[]{:S(2)}, u32[]{:S(2)}) collective-permute-start(f32[32,8,256]{2,1,0:T(8,128)} %get-tuple-element.71), channel_id=1, source_target_pairs={{0,4},{1,5},{2,6},{3,7},{4,0},{5,1},{6,2},{7,3},{8,12},{9,13},{10,... | collective-permute-start | bytes 786440 | tf_op jit(solution)/shard_map/ppermute | solution.py:226
  30.9 2.7 collective-permute-start.8
  38.5 2.5 collective-permute-start.9
  40.9 3.5 %collective-permute-done.7 = f32[32,8,256]{2,1,0:T(8,128)} collective-permute-done((f32[32,8,256]{2,1,0:T(8,128)}, f32[32,8,256]{2,1,0:T(8,128)}, u32[]{:S(2)}, u32[]{:S(2)}) %collective-permute-start.7) | collective-permute-done | bytes 262176 | tf_op jit(solution)/shard_map/ppermute | solution.py:226
  46.8 10.5 %collective-permute-done.8 = f32[32,8,256]{2,1,0:T(8,128)} collective-permute-done((f32[32,8,256]{2,1,0:T(8,128)}, f32[32,8,256]{2,1,0:T(8,128)}, u32[]{:S(2)}, u32[]{:S(2)}) %collective-permute-start.8) | collective-permute-done | bytes 262176 | tf_op jit(solution)/shard_map/ppermute | solution.py:226
  57.2 2.7 collective-permute-start.11
  60.1 3.7 %collective-permute-done.9 = f32[32,8,256]{2,1,0:T(8,128)S(1)} collective-permute-done((f32[32,8,256]{2,1,0:T(8,128)S(1)}, f32[32,8,256]{2,1,0:T(8,128)S(1)}, u32[]{:S(2)}, u32[]{:S(2)}) %collective-permute-start.9) | collective-permute-done | bytes 262176 | tf_op jit(solution)/shard_map/ppermute | solution.py:226
  63.8 7.2 %collective-permute-done.10 = f32[32,8,256]{2,1,0:T(8,128)S(1)} collective-permute-done((f32[32,8,256]{2,1,0:T(8,128)S(1)}, f32[32,8,256]{2,1,0:T(8,128)S(1)}, u32[]{:S(2)}, u32[]{:S(2)}) %collective-permute-start.10) | collective-permute-done | bytes 262176 | tf_op jit(solution)/shard_map/ppermute | solution.py:226
  71.0 5.5 %collective-permute-done.11 = f32[32,8,256]{2,1,0:T(8,128)S(1)} collective-permute-done((f32[32,8,256]{2,1,0:T(8,128)S(1)}, f32[32,8,256]{2,1,0:T(8,128)S(1)}, u32[]{:S(2)}, u32[]{:S(2)}) %collective-permute-start.11) | collective-permute-done | bytes 262176 | tf_op jit(solution)/shard_map/ppermute | solution.py:226
  77.4 2.9 radial_term.3
  81.2 3.9 %collective-permute-start.17 = (f32[32,8,256]{2,1,0:T(8,128)S(1)}, f32[32,8,256]{2,1,0:T(8,128)S(1)}, u32[]{:S(2)}, u32[]{:S(2)}) collective-permute-start(f32[32,8,256]{2,1,0:T(8,128)S(1)} %bitcast.124), channel_id=1, source_target_pairs={{0,12},{1,13},{2,14},{3,15},{4,8},{5,9},{6,10},{7,11},{8,4},{9,5},... | collective-permute-start | bytes 786440 | tf_op jit(solution)/shard_map/ppermute | solution.py:226
  87.4 6.2 %local_terms.3 = (f32[32,8,256]{2,1,0:T(8,128)S(1)}, f32[32,8,256]{2,1,0:T(8,128)S(1)}, f32[32,8,256]{2,1,0:T(8,128)S(1)}, f32[32,8,256]{2,1,0:T(8,128)S(1)}, f3...) custom-call(s32[3]{0:T(128)S(1)} %pad_add_fusion.ids, ...), custom_call_target="tpu_custom_call" | custom-call | flops 2000000000 | bytes 14000000 | tf_op jit(solution)/shard_map/local_terms/pallas_call | solution.py:138
  93.7 18.8 %collective-permute-done.12 = f32[32,8,256]{2,1,0:T(8,128)S(1)} collective-permute-done((f32[32,8,256]{2,1,0:T(8,128)S(1)}, f32[32,8,256]{2,1,0:T(8,128)S(1)}, u32[]{:S(2)}, u32[]{:S(2)}) %collective-permute-start.12) | collective-permute-done | bytes 262176 | tf_op jit(solution)/shard_map/ppermute | solution.py:226
  115.3 5.1 %collective-permute-done.14 = f32[32,8,256]{2,1,0:T(8,128)S(1)} collective-permute-done((f32[32,8,256]{2,1,0:T(8,128)S(1)}, f32[32,8,256]{2,1,0:T(8,128)S(1)}, u32[]{:S(2)}, u32[]{:S(2)}) %collective-permute-start.14) | collective-permute-done | bytes 262176 | tf_op jit(solution)/shard_map/ppermute | solution.py:226
  120.4 21.9 %collective-permute-done.15 = f32[32,8,256]{2,1,0:T(8,128)S(1)} collective-permute-done((f32[32,8,256]{2,1,0:T(8,128)S(1)}, f32[32,8,256]{2,1,0:T(8,128)S(1)}, u32[]{:S(2)}, u32[]{:S(2)}) %collective-permute-start.15) | collective-permute-done | bytes 262176 | tf_op jit(solution)/shard_map/ppermute | solution.py:226
  144.5 3.6 %collective-permute-start.19 = (f32[8,32,8,256]{3,2,1,0:T(8,128)S(1)}, f32[8,32,8,256]{3,2,1,0:T(8,128)S(1)}, u32[]{:S(2)}, u32[]{:S(2)}) collective-permute-start(f32[8,32,8,256]{3,2,1,0:T(8,128)S(1)} %bitcast_dynamic-update-slice_fusion.16.cur.rest_0_), channel_id=1, source_target_pairs={{0,1},{1,0},{2,3},{3,2},{4,5},{5,4},{6,7},{7,6},{8,9},{9,8},{10,11... | collective-permute-start | bytes 6291464 | tf_op jit(solution)/shard_map/ppermute | solution.py:223
  151.9 4.0 %collective-permute-done.21 = f32[32,8,256]{2,1,0:T(8,128)S(1)} collective-permute-done((f32[32,8,256]{2,1,0:T(8,128)S(1)}, f32[32,8,256]{2,1,0:T(8,128)S(1)}, u32[]{:S(2)}, u32[]{:S(2)}) %collective-permute-start.21) | collective-permute-done | bytes 262176 | tf_op jit(solution)/shard_map/ppermute | solution.py:226
  156.9 5.4 %collective-permute-done.22 = f32[32,8,256]{2,1,0:T(8,128)S(1)} collective-permute-done((f32[32,8,256]{2,1,0:T(8,128)S(1)}, f32[32,8,256]{2,1,0:T(8,128)S(1)}, u32[]{:S(2)}, u32[]{:S(2)}) %collective-permute-start.22) | collective-permute-done | bytes 262176 | tf_op jit(solution)/shard_map/ppermute | solution.py:226
  164.3 3.3 %collective-permute-start.26 = (f32[32,8,256]{2,1,0:T(8,128)S(1)}, f32[32,8,256]{2,1,0:T(8,128)S(1)}, u32[]{:S(2)}, u32[]{:S(2)}) collective-permute-start(f32[32,8,256]{2,1,0:T(8,128)S(1)} %get-tuple-element.88), channel_id=1, source_target_pairs={{0,12},{1,13},{2,14},{3,15},{4,8},{5,9},{6,10},{7,11},{8,4},{9,5},... | collective-permute-start | bytes 786440 | tf_op jit(solution)/shard_map/ppermute | solution.py:226
  169.2 2.4 collective-permute-done.25
  171.6 7.4 %collective-permute-done.26 = f32[32,8,256]{2,1,0:T(8,128)S(1)} collective-permute-done((f32[32,8,256]{2,1,0:T(8,128)S(1)}, f32[32,8,256]{2,1,0:T(8,128)S(1)}, u32[]{:S(2)}, u32[]{:S(2)}) %collective-permute-start.26) | collective-permute-done | bytes 262176 | tf_op jit(solution)/shard_map/ppermute | solution.py:226
  179.0 5.1 %collective-permute-done.27 = f32[32,8,256]{2,1,0:T(8,128)S(1)} collective-permute-done((f32[32,8,256]{2,1,0:T(8,128)S(1)}, f32[32,8,256]{2,1,0:T(8,128)S(1)}, u32[]{:S(2)}, u32[]{:S(2)}) %collective-permute-start.27) | collective-permute-done | bytes 262176 | tf_op jit(solution)/shard_map/ppermute | solution.py:226
  184.1 2.9 radial_term.4
  192.9 4.1 %local_terms.4 = (f32[32,8,256]{2,1,0:T(8,128)S(1)}, f32[32,8,256]{2,1,0:T(8,128)S(1)}, f32[32,8,256]{2,1,0:T(8,128)S(1)}, f32[32,8,256]{2,1,0:T(8,128)S(1)}, f3...) custom-call(s32[3]{0:T(128)S(1)} %pad_add_fusion.ids, ...), custom_call_target="tpu_custom_call" | custom-call | flops 2000000000 | bytes 14000000 | tf_op jit(solution)/shard_map/local_terms/pallas_call | solution.py:138
  198.8 4.0 %collective-permute-start.33 = (f32[32,8,256]{2,1,0:T(8,128)S(1)}, f32[32,8,256]{2,1,0:T(8,128)S(1)}, u32[]{:S(2)}, u32[]{:S(2)}) collective-permute-start(f32[32,8,256]{2,1,0:T(8,128)S(1)} %bitcast.128), channel_id=1, source_target_pairs={{0,12},{1,13},{2,14},{3,15},{4,8},{5,9},{6,10},{7,11},{8,4},{9,5},... | collective-permute-start | bytes 786440 | tf_op jit(solution)/shard_map/ppermute | solution.py:226
  202.8 2.4 collective-permute-start.34
  205.5 20.0 %collective-permute-done.32 = f32[32,8,256]{2,1,0:T(8,128)S(1)} collective-permute-done((f32[32,8,256]{2,1,0:T(8,128)S(1)}, f32[32,8,256]{2,1,0:T(8,128)S(1)}, u32[]{:S(2)}, u32[]{:S(2)}) %collective-permute-start.32) | collective-permute-done | bytes 262176 | tf_op jit(solution)/shard_map/ppermute | solution.py:226
  225.5 5.1 %collective-permute-done.33 = f32[32,8,256]{2,1,0:T(8,128)S(1)} collective-permute-done((f32[32,8,256]{2,1,0:T(8,128)S(1)}, f32[32,8,256]{2,1,0:T(8,128)S(1)}, u32[]{:S(2)}, u32[]{:S(2)}) %collective-permute-start.33) | collective-permute-done | bytes 262176 | tf_op jit(solution)/shard_map/ppermute | solution.py:226
  230.7 6.3 %collective-permute-done.34 = f32[32,8,256]{2,1,0:T(8,128)S(1)} collective-permute-done((f32[32,8,256]{2,1,0:T(8,128)S(1)}, f32[32,8,256]{2,1,0:T(8,128)S(1)}, u32[]{:S(2)}, u32[]{:S(2)}) %collective-permute-start.34) | collective-permute-done | bytes 262176 | tf_op jit(solution)/shard_map/ppermute | solution.py:226
  238.9 2.9 collective-permute-start.35
  241.8 2.5 collective-permute-start.43
  248.4 5.0 %collective-permute-done.43 = f32[32,8,256]{2,1,0:T(8,128)S(1)} collective-permute-done((f32[32,8,256]{2,1,0:T(8,128)S(1)}, f32[32,8,256]{2,1,0:T(8,128)S(1)}, u32[]{:S(2)}, u32[]{:S(2)}) %collective-permute-start.43) | collective-permute-done | bytes 262176 | tf_op jit(solution)/shard_map/ppermute | solution.py:226
  254.5 4.2 %collective-permute-done.42 = f32[32,8,256]{2,1,0:T(8,128)S(1)} collective-permute-done((f32[32,8,256]{2,1,0:T(8,128)S(1)}, f32[32,8,256]{2,1,0:T(8,128)S(1)}, u32[]{:S(2)}, u32[]{:S(2)}) %collective-permute-start.42) | collective-permute-done | bytes 262176 | tf_op jit(solution)/shard_map/ppermute | solution.py:226
  260.4 3.2 %collective-permute-done.41 = f32[32,8,256]{2,1,0:T(8,128)S(1)} collective-permute-done((f32[32,8,256]{2,1,0:T(8,128)S(1)}, f32[32,8,256]{2,1,0:T(8,128)S(1)}, u32[]{:S(2)}, u32[]{:S(2)}) %collective-permute-start.41) | collective-permute-done | bytes 262176 | tf_op jit(solution)/shard_map/ppermute | solution.py:226
  265.7 3.7 %collective-permute-done.40 = f32[32,8,256]{2,1,0:T(8,128)S(1)} collective-permute-done((f32[32,8,256]{2,1,0:T(8,128)S(1)}, f32[32,8,256]{2,1,0:T(8,128)S(1)}, u32[]{:S(2)}, u32[]{:S(2)}) %collective-permute-start.40) | collective-permute-done | bytes 262176 | tf_op jit(solution)/shard_map/ppermute | solution.py:226
  269.7 4.2 %collective-permute-start.52 = (f32[8,16,8,256]{3,2,1,0:T(8,128)S(1)}, f32[8,16,8,256]{3,2,1,0:T(8,128)S(1)}, u32[]{:S(2)}, u32[]{:S(2)}) collective-permute-start(f32[8,16,8,256]{3,2,1,0:T(8,128)S(1)} %slice.24), channel_id=1, source_target_pairs={{0,1},{1,0},{2,3},{3,2},{4,5},{5,4},{6,7},{7,6},{8,9},{9,8},{10,11... | collective-permute-start | bytes 3145736 | tf_op jit(solution)/shard_map/ppermute | solution.py:223
  273.9 2.5 collective-permute-done.37
  276.4 2.5 radial_term.5
  284.2 4.1 %local_terms.5 = (f32[32,8,256]{2,1,0:T(8,128)S(1)}, f32[32,8,256]{2,1,0:T(8,128)S(1)}, f32[32,8,256]{2,1,0:T(8,128)S(1)}, f32[32,8,256]{2,1,0:T(8,128)S(1)}, f3...) custom-call(s32[3]{0:T(128)S(1)} %pad_add_fusion.ids, ...), custom_call_target="tpu_custom_call" | custom-call | flops 2000000000 | bytes 14000000 | tf_op jit(solution)/shard_map/local_terms/pallas_call | solution.py:138
  290.2 3.0 collective-permute-done.45
  297.5 8.5 %collective-permute-done.49 = f32[32,8,256]{2,1,0:T(8,128)S(1)} collective-permute-done((f32[32,8,256]{2,1,0:T(8,128)S(1)}, f32[32,8,256]{2,1,0:T(8,128)S(1)}, u32[]{:S(2)}, u32[]{:S(2)}) %collective-permute-start.49) | collective-permute-done | bytes 262176 | tf_op jit(solution)/shard_map/ppermute | solution.py:226
  306.0 3.7 %collective-permute-done.50 = f32[32,8,256]{2,1,0:T(8,128)S(1)} collective-permute-done((f32[32,8,256]{2,1,0:T(8,128)S(1)}, f32[32,8,256]{2,1,0:T(8,128)S(1)}, u32[]{:S(2)}, u32[]{:S(2)}) %collective-permute-start.50) | collective-permute-done | bytes 262176 | tf_op jit(solution)/shard_map/ppermute | solution.py:226
  309.9 3.2 collective-permute-start.51
  313.0 3.5 %finish.3 = f32[2,16,64,256]{3,2,1,0:T(8,128)} custom-call(s32[3]{0:T(128)S(1)} %pad_add_fusion.ids, f32[8,32,8,256]{3,2,1,0:T(8,128)S(1)} %get-tuple-element.124.cur.own, f32[8,16,8,256]{3,2,1,0:T(8,128)S(1)} %collective-permute-done.52.other), custom_call_target="tpu_custom_call" | custom-call | tf_op jit(solution)/shard_map/finish/pallas_call | solution.py:197
  316.6 3.5 %finish.2 = f32[2,16,64,256]{3,2,1,0:T(8,128)} custom-call(s32[3]{0:T(128)S(1)} %pad_add_fusion.ids, f32[8,32,8,256]{3,2,1,0:T(8,128)S(1)} %bitcast_dynamic-update-slice_fusion.own, f32[8,16,8,256]{3,2,1,0:T(8,128)S(1)} %collective-permute-done.51.other), custom_call_target="tpu_custom_call" | custom-call | tf_op jit(solution)/shard_map/finish/pallas_call | solution.py:197
  (142 shorter events, 68.1 us)
Async XLA Ops:
  19.6 66.5 %collective-permute-start.3 = (f32[8,32,8,256]{3,2,1,0:T(8,128)S(1)}, f32[8,32,8,256]{3,2,1,0:T(8,128)}, u32[]{:S(2)}, u32[]{:S(2)}) collective-permute-start(f32[8,32,8,256]{3,2,1,0:T(8,128)S(1)} %get-tuple-element.63.cur.rest_0_), channel_id=1, source_target_pairs={{1,16},{3,18},{5,20},{7,22},{9,24},{11,26},{13,28},{15,30},{16,1},... | collective-permute-start | bytes 6291464 | tf_op jit(solution)/shard_map/ppermute | solution.py:236
  21.8 65.2 %collective-permute-start.2 = (f32[8,32,8,256]{3,2,1,0:T(8,128)S(1)}, f32[8,32,8,256]{3,2,1,0:T(8,128)}, u32[]{:S(2)}, u32[]{:S(2)}) collective-permute-start(f32[8,32,8,256]{3,2,1,0:T(8,128)S(1)} %get-tuple-element.63.cur.rest_0_), channel_id=1, source_target_pairs={{0,1},{1,0},{2,3},{3,2},{4,5},{5,4},{6,7},{7,6},{8,9},{9,8},{10,11... | collective-permute-start | bytes 6291464 | tf_op jit(solution)/shard_map/ppermute | solution.py:223
  22.4 8.3 %collective-permute-start.5 = (f32[32,8,256]{2,1,0:T(8,128)S(1)}, f32[32,8,256]{2,1,0:T(8,128)S(1)}, u32[]{:S(2)}, u32[]{:S(2)}) collective-permute-start(f32[32,8,256]{2,1,0:T(8,128)S(1)} %get-tuple-element.70), channel_id=1, source_target_pairs={{0,2},{1,3},{2,0},{3,1},{4,6},{5,7},{6,4},{7,5},{8,10},{9,11},{10,... | collective-permute-start | bytes 786440 | tf_op jit(solution)/shard_map/ppermute | solution.py:226
  26.6 11.8 %collective-permute-start.6 = (f32[32,8,256]{2,1,0:T(8,128)}, f32[32,8,256]{2,1,0:T(8,128)}, u32[]{:S(2)}, u32[]{:S(2)}) collective-permute-start(f32[32,8,256]{2,1,0:T(8,128)} %get-tuple-element.71), channel_id=1, source_target_pairs={{0,4},{1,5},{2,6},{3,7},{4,0},{5,1},{6,2},{7,3},{8,12},{9,13},{10,... | collective-permute-start | bytes 786440 | tf_op jit(solution)/shard_map/ppermute | solution.py:226
  29.9 14.5 %collective-permute-start.7 = (f32[32,8,256]{2,1,0:T(8,128)}, f32[32,8,256]{2,1,0:T(8,128)}, u32[]{:S(2)}, u32[]{:S(2)}) collective-permute-start(f32[32,8,256]{2,1,0:T(8,128)} %get-tuple-element.72), channel_id=1, source_target_pairs={{0,6},{1,7},{2,4},{3,5},{4,2},{5,3},{6,0},{7,1},{8,14},{9,15},{10,... | collective-permute-start | bytes 786440 | tf_op jit(solution)/shard_map/ppermute | solution.py:226
  30.9 26.4 %collective-permute-start.8 = (f32[32,8,256]{2,1,0:T(8,128)}, f32[32,8,256]{2,1,0:T(8,128)}, u32[]{:S(2)}, u32[]{:S(2)}) collective-permute-start(f32[32,8,256]{2,1,0:T(8,128)} %get-tuple-element.73), channel_id=1, source_target_pairs={{0,8},{1,9},{2,10},{3,11},{4,12},{5,13},{6,14},{7,15},{8,0},{9,1},... | collective-permute-start | bytes 786440 | tf_op jit(solution)/shard_map/ppermute | solution.py:226
  38.5 25.3 %collective-permute-start.9 = (f32[32,8,256]{2,1,0:T(8,128)S(1)}, f32[32,8,256]{2,1,0:T(8,128)S(1)}, u32[]{:S(2)}, u32[]{:S(2)}) collective-permute-start(f32[32,8,256]{2,1,0:T(8,128)S(1)} %copy-done.11), channel_id=1, source_target_pairs={{0,10},{1,11},{2,8},{3,9},{4,14},{5,15},{6,12},{7,13},{8,2},{9,3},... | collective-permute-start | bytes 786440 | tf_op jit(solution)/shard_map/ppermute | solution.py:226
  44.4 26.6 %collective-permute-start.10 = (f32[32,8,256]{2,1,0:T(8,128)S(1)}, f32[32,8,256]{2,1,0:T(8,128)S(1)}, u32[]{:S(2)}, u32[]{:S(2)}) collective-permute-start(f32[32,8,256]{2,1,0:T(8,128)S(1)} %copy-done.7), channel_id=1, source_target_pairs={{0,12},{1,13},{2,14},{3,15},{4,8},{5,9},{6,10},{7,11},{8,4},{9,5},... | collective-permute-start | bytes 786440 | tf_op jit(solution)/shard_map/ppermute | solution.py:226
  57.2 19.3 %collective-permute-start.11 = (f32[32,8,256]{2,1,0:T(8,128)S(1)}, f32[32,8,256]{2,1,0:T(8,128)S(1)}, u32[]{:S(2)}, u32[]{:S(2)}) collective-permute-start(f32[32,8,256]{2,1,0:T(8,128)S(1)} %copy-done.5), channel_id=1, source_target_pairs={{0,14},{1,15},{2,12},{3,13},{4,10},{5,11},{6,8},{7,9},{8,6},{9,7},... | collective-permute-start | bytes 786440 | tf_op jit(solution)/shard_map/ppermute | solution.py:226
  80.4 62.1 %collective-permute-start.18 = (f32[32,8,256]{2,1,0:T(8,128)S(1)}, f32[32,8,256]{2,1,0:T(8,128)S(1)}, u32[]{:S(2)}, u32[]{:S(2)}) collective-permute-start(f32[32,8,256]{2,1,0:T(8,128)S(1)} %bitcast.125), channel_id=1, source_target_pairs={{0,14},{1,15},{2,12},{3,13},{4,10},{5,11},{6,8},{7,9},{8,6},{9,7},... | collective-permute-start | bytes 786440 | tf_op jit(solution)/shard_map/ppermute | solution.py:226
  81.2 61.3 %collective-permute-start.17 = (f32[32,8,256]{2,1,0:T(8,128)S(1)}, f32[32,8,256]{2,1,0:T(8,128)S(1)}, u32[]{:S(2)}, u32[]{:S(2)}) collective-permute-start(f32[32,8,256]{2,1,0:T(8,128)S(1)} %bitcast.124), channel_id=1, source_target_pairs={{0,12},{1,13},{2,14},{3,15},{4,8},{5,9},{6,10},{7,11},{8,4},{9,5},... | collective-permute-start | bytes 786440 | tf_op jit(solution)/shard_map/ppermute | solution.py:226
  85.0 57.4 %collective-permute-start.16 = (f32[32,8,256]{2,1,0:T(8,128)S(1)}, f32[32,8,256]{2,1,0:T(8,128)S(1)}, u32[]{:S(2)}, u32[]{:S(2)}) collective-permute-start(f32[32,8,256]{2,1,0:T(8,128)S(1)} %bitcast.123), channel_id=1, source_target_pairs={{0,10},{1,11},{2,8},{3,9},{4,14},{5,15},{6,12},{7,13},{8,2},{9,3},... | collective-permute-start | bytes 786440 | tf_op jit(solution)/shard_map/ppermute | solution.py:226
  86.1 28.1 %collective-permute-start.13 = (f32[32,8,256]{2,1,0:T(8,128)S(1)}, f32[32,8,256]{2,1,0:T(8,128)S(1)}, u32[]{:S(2)}, u32[]{:S(2)}) collective-permute-start(f32[32,8,256]{2,1,0:T(8,128)S(1)} %bitcast.120), channel_id=1, source_target_pairs={{0,4},{1,5},{2,6},{3,7},{4,0},{5,1},{6,2},{7,3},{8,12},{9,13},{10,... | collective-permute-start | bytes 786440 | tf_op jit(solution)/shard_map/ppermute | solution.py:226
  86.9 25.5 %collective-permute-start.12 = (f32[32,8,256]{2,1,0:T(8,128)S(1)}, f32[32,8,256]{2,1,0:T(8,128)S(1)}, u32[]{:S(2)}, u32[]{:S(2)}) collective-permute-start(f32[32,8,256]{2,1,0:T(8,128)S(1)} %bitcast.119), channel_id=1, source_target_pairs={{0,2},{1,3},{2,0},{3,1},{4,6},{5,7},{6,4},{7,5},{8,10},{9,11},{10,... | collective-permute-start | bytes 786440 | tf_op jit(solution)/shard_map/ppermute | solution.py:226
  112.5 7.9 %collective-permute-start.14 = (f32[32,8,256]{2,1,0:T(8,128)S(1)}, f32[32,8,256]{2,1,0:T(8,128)S(1)}, u32[]{:S(2)}, u32[]{:S(2)}) collective-permute-start(f32[32,8,256]{2,1,0:T(8,128)S(1)} %bitcast.121), channel_id=1, source_target_pairs={{0,6},{1,7},{2,4},{3,5},{4,2},{5,3},{6,0},{7,1},{8,14},{9,15},{10,... | collective-permute-start | bytes 786440 | tf_op jit(solution)/shard_map/ppermute | solution.py:226
  114.2 28.2 %collective-permute-start.15 = (f32[32,8,256]{2,1,0:T(8,128)S(1)}, f32[32,8,256]{2,1,0:T(8,128)S(1)}, u32[]{:S(2)}, u32[]{:S(2)}) collective-permute-start(f32[32,8,256]{2,1,0:T(8,128)S(1)} %bitcast.122), channel_id=1, source_target_pairs={{0,8},{1,9},{2,10},{3,11},{4,12},{5,13},{6,14},{7,15},{8,0},{9,1},... | collective-permute-start | bytes 786440 | tf_op jit(solution)/shard_map/ppermute | solution.py:226
  142.5 47.9 %collective-permute-start.20 = (f32[8,32,8,256]{3,2,1,0:T(8,128)S(1)}, f32[8,32,8,256]{3,2,1,0:T(8,128)S(1)}, u32[]{:S(2)}, u32[]{:S(2)}) collective-permute-start(f32[8,32,8,256]{3,2,1,0:T(8,128)S(1)} %bitcast_dynamic-update-slice_fusion.16.cur.rest_0_), channel_id=1, source_target_pairs={{1,16},{3,18},{5,20},{7,22},{9,24},{11,26},{13,28},{15,30},{16,1},... | collective-permute-start | bytes 6291464 | tf_op jit(solution)/shard_map/ppermute | solution.py:236
  144.5 47.1 %collective-permute-start.19 = (f32[8,32,8,256]{3,2,1,0:T(8,128)S(1)}, f32[8,32,8,256]{3,2,1,0:T(8,128)S(1)}, u32[]{:S(2)}, u32[]{:S(2)}) collective-permute-start(f32[8,32,8,256]{3,2,1,0:T(8,128)S(1)} %bitcast_dynamic-update-slice_fusion.16.cur.rest_0_), channel_id=1, source_target_pairs={{0,1},{1,0},{2,3},{3,2},{4,5},{5,4},{6,7},{7,6},{8,9},{9,8},{10,11... | collective-permute-start | bytes 6291464 | tf_op jit(solution)/shard_map/ppermute | solution.py:223
  148.1 7.9 %collective-permute-start.21 = (f32[32,8,256]{2,1,0:T(8,128)S(1)}, f32[32,8,256]{2,1,0:T(8,128)S(1)}, u32[]{:S(2)}, u32[]{:S(2)}) collective-permute-start(f32[32,8,256]{2,1,0:T(8,128)S(1)} %get-tuple-element.78), channel_id=1, source_target_pairs={{0,2},{1,3},{2,0},{3,1},{4,6},{5,7},{6,4},{7,5},{8,10},{9,11},{10,... | collective-permute-start | bytes 786440 | tf_op jit(solution)/shard_map/ppermute | solution.py:226
  148.1 14.2 %collective-permute-start.22 = (f32[32,8,256]{2,1,0:T(8,128)S(1)}, f32[32,8,256]{2,1,0:T(8,128)S(1)}, u32[]{:S(2)}, u32[]{:S(2)}) collective-permute-start(f32[32,8,256]{2,1,0:T(8,128)S(1)} %get-tuple-element.80), channel_id=1, source_target_pairs={{0,4},{1,5},{2,6},{3,7},{4,0},{5,1},{6,2},{7,3},{8,12},{9,13},{10,... | collective-permute-start | bytes 786440 | tf_op jit(solution)/shard_map/ppermute | solution.py:226
  150.3 14.0 %collective-permute-start.23 = (f32[32,8,256]{2,1,0:T(8,128)S(1)}, f32[32,8,256]{2,1,0:T(8,128)S(1)}, u32[]{:S(2)}, u32[]{:S(2)}) collective-permute-start(f32[32,8,256]{2,1,0:T(8,128)S(1)} %get-tuple-element.82), channel_id=1, source_target_pairs={{0,6},{1,7},{2,4},{3,5},{4,2},{5,3},{6,0},{7,1},{8,14},{9,15},{10,... | collective-permute-start | bytes 786440 | tf_op jit(solution)/shard_map/ppermute | solution.py:226
  155.9 11.6 %collective-permute-start.24 = (f32[32,8,256]{2,1,0:T(8,128)S(1)}, f32[32,8,256]{2,1,0:T(8,128)S(1)}, u32[]{:S(2)}, u32[]{:S(2)}) collective-permute-start(f32[32,8,256]{2,1,0:T(8,128)S(1)} %get-tuple-element.84), channel_id=1, source_target_pairs={{0,8},{1,9},{2,10},{3,11},{4,12},{5,13},{6,14},{7,15},{8,0},{9,1},... | collective-permute-start | bytes 786440 | tf_op jit(solution)/shard_map/ppermute | solution.py:226
  162.3 9.3 %collective-permute-start.25 = (f32[32,8,256]{2,1,0:T(8,128)S(1)}, f32[32,8,256]{2,1,0:T(8,128)S(1)}, u32[]{:S(2)}, u32[]{:S(2)}) collective-permute-start(f32[32,8,256]{2,1,0:T(8,128)S(1)} %get-tuple-element.86), channel_id=1, source_target_pairs={{0,10},{1,11},{2,8},{3,9},{4,14},{5,15},{6,12},{7,13},{8,2},{9,3},... | collective-permute-start | bytes 786440 | tf_op jit(solution)/shard_map/ppermute | solution.py:226
  164.3 14.7 %collective-permute-start.26 = (f32[32,8,256]{2,1,0:T(8,128)S(1)}, f32[32,8,256]{2,1,0:T(8,128)S(1)}, u32[]{:S(2)}, u32[]{:S(2)}) collective-permute-start(f32[32,8,256]{2,1,0:T(8,128)S(1)} %get-tuple-element.88), channel_id=1, source_target_pairs={{0,12},{1,13},{2,14},{3,15},{4,8},{5,9},{6,10},{7,11},{8,4},{9,5},... | collective-permute-start | bytes 786440 | tf_op jit(solution)/shard_map/ppermute | solution.py:226
  167.6 16.6 %collective-permute-start.27 = (f32[32,8,256]{2,1,0:T(8,128)S(1)}, f32[32,8,256]{2,1,0:T(8,128)S(1)}, u32[]{:S(2)}, u32[]{:S(2)}) collective-permute-start(f32[32,8,256]{2,1,0:T(8,128)S(1)} %get-tuple-element.90), channel_id=1, source_target_pairs={{0,14},{1,15},{2,12},{3,13},{4,10},{5,11},{6,8},{7,9},{8,6},{9,7},... | collective-permute-start | bytes 786440 | tf_op jit(solution)/shard_map/ppermute | solution.py:226
  187.1 15.8 %collective-permute-start.29 = (f32[32,8,256]{2,1,0:T(8,128)S(1)}, f32[32,8,256]{2,1,0:T(8,128)S(1)}, u32[]{:S(2)}, u32[]{:S(2)}) collective-permute-start(f32[32,8,256]{2,1,0:T(8,128)S(1)} %bitcast.138), channel_id=1, source_target_pairs={{0,4},{1,5},{2,6},{3,7},{4,0},{5,1},{6,2},{7,3},{8,12},{9,13},{10,... | collective-permute-start | bytes 786440 | tf_op jit(solution)/shard_map/ppermute | solution.py:226
  187.6 11.1 %collective-permute-start.28 = (f32[32,8,256]{2,1,0:T(8,128)S(1)}, f32[32,8,256]{2,1,0:T(8,128)S(1)}, u32[]{:S(2)}, u32[]{:S(2)}) collective-permute-start(f32[32,8,256]{2,1,0:T(8,128)S(1)} %bitcast.145), channel_id=1, source_target_pairs={{0,2},{1,3},{2,0},{3,1},{4,6},{5,7},{6,4},{7,5},{8,10},{9,11},{10,... | collective-permute-start | bytes 786440 | tf_op jit(solution)/shard_map/ppermute | solution.py:226
  188.7 16.6 %collective-permute-start.30 = (f32[32,8,256]{2,1,0:T(8,128)S(1)}, f32[32,8,256]{2,1,0:T(8,128)S(1)}, u32[]{:S(2)}, u32[]{:S(2)}) collective-permute-start(f32[32,8,256]{2,1,0:T(8,128)S(1)} %bitcast.135), channel_id=1, source_target_pairs={{0,6},{1,7},{2,4},{3,5},{4,2},{5,3},{6,0},{7,1},{8,14},{9,15},{10,... | collective-permute-start | bytes 786440 | tf_op jit(solution)/shard_map/ppermute | solution.py:226
  190.4 15.0 %collective-permute-start.31 = (f32[32,8,256]{2,1,0:T(8,128)S(1)}, f32[32,8,256]{2,1,0:T(8,128)S(1)}, u32[]{:S(2)}, u32[]{:S(2)}) collective-permute-start(f32[32,8,256]{2,1,0:T(8,128)S(1)} %bitcast.133), channel_id=1, source_target_pairs={{0,8},{1,9},{2,10},{3,11},{4,12},{5,13},{6,14},{7,15},{8,0},{9,1},... | collective-permute-start | bytes 786440 | tf_op jit(solution)/shard_map/ppermute | solution.py:226
  191.5 33.9 %collective-permute-start.32 = (f32[32,8,256]{2,1,0:T(8,128)S(1)}, f32[32,8,256]{2,1,0:T(8,128)S(1)}, u32[]{:S(2)}, u32[]{:S(2)}) collective-permute-start(f32[32,8,256]{2,1,0:T(8,128)S(1)} %bitcast.131), channel_id=1, source_target_pairs={{0,10},{1,11},{2,8},{3,9},{4,14},{5,15},{6,12},{7,13},{8,2},{9,3},... | collective-permute-start | bytes 786440 | tf_op jit(solution)/shard_map/ppermute | solution.py:226
  198.8 31.9 %collective-permute-start.33 = (f32[32,8,256]{2,1,0:T(8,128)S(1)}, f32[32,8,256]{2,1,0:T(8,128)S(1)}, u32[]{:S(2)}, u32[]{:S(2)}) collective-permute-start(f32[32,8,256]{2,1,0:T(8,128)S(1)} %bitcast.128), channel_id=1, source_target_pairs={{0,12},{1,13},{2,14},{3,15},{4,8},{5,9},{6,10},{7,11},{8,4},{9,5},... | collective-permute-start | bytes 786440 | tf_op jit(solution)/shard_map/ppermute | solution.py:226
  202.8 34.1 %collective-permute-start.34 = (f32[32,8,256]{2,1,0:T(8,128)S(1)}, f32[32,8,256]{2,1,0:T(8,128)S(1)}, u32[]{:S(2)}, u32[]{:S(2)}) collective-permute-start(f32[32,8,256]{2,1,0:T(8,128)S(1)} %bitcast.127), channel_id=1, source_target_pairs={{0,14},{1,15},{2,12},{3,13},{4,10},{5,11},{6,8},{7,9},{8,6},{9,7},... | collective-permute-start | bytes 786440 | tf_op jit(solution)/shard_map/ppermute | solution.py:226
  237.0 45.5 %collective-permute-start.36 = (f32[8,32,8,256]{3,2,1,0:T(8,128)S(1)}, f32[8,32,8,256]{3,2,1,0:T(8,128)S(1)}, u32[]{:S(2)}, u32[]{:S(2)}) collective-permute-start(f32[8,32,8,256]{3,2,1,0:T(8,128)S(1)} %get-tuple-element.124.cur.own), channel_id=1, source_target_pairs={{1,16},{3,18},{5,20},{7,22},{9,24},{11,26},{13,28},{15,30},{16,1},... | collective-permute-start | bytes 6291464 | tf_op jit(solution)/shard_map/ppermute | solution.py:236
  238.9 44.1 %collective-permute-start.35 = (f32[8,32,8,256]{3,2,1,0:T(8,128)S(1)}, f32[8,32,8,256]{3,2,1,0:T(8,128)S(1)}, u32[]{:S(2)}, u32[]{:S(2)}) collective-permute-start(f32[8,32,8,256]{3,2,1,0:T(8,128)S(1)} %get-tuple-element.124.cur.own), channel_id=1, source_target_pairs={{0,1},{1,0},{2,3},{3,2},{4,5},{5,4},{6,7},{7,6},{8,9},{9,8},{10,11... | collective-permute-start | bytes 6291464 | tf_op jit(solution)/shard_map/ppermute | solution.py:223
  241.8 11.6 %collective-permute-start.43 = (f32[32,8,256]{2,1,0:T(8,128)S(1)}, f32[32,8,256]{2,1,0:T(8,128)S(1)}, u32[]{:S(2)}, u32[]{:S(2)}) collective-permute-start(f32[32,8,256]{2,1,0:T(8,128)S(1)} %get-tuple-element.125), channel_id=1, source_target_pairs={{0,14},{1,15},{2,12},{3,13},{4,10},{5,11},{6,8},{7,9},{8,6},{9,7},... | collective-permute-start | bytes 786440 | tf_op jit(solution)/shard_map/ppermute | solution.py:226
  244.4 14.3 %collective-permute-start.42 = (f32[32,8,256]{2,1,0:T(8,128)S(1)}, f32[32,8,256]{2,1,0:T(8,128)S(1)}, u32[]{:S(2)}, u32[]{:S(2)}) collective-permute-start(f32[32,8,256]{2,1,0:T(8,128)S(1)} %get-tuple-element.127), channel_id=1, source_target_pairs={{0,12},{1,13},{2,14},{3,15},{4,8},{5,9},{6,10},{7,11},{8,4},{9,5},... | collective-permute-start | bytes 786440 | tf_op jit(solution)/shard_map/ppermute | solution.py:226
  246.2 17.5 %collective-permute-start.41 = (f32[32,8,256]{2,1,0:T(8,128)S(1)}, f32[32,8,256]{2,1,0:T(8,128)S(1)}, u32[]{:S(2)}, u32[]{:S(2)}) collective-permute-start(f32[32,8,256]{2,1,0:T(8,128)S(1)} %get-tuple-element.129), channel_id=1, source_target_pairs={{0,10},{1,11},{2,8},{3,9},{4,14},{5,15},{6,12},{7,13},{8,2},{9,3},... | collective-permute-start | bytes 786440 | tf_op jit(solution)/shard_map/ppermute | solution.py:226
  253.4 16.0 %collective-permute-start.40 = (f32[32,8,256]{2,1,0:T(8,128)S(1)}, f32[32,8,256]{2,1,0:T(8,128)S(1)}, u32[]{:S(2)}, u32[]{:S(2)}) collective-permute-start(f32[32,8,256]{2,1,0:T(8,128)S(1)} %get-tuple-element.131), channel_id=1, source_target_pairs={{0,8},{1,9},{2,10},{3,11},{4,12},{5,13},{6,14},{7,15},{8,0},{9,1},... | collective-permute-start | bytes 786440 | tf_op jit(solution)/shard_map/ppermute | solution.py:226
  258.7 11.1 %collective-permute-start.39 = (f32[32,8,256]{2,1,0:T(8,128)S(1)}, f32[32,8,256]{2,1,0:T(8,128)S(1)}, u32[]{:S(2)}, u32[]{:S(2)}) collective-permute-start(f32[32,8,256]{2,1,0:T(8,128)S(1)} %get-tuple-element.133), channel_id=1, source_target_pairs={{0,6},{1,7},{2,4},{3,5},{4,2},{5,3},{6,0},{7,1},{8,14},{9,15},{10,... | collective-permute-start | bytes 786440 | tf_op jit(solution)/shard_map/ppermute | solution.py:226
  263.7 10.2 %collective-permute-start.38 = (f32[32,8,256]{2,1,0:T(8,128)S(1)}, f32[32,8,256]{2,1,0:T(8,128)S(1)}, u32[]{:S(2)}, u32[]{:S(2)}) collective-permute-start(f32[32,8,256]{2,1,0:T(8,128)S(1)} %get-tuple-element.135), channel_id=1, source_target_pairs={{0,4},{1,5},{2,6},{3,7},{4,0},{5,1},{6,2},{7,3},{8,12},{9,13},{10,... | collective-permute-start | bytes 786440 | tf_op jit(solution)/shard_map/ppermute | solution.py:226
  269.7 43.3 %collective-permute-start.52 = (f32[8,16,8,256]{3,2,1,0:T(8,128)S(1)}, f32[8,16,8,256]{3,2,1,0:T(8,128)S(1)}, u32[]{:S(2)}, u32[]{:S(2)}) collective-permute-start(f32[8,16,8,256]{3,2,1,0:T(8,128)S(1)} %slice.24), channel_id=1, source_target_pairs={{0,1},{1,0},{2,3},{3,2},{4,5},{5,4},{6,7},{7,6},{8,9},{9,8},{10,11... | collective-permute-start | bytes 3145736 | tf_op jit(solution)/shard_map/ppermute | solution.py:223
  278.9 9.5 %collective-permute-start.44 = (f32[32,8,256]{2,1,0:T(8,128)S(1)}, f32[32,8,256]{2,1,0:T(8,128)S(1)}, u32[]{:S(2)}, u32[]{:S(2)}) collective-permute-start(f32[32,8,256]{2,1,0:T(8,128)S(1)} %bitcast.147), channel_id=1, source_target_pairs={{0,2},{1,3},{2,0},{3,1},{4,6},{5,7},{6,4},{7,5},{8,10},{9,11},{10,... | collective-permute-start | bytes 786440 | tf_op jit(solution)/shard_map/ppermute | solution.py:226
  280.6 12.7 %collective-permute-start.45 = (f32[32,8,256]{2,1,0:T(8,128)S(1)}, f32[32,8,256]{2,1,0:T(8,128)S(1)}, u32[]{:S(2)}, u32[]{:S(2)}) collective-permute-start(f32[32,8,256]{2,1,0:T(8,128)S(1)} %bitcast.140), channel_id=1, source_target_pairs={{0,4},{1,5},{2,6},{3,7},{4,0},{5,1},{6,2},{7,3},{8,12},{9,13},{10,... | collective-permute-start | bytes 786440 | tf_op jit(solution)/shard_map/ppermute | solution.py:226
  282.5 13.3 %collective-permute-start.46 = (f32[32,8,256]{2,1,0:T(8,128)S(1)}, f32[32,8,256]{2,1,0:T(8,128)S(1)}, u32[]{:S(2)}, u32[]{:S(2)}) collective-permute-start(f32[32,8,256]{2,1,0:T(8,128)S(1)} %bitcast.136), channel_id=1, source_target_pairs={{0,6},{1,7},{2,4},{3,5},{4,2},{5,3},{6,0},{7,1},{8,14},{9,15},{10,... | collective-permute-start | bytes 786440 | tf_op jit(solution)/shard_map/ppermute | solution.py:226
  283.1 14.3 %collective-permute-start.47 = (f32[32,8,256]{2,1,0:T(8,128)S(1)}, f32[32,8,256]{2,1,0:T(8,128)S(1)}, u32[]{:S(2)}, u32[]{:S(2)}) collective-permute-start(f32[32,8,256]{2,1,0:T(8,128)S(1)} %bitcast.134), channel_id=1, source_target_pairs={{0,8},{1,9},{2,10},{3,11},{4,12},{5,13},{6,14},{7,15},{8,0},{9,1},... | collective-permute-start | bytes 786440 | tf_op jit(solution)/shard_map/ppermute | solution.py:226
  288.4 9.0 %collective-permute-start.48 = (f32[32,8,256]{2,1,0:T(8,128)S(1)}, f32[32,8,256]{2,1,0:T(8,128)S(1)}, u32[]{:S(2)}, u32[]{:S(2)}) collective-permute-start(f32[32,8,256]{2,1,0:T(8,128)S(1)} %bitcast.132), channel_id=1, source_target_pairs={{0,10},{1,11},{2,8},{3,9},{4,14},{5,15},{6,12},{7,13},{8,2},{9,3},... | collective-permute-start | bytes 786440 | tf_op jit(solution)/shard_map/ppermute | solution.py:226
  293.2 12.8 %collective-permute-start.49 = (f32[32,8,256]{2,1,0:T(8,128)S(1)}, f32[32,8,256]{2,1,0:T(8,128)S(1)}, u32[]{:S(2)}, u32[]{:S(2)}) collective-permute-start(f32[32,8,256]{2,1,0:T(8,128)S(1)} %bitcast.130), channel_id=1, source_target_pairs={{0,12},{1,13},{2,14},{3,15},{4,8},{5,9},{6,10},{7,11},{8,4},{9,5},... | collective-permute-start | bytes 786440 | tf_op jit(solution)/shard_map/ppermute | solution.py:226
  295.8 13.9 %collective-permute-start.50 = (f32[32,8,256]{2,1,0:T(8,128)S(1)}, f32[32,8,256]{2,1,0:T(8,128)S(1)}, u32[]{:S(2)}, u32[]{:S(2)}) collective-permute-start(f32[32,8,256]{2,1,0:T(8,128)S(1)} %bitcast.129), channel_id=1, source_target_pairs={{0,14},{1,15},{2,12},{3,13},{4,10},{5,11},{6,8},{7,9},{8,6},{9,7},... | collective-permute-start | bytes 786440 | tf_op jit(solution)/shard_map/ppermute | solution.py:226
  (21 other events, 233.1 us)

commit v2 on v1

v2 whole, which is shorter than its diff:
```python
import functools

import jax
import jax.numpy as jnp
from jax import lax
from jax.experimental import pallas as pl
from jax.experimental.pallas import tpu as pltpu
from jax.sharding import PartitionSpec as P

SHIFT = 4.0
SPREAD = 7.0
CHIPS = 8
OCT = 8
CUTS = (3, 5)
F32 = jnp.float32
BF16 = jnp.bfloat16


def split(x):
    high = x.astype(BF16)
    return high, (x - high.astype(F32)).astype(BF16)


def mm(a, b):
    return jnp.dot(a, b, preferred_element_type=F32)


def params():
    return pltpu.CompilerParams(vmem_limit_bytes=32 * 1024 * 1024)


def prep(ids, radial, bond, angle):
    def kernel(ids, radial, bond, angle, rad_h, rad_l, bond_cat, ang_h, ang_l, tmp):
        def rows(ref):
            return jnp.concatenate(
                [ref[pl.ds(pl.multiple_of((i ^ ids[1]) * 16, 16), 16), :] for i in range(16)], 0
            )

        tmp[...] = rows(radial).T
        rad_h[...], rad_l[...] = split(rows(tmp) / SPREAD)
        high, low = split(bond[...] / SPREAD)
        bond_cat[...] = jnp.concatenate([high, high, low], 1)
        ang_h[...], ang_l[...] = split(angle[...].T / SPREAD)

    big = jax.ShapeDtypeStruct((256, 256), BF16)
    vm = pl.BlockSpec(memory_space=pltpu.VMEM)
    return pl.pallas_call(
        kernel,
        out_shape=(big, big, jax.ShapeDtypeStruct((64, 192), BF16), big, big),
        in_specs=[pl.BlockSpec(memory_space=pltpu.SMEM), vm, vm, vm],
        out_specs=(vm,) * 5,
        scratch_shapes=[pltpu.VMEM((256, 256), F32)],
        compiler_params=params(),
        name="prep",
    )(ids, radial, bond, angle)


def start(ids, ext, own, other):
    step = 8
    half = 16 // step

    def kernel(ids, ext, own, other, whole):
        i = pl.program_id(0)
        line = lax.broadcasted_iota(jnp.int32, (64, 256), 0)
        for r in range(step):
            x = jnp.where(i < half, own[0, r], other[r])
            whole[:, r] = jnp.where(line < ext[i * step + r], x, 0.0).reshape(CHIPS, OCT, 256)

    return pl.pallas_call(
        kernel,
        grid_spec=pltpu.PrefetchScalarGridSpec(
            num_scalar_prefetch=2,
            grid=(32 // step,),
            in_specs=[
                pl.BlockSpec((1, step, 64, 256), lambda i, ids, ext: (ids[1], jnp.minimum(i, half - 1), 0, 0)),
                pl.BlockSpec((step, 64, 256), lambda i, ids, ext: (jnp.maximum(i - half, 0), 0, 0)),
            ],
            out_specs=pl.BlockSpec((CHIPS, step, OCT, 256), lambda i, ids, ext: (0, i, 0, 0)),
        ),
        out_shape=pltpu.HBM((CHIPS, 32, OCT, 256), F32),
        compiler_params=params(),
        name="start",
    )(ids, ext, own, other)


def local_terms(ext, coef, cur, near, far, far_mid, far_top, pot, bond_cat, ang_h, ang_l, prev):
    step = 4

    def kernel(ext, coef, cur, near, far, far_mid, far_top, pot, bond_cat, ang_h, ang_l, *rest):
        prev, out = (rest[0], rest[1]) if len(rest) > 1 else (None, rest[0])
        first = pl.program_id(0) * step
        line = lax.broadcasted_iota(jnp.int32, (64, 256), 0)
        xs = [cur[:, r].reshape(64, 256) for r in range(step)]
        high, low = split(jnp.concatenate(xs, 0))
        angle = mm(high, ang_h[...]) + mm(low, ang_h[...]) + mm(high, ang_l[...])
        for r in range(step):
            part = slice(r * 64, r * 64 + 64)
            stack = jnp.concatenate([high[part], low[part], high[part]], 0)
            total = angle[part] + mm(bond_cat[...], stack)
            total = total + (pot[r] - SHIFT) * (1.0 / SPREAD) * xs[r]
            weight = coef[2 + first + r] * (1.0 / SPREAD)
            total = total - (weight * coef[0]) * near[:, r].reshape(64, 256)
            total = total - (weight * coef[1]) * jnp.concatenate(
                [f[:, r].reshape(-1, 256) for f in (far, far_mid, far_top)], 0
            )
            total = jnp.where(line < ext[first + r], total, 0.0)
            if prev is not None:
                total = 2.0 * total - prev[:, r].reshape(64, 256)
            out[:, r] = total.reshape(CHIPS, OCT, 256)

    whole = pl.BlockSpec((CHIPS, step, OCT, 256), lambda i: (0, i, 0, 0))
    def crossed(count):
        return pl.BlockSpec((count, step, OCT, 256), lambda i: (0, (i + 16 // step) % (32 // step), 0, 0))

    smem = pl.BlockSpec(memory_space=pltpu.SMEM)
    args = [ext, coef, cur, near, far, far_mid, far_top, pot, bond_cat, ang_h, ang_l]
    specs = [smem, smem, whole, crossed(CHIPS), crossed(CUTS[0]), crossed(CUTS[1] - CUTS[0]), crossed(CHIPS - CUTS[1]), pl.BlockSpec((step, 64, 256), lambda i: (i, 0, 0))]
    specs += [
        pl.BlockSpec((64, 192), lambda i: (0, 0)),
        pl.BlockSpec((256, 256), lambda i: (0, 0)),
        pl.BlockSpec((256, 256), lambda i: (0, 0)),
    ]
    if prev is not None:
        args.append(prev)
        specs.append(whole)
    return pl.pallas_call(
        kernel,
        grid=(32 // step,),
        in_specs=specs,
        out_specs=whole,
        out_shape=pltpu.HBM((CHIPS, 32, OCT, 256), F32),
        compiler_params=params(),
        cost_estimate=pl.CostEstimate(flops=2_000_000_000, bytes_accessed=14_000_000, transcendentals=0),
        name="local_terms",
    )(*args)


def radial_term(ids, ext_col, rad_h, rad_l, packet, scale, more=None):
    rows = CHIPS * 32 * OCT
    flat = [p.reshape(rows, 256) for p in ((packet,) if more is None else (packet, more))]
    count = len(flat)

    def kernel(ids, ext_col, rad_h, rad_l, *refs):
        ins, out = refs[:count], refs[count]

        def column(q):
            at = pl.ds(q, 256, stride=OCT)
            return ins[0][at, :] + ins[1][at, :] if count > 1 else ins[0][at, :]

        for q in range(0, OCT, 2):
            high, low = split(jnp.concatenate([column(q), column(q + 1)], 1))
            total = mm(rad_h[...], high) + mm(rad_h[...], low) + mm(rad_l[...], high)
            for i in range(2):
                half = total[:, i * 128 : i * 128 + 128]
                half = jnp.where(ext_col[...] > ids[0] * OCT + q + i, half * scale, 0.0)
                out[pl.ds(q + i, 256, stride=OCT), :] = half

    lanes = pl.BlockSpec((rows, 128), lambda i: (0, i))
    full = pl.BlockSpec((256, 256), lambda i: (0, 0))
    out = pl.pallas_call(
        kernel,
        grid=(2,),
        in_specs=[
            pl.BlockSpec(memory_space=pltpu.SMEM), pl.BlockSpec((256, 1), lambda i: (0, 0)), full, full
        ] + [lanes] * count,
        out_specs=lanes,
        out_shape=pltpu.HBM((rows, 256), F32),
        compiler_params=params(),
        cost_estimate=pl.CostEstimate(flops=2_000_000_000, bytes_accessed=5_000_000, transcendentals=0),
        name="radial_term",
    )(ids, ext_col, rad_h, rad_l, *flat)
    return out.reshape(CHIPS, 32, OCT, 256)


def finish(ids, own, other):
    def kernel(ids, own, other, out):
        out[ids[1]] = own[0]
        out[1 - ids[1]] = other[0]

    return pl.pallas_call(
        kernel,
        grid_spec=pltpu.PrefetchScalarGridSpec(
            num_scalar_prefetch=1,
            grid=(CHIPS,),
            in_specs=[
                pl.BlockSpec((1, 16, OCT, 256), lambda j, ids: (j, 0, 0, 0)),
                pl.BlockSpec((1, 16, OCT, 256), lambda j, ids: (j, 0, 0, 0)),
            ],
            out_specs=pl.BlockSpec((2, 16, OCT, 256), lambda j, ids: (0, 0, j, 0)),
        ),
        out_shape=jax.ShapeDtypeStruct((2, 16, 64, 256), F32),
        compiler_params=params(),
        name="finish",
    )(ids, own, other)


def shards(initial_packet, extents, potential, coriolis_weight, radial_kinetic, bond_kinetic, angle_kinetic):
    ka, ga = lax.axis_index("ka"), lax.axis_index("ga")
    chip, core = ga // 2, ga % 2
    ids = jnp.stack([chip, core]).astype(jnp.int32)
    groups = lax.axis_size("ka")
    members = lax.axis_size("ga")
    top = jnp.float32((2 * groups - 1) * (2 * groups))

    def swap_core(x):
        return lax.ppermute(x, "ga", [(g, g ^ 1) for g in range(members)])

    def swap_far(x, octets):
        count = groups if octets.start < CUTS[1] else groups // 2
        pairs = [
            (i * members + g, k * members + (g ^ 1))
            for i in range(count)
            for g in range(members)
            for k in (i + 1 if g % 2 else i - 1,)
            if 0 <= k < count
        ]
        return lax.ppermute(x[octets], ("ka", "ga"), pairs)

    def halo(t, turned):
        near = swap_core(t)
        low = swap_far(t, slice(0, CUTS[0]))
        top = swap_far(t, slice(CUTS[1], CHIPS))
        turned, near, low, top = lax.optimization_barrier((turned, near, low, top))
        t, turned = lax.optimization_barrier((t, turned))
        return turned, (near, low, swap_far(t, slice(*CUTS)), top)

    same_core = [list(range(c, members, 2)) for c in range(2)]

    def turn(x):
        return lax.all_to_all(x, "ga", 0, 0, axis_index_groups=same_core, tiled=True)

    other = swap_core(lax.dynamic_index_in_dim(initial_packet, 1 - core, 0, keepdims=False))
    pot = jnp.concatenate([potential, swap_core(potential)], 0)
    weight = jnp.concatenate([coriolis_weight, swap_core(coriolis_weight)])
    kvalue = (2 * ka + core).astype(F32)
    upper = jnp.sqrt(top - kvalue * (kvalue + 1.0))
    lower = jnp.where(kvalue > 0.0, jnp.sqrt(top - kvalue * (kvalue - 1.0)), 0.0)
    coef = jnp.concatenate(
        [jnp.stack([jnp.where(core == 0, upper, lower), jnp.where(core == 0, lower, upper)]), weight]
    )
    ext = lax.dynamic_index_in_dim(extents, core, 0, keepdims=False).reshape(16, 16)
    ext = jnp.where(core == 0, ext, ext.reshape(8, 2, 16)[:, ::-1].reshape(16, 16)).reshape(256)
    ext_col = ext[:, None]
    ext = lax.dynamic_slice_in_dim(ext, chip * 32, 32)

    rad_h, rad_l, bond_cat, ang_h, ang_l = prep(ids, radial_kinetic, bond_kinetic, angle_kinetic)

    def local(cur, halos, prev=None):
        return local_terms(ext, coef, cur, *halos, pot, bond_cat, ang_h, ang_l, prev)

    def radial(packet, scale, more=None):
        return radial_term(ids, ext_col, rad_h, rad_l, packet, scale, more)

    def outputs(whole):
        return finish(ids, whole, swap_core(whole[:, 16:]))

    t0 = start(ids, ext, initial_packet, other)
    turned, h0 = halo(t0, turn(t0))
    b0 = radial(turned, 1.0)
    a0 = local(t0, h0)
    t1 = a0 + turn(b0)
    turned, h1 = halo(t1, turn(a0))
    b1 = radial(turned, 2.0, b0)
    c1 = local(t1, h1, t0)
    t2 = c1 + turn(b1)
    turned, h2 = halo(t2, turn(t2))
    b2 = radial(turned, 2.0)
    c2 = local(t2, h2, t1)
    former = outputs(t2)
    c2, former = lax.optimization_barrier((c2, former))
    t3 = c2 + turn(b2)
    return outputs(t3), former


def solution(mesh):
    return jax.shard_map(
        shards,
        mesh=mesh,
        in_specs=(
            P("ka", "ga", None, None),
            P("ka", None),
            P("ga", None, None),
            P("ga"),
            P(),
            P(),
            P(),
        ),
        out_specs=(P("ka", "ga", None, None), P("ka", "ga", None, None)),
        check_vma=False,
    )
```

time: 323 us -> 257 us (0.80)
  waiting for transfers between devices: 176 us -> 106 us
  starting transfers between devices: 93 us -> 61.3 us
  local copies, waits for them, and re-layouts: 9.62 us -> 30.1 us
  other arithmetic: 1.18 us -> 11.3 us
  Pallas kernels: 38.9 us -> 46.1 us
    ppermute x45 -> x9, waiting for transfers between devices: 172 us -> 45.2 us  [swap_far(): return lax.ppermute(x[octets], ('ka', 'ga'), pairs)]
    all_to_all x0 -> x6, waiting for transfers between devices: none -> 57.1 us  [turn(): lax.all_to_all(x, 'ga', 0, 0, axis_index_groups=same_core, tiled=True)]
    ppermute x45 -> x9, starting transfers between devices: 74.9 us -> 22.9 us  [swap_far(): return lax.ppermute(x[octets], ('ka', 'ga'), pairs)]
    all_to_all x0 -> x6, starting transfers between devices: none -> 27.9 us  [turn(): lax.all_to_all(x, 'ga', 0, 0, axis_index_groups=same_core, tiled=True)]
    add x0 -> x3, other arithmetic: none -> 10.2 us  [the longest x1 3.83 us: shards(): t2 = c1 + turn(b1)]
    slice x2 -> x6, local copies, waits for them, and re-layouts: 0.08 us -> 8.42 us  [swap_far(): return lax.ppermute(x[octets], ('ka', 'ga'), pairs)]
    ppermute x8, starting transfers between devices: 18.1 us -> 10.6 us  [swap_core(): return lax.ppermute(x, 'ga', [(g, g ^ 1) for g in range(members)])]
    pallas_call x3, Pallas kernels: 14.5 us -> 21.6 us  [local_terms(): pl.pallas_call(kernel, grid=(32 // step,), in_specs=specs, out_specs=whol...]
  transfers between devices with their start and end apart: 53 -> 23, of which waited for: 30 -> 15; matrix products, arithmetic and copies ran while one was open for 1% -> 7% of each run, Pallas kernels for 9% -> 11%
where the time goes in v2:
time: 257 us; the launch traced here: 256 us
  waiting for transfers between devices  106 us (41%)
  starting transfers between devices  61.3 us (24%)
  Pallas kernels  46.1 us (18%)
  local copies, waits for them, and re-layouts  30.1 us (12%)
  other arithmetic  11.3 us (4%)
    all_to_all x6, waiting for transfers between devices, turn(): lax.all_to_all(x, 'ga', 0, 0, axis_index_groups=same_core, tiled=True)  57.1 us
    ppermute x9, waiting for transfers between devices, swap_far(): return lax.ppermute(x[octets], ('ka', 'ga'), pairs)  45.2 us
    all_to_all x6, starting transfers between devices, turn(): lax.all_to_all(x, 'ga', 0, 0, axis_index_groups=same_core, tiled=True)  27.9 us
    ppermute x9, starting transfers between devices, swap_far(): return lax.ppermute(x[octets], ('ka', 'ga'), pairs)  22.9 us
    pallas_call x3, Pallas kernels, local_terms(): pl.pallas_call(kernel, grid=(32 // step,), in_specs=specs, out_specs=whol...  21.6 us
    unnamed x41, local copies, waits for them, and re-layouts  12.6 us
    pallas_call x3, Pallas kernels, radial_term(): pl.pallas_call(kernel, grid=(2,), in_specs=[pl.BlockSpec(memory_space=plt...  11.8 us
    ppermute x8, starting transfers between devices, swap_core(): return lax.ppermute(x, 'ga', [(g, g ^ 1) for g in range(members)])  10.6 us
  transfers between devices with their start and end apart: 23, of which 15 were waited for; matrix products, arithmetic and copies ran while one was open for 7% of the time, Pallas kernels for 11%

profile of v2, /device:TPU:1, one launch (start us, length us, event | category | flops | bytes accessed | tf_op | source)
XLA Modules:
  0.0 255.5 jit_solution(1856195077532285469)
XLA Ops:
  0.7 2.4 dynamic-slice_bitcast_fusion
  3.1 3.2 %collective-permute-start.1 = (f32[16,64,256]{2,1,0:T(8,128)}, f32[16,64,256]{2,1,0:T(8,128)S(1)}, u32[]{:S(2)}, u32[]{:S(2)}) collective-permute-start(f32[16,64,256]{2,1,0:T(8,128)} %dynamic-slice_bitcast_fusion), channel_id=1, source_target_pairs={{0,1},{1,0},{2,3},{3,2},{4,5},{5,4},{6,7},{7,6},{8,9},{9,8},{10,11... | collective-permute-start | bytes 3145736 | tf_op jit(solution)/shard_map/ppermute | solution.py:206
  8.8 2.4 start.1.cur.rest_0_
  11.7 5.0 %all-to-all-start = ((f32[8,32,8,256]{3,2,1,0:T(8,128)}), f32[8,32,8,256]{3,2,1,0:T(8,128)}, u32[]{:S(2)}, u32[]{:S(2)}) async-start(f32[8,32,8,256]{3,2,1,0:T(8,128)} %start.1.cur.rest_0_), calls=%async_computation | async-start | bytes 4194304 | tf_op jit(solution)/shard_map/all_to_all | solution.py:230
  18.0 3.8 %collective-permute-start.4 = (f32[3,32,8,256]{3,2,1,0:T(8,128)}, f32[3,32,8,256]{3,2,1,0:T(8,128)S(1)}, u32[]{:S(2)}, u32[]{:S(2)}) collective-permute-start(f32[3,32,8,256]{3,2,1,0:T(8,128)} %get-tuple-element.58), channel_id=1, source_target_pairs={{1,16},{3,18},{5,20},{7,22},{9,24},{11,26},{13,28},{15,30},{16,1},... | collective-permute-start | bytes 2359304 | tf_op jit(solution)/shard_map/ppermute | solution.py:217
  21.8 1.9 collective-permute-start.3
  28.1 4.0 %collective-permute-done.4.far_top = f32[3,32,8,256]{3,2,1,0:T(8,128)S(1)} collective-permute-done((f32[3,32,8,256]{3,2,1,0:T(8,128)}, f32[3,32,8,256]{3,2,1,0:T(8,128)S(1)}, u32[]{:S(2)}, u32[]{:S(2)}) %collective-permute-start.4) | collective-permute-done | bytes 786464 | tf_op jit(solution)/shard_map/ppermute | solution.py:217
  32.1 8.4 %collective-permute-done.3.far = f32[3,32,8,256]{3,2,1,0:T(8,128)} collective-permute-done((f32[3,32,8,256]{3,2,1,0:T(8,128)}, f32[3,32,8,256]{3,2,1,0:T(8,128)}, u32[]{:S(2)}, u32[]{:S(2)}) %collective-permute-start.3) | collective-permute-done | bytes 786464 | tf_op jit(solution)/shard_map/ppermute | solution.py:217
  40.5 10.7 %all-to-all-done = f32[8,32,8,256]{3,2,1,0:T(8,128)} async-done(((f32[8,32,8,256]{3,2,1,0:T(8,128)}), f32[8,32,8,256]{3,2,1,0:T(8,128)}, u32[]{:S(2)}, u32[]{:S(2)}) %all-to-all-start) | async-done | bytes 2097184 | tf_op jit(solution)/shard_map/all_to_all | solution.py:230
  53.1 3.8 %radial_term.3.refs_1_ = f32[2048,256]{1,0:T(8,128)} custom-call(s32[2]{0:T(128)S(1)} %pad_add_fusion.ids, s32[256,1]{1,0:T(8,128)S(1)} %broadcast_select_fusion.ext_col, bf16[256,256]{1,0:T(8,128)(2,1)S(1)} %copy-done.12, bf16[256,256]{1,0:T(8,128)(2,1)S(1)} %copy-done.15, f32[2048,256]{1,0:T(8,128)} %bitcast.7.refs_0_), custom_call_target="tpu_custom_call" | custom-call | flops 2000000000 | bytes 5000000 | tf_op jit(solution)/shard_map/radial_term/pallas_call | solution.py:160
  56.9 4.5 %all-to-all-start.1 = ((f32[8,32,8,256]{3,2,1,0:T(8,128)}), f32[8,32,8,256]{3,2,1,0:T(8,128)}, u32[]{:S(2)}, u32[]{:S(2)}) async-start(f32[8,32,8,256]{3,2,1,0:T(8,128)} %bitcast.14), calls=%async_computation.1 | async-start | bytes 4194304 | tf_op jit(solution)/shard_map/all_to_all | solution.py:230
  63.6 1.9 collective-permute-start.5
  65.7 2.3 constant_dynamic-update-slice_fusion.1
  68.1 2.3 constant_dynamic-update-slice_fusion.pot
  70.4 4.3 %collective-permute-done.5.far_mid = f32[2,32,8,256]{3,2,1,0:T(8,128)} collective-permute-done((f32[2,32,8,256]{3,2,1,0:T(8,128)}, f32[2,32,8,256]{3,2,1,0:T(8,128)}, u32[]{:S(2)}, u32[]{:S(2)}) %collective-permute-start.5) | collective-permute-done | bytes 524320 | tf_op jit(solution)/shard_map/ppermute | solution.py:217
  74.7 1.6 copy-done.1
  76.3 7.0 %local_terms.3 = f32[8,32,8,256]{3,2,1,0:T(8,128)} custom-call(s32[32]{0:T(128)S(1)} %dynamic_slice.12.ext, f32[34]{0:T(128)S(1)} %pad_maximum_fusion.coef, f32[8,32,8,256]{3,2,1,0:T(8,128)S(1)} %copy-done, f32[8,32,8,256]{3,2,1,0:T(8,128)} %collective-permute-done.2.near, f32[3,32,8,256]{3,2,1,0:T(8,128)} %collective-permute-done.3.far, ...), custom_call_target="tpu_custom_call" | custom-call | flops 2000000000 | bytes 14000000 | tf_op jit(solution)/shard_map/local_terms/pallas_call | solution.py:126
  83.3 8.8 %all-to-all-done.1 = f32[8,32,8,256]{3,2,1,0:T(8,128)} async-done(((f32[8,32,8,256]{3,2,1,0:T(8,128)}), f32[8,32,8,256]{3,2,1,0:T(8,128)}, u32[]{:S(2)}, u32[]{:S(2)}) %all-to-all-start.1) | async-done | bytes 2097184 | tf_op jit(solution)/shard_map/all_to_all | solution.py:230
  92.1 3.8 %add.39.cur.rest_0_ = f32[8,32,8,256]{3,2,1,0:T(8,128)} add(f32[8,32,8,256]{3,2,1,0:T(8,128)} %local_terms.3, f32[8,32,8,256]{3,2,1,0:T(8,128)} %all-to-all-done.1) | non-fusion elementwise | flops 524288 | bytes 6291456 | tf_op jit(solution)/shard_map/add | solution.py:261
  95.9 2.2 collective-permute-start.7
  98.1 4.4 %all-to-all-start.2 = ((f32[8,32,8,256]{3,2,1,0:T(8,128)}), f32[8,32,8,256]{3,2,1,0:T(8,128)}, u32[]{:S(2)}, u32[]{:S(2)}) async-start(f32[8,32,8,256]{3,2,1,0:T(8,128)} %local_terms.3), calls=%async_computation.2 | async-start | bytes 4194304 | tf_op jit(solution)/shard_map/all_to_all | solution.py:230
  102.5 2.7 %fusion.2 = (f32[3,32,8,256]{3,2,1,0:T(8,128)}, f32[3,32,8,256]{3,2,1,0:T(8,128)}) fusion(f32[8,32,8,256]{3,2,1,0:T(8,128)} %add.39.cur.rest_0_), kind=kLoop, calls=%fused_computation.10 | loop fusion | bytes 3145728 | tf_op jit(solution)/shard_map/slice | solution.py:217
  105.2 1.9 collective-permute-start.9
  107.2 3.6 %collective-permute-start.8 = (f32[3,32,8,256]{3,2,1,0:T(8,128)}, f32[3,32,8,256]{3,2,1,0:T(8,128)}, u32[]{:S(2)}, u32[]{:S(2)}) collective-permute-start(f32[3,32,8,256]{3,2,1,0:T(8,128)} %get-tuple-element.57), channel_id=1, source_target_pairs={{1,16},{3,18},{5,20},{7,22},{9,24},{11,26},{13,28},{15,30},{16,1},... | collective-permute-start | bytes 2359304 | tf_op jit(solution)/shard_map/ppermute | solution.py:217
  110.8 25.8 %all-to-all-done.2 = f32[8,32,8,256]{3,2,1,0:T(8,128)} async-done(((f32[8,32,8,256]{3,2,1,0:T(8,128)}), f32[8,32,8,256]{3,2,1,0:T(8,128)}, u32[]{:S(2)}, u32[]{:S(2)}) %all-to-all-start.2) | async-done | bytes 2097184 | tf_op jit(solution)/shard_map/all_to_all | solution.py:230
  139.2 4.1 %radial_term.4 = f32[2048,256]{1,0:T(8,128)} custom-call(s32[2]{0:T(128)S(1)} %pad_add_fusion.ids, s32[256,1]{1,0:T(8,128)S(1)} %broadcast_select_fusion.ext_col, bf16[256,256]{1,0:T(8,128)(2,1)S(1)} %copy-done.13, bf16[256,256]{1,0:T(8,128)(2,1)S(1)} %copy-done.16, f32[2048,256]{1,0:T(8,128)} %bitcast.9.refs_0_, f32[2048,256]{1,0:T(8,128)S(1)} %copy-done.5), custom_call_target="tpu_custom_call" | custom-call | flops 2000000000 | bytes 5000000 | tf_op jit(solution)/shard_map/radial_term/pallas_call | solution.py:160
  143.3 4.4 %all-to-all-start.3 = ((f32[8,32,8,256]{3,2,1,0:T(8,128)}), f32[8,32,8,256]{3,2,1,0:T(8,128)}, u32[]{:S(2)}, u32[]{:S(2)}) async-start(f32[8,32,8,256]{3,2,1,0:T(8,128)} %bitcast.16), calls=%async_computation.3 | async-start | bytes 4194304 | tf_op jit(solution)/shard_map/all_to_all | solution.py:230
  148.8 1.9 collective-permute-start.10
  150.7 9.0 %collective-permute-done.10.far_mid = f32[2,32,8,256]{3,2,1,0:T(8,128)S(1)} collective-permute-done((f32[2,32,8,256]{3,2,1,0:T(8,128)S(1)}, f32[2,32,8,256]{3,2,1,0:T(8,128)S(1)}, u32[]{:S(2)}, u32[]{:S(2)}) %collective-permute-start.10) | collective-permute-done | bytes 524320 | tf_op jit(solution)/shard_map/ppermute | solution.py:217
  161.2 7.3 %local_terms.4 = f32[8,32,8,256]{3,2,1,0:T(8,128)} custom-call(s32[32]{0:T(128)S(1)} %dynamic_slice.12.ext, f32[34]{0:T(128)S(1)} %pad_maximum_fusion.coef, f32[8,32,8,256]{3,2,1,0:T(8,128)} %add.39.cur.rest_0_, f32[8,32,8,256]{3,2,1,0:T(8,128)} %collective-permute-done.7.near, f32[3,32,8,256]{3,2,1,0:T(8,128)} %collective-permute-done.8.far, ...), custom_call_target="tpu_custom_call" | custom-call | flops 2000000000 | bytes 14000000 | tf_op jit(solution)/shard_map/local_terms/pallas_call | solution.py:126
  168.6 5.3 %all-to-all-done.3 = f32[8,32,8,256]{3,2,1,0:T(8,128)} async-done(((f32[8,32,8,256]{3,2,1,0:T(8,128)}), f32[8,32,8,256]{3,2,1,0:T(8,128)}, u32[]{:S(2)}, u32[]{:S(2)}) %all-to-all-start.3) | async-done | bytes 2097184 | tf_op jit(solution)/shard_map/all_to_all | solution.py:230
  173.9 3.8 %add.40.cur.own = f32[8,32,8,256]{3,2,1,0:T(8,128)} add(f32[8,32,8,256]{3,2,1,0:T(8,128)} %local_terms.4, f32[8,32,8,256]{3,2,1,0:T(8,128)} %all-to-all-done.3) | non-fusion elementwise | flops 524288 | bytes 6291456 | tf_op jit(solution)/shard_map/add | solution.py:265
  178.9 4.5 %all-to-all-start.4 = ((f32[8,32,8,256]{3,2,1,0:T(8,128)}), f32[8,32,8,256]{3,2,1,0:T(8,128)}, u32[]{:S(2)}, u32[]{:S(2)}) async-start(f32[8,32,8,256]{3,2,1,0:T(8,128)} %add.40.cur.own), calls=%async_computation.4 | async-start | bytes 4194304 | tf_op jit(solution)/shard_map/all_to_all | solution.py:230
  184.8 1.9 collective-permute-start.13
  186.7 3.6 %collective-permute-start.12 = (f32[3,32,8,256]{3,2,1,0:T(8,128)S(1)}, f32[3,32,8,256]{3,2,1,0:T(8,128)S(1)}, u32[]{:S(2)}, u32[]{:S(2)}) collective-permute-start(f32[3,32,8,256]{3,2,1,0:T(8,128)S(1)} %get-tuple-element.55), channel_id=1, source_target_pairs={{1,16},{3,18},{5,20},{7,22},{9,24},{11,26},{13,28},{15,30},{16,1},... | collective-permute-start | bytes 2359304 | tf_op jit(solution)/shard_map/ppermute | solution.py:217
  190.4 8.1 %collective-permute-done.13.far_top = f32[3,32,8,256]{3,2,1,0:T(8,128)S(1)} collective-permute-done((f32[3,32,8,256]{3,2,1,0:T(8,128)S(1)}, f32[3,32,8,256]{3,2,1,0:T(8,128)S(1)}, u32[]{:S(2)}, u32[]{:S(2)}) %collective-permute-start.13) | collective-permute-done | bytes 786464 | tf_op jit(solution)/shard_map/ppermute | solution.py:217
  198.5 8.4 %collective-permute-done.12.far = f32[3,32,8,256]{3,2,1,0:T(8,128)S(1)} collective-permute-done((f32[3,32,8,256]{3,2,1,0:T(8,128)S(1)}, f32[3,32,8,256]{3,2,1,0:T(8,128)S(1)}, u32[]{:S(2)}, u32[]{:S(2)}) %collective-permute-start.12) | collective-permute-done | bytes 786464 | tf_op jit(solution)/shard_map/ppermute | solution.py:217
  207.8 1.8 all-to-all-done.4
  210.6 3.9 %radial_term.5 = f32[2048,256]{1,0:T(8,128)} custom-call(s32[2]{0:T(128)S(1)} %pad_add_fusion.ids, s32[256,1]{1,0:T(8,128)S(1)} %broadcast_select_fusion.ext_col, bf16[256,256]{1,0:T(8,128)(2,1)S(1)} %copy-done.13, bf16[256,256]{1,0:T(8,128)(2,1)S(1)} %copy-done.17, f32[2048,256]{1,0:T(8,128)} %bitcast.11.refs_0_), custom_call_target="tpu_custom_call" | custom-call | flops 2000000000 | bytes 5000000 | tf_op jit(solution)/shard_map/radial_term/pallas_call | solution.py:160
  214.4 5.2 %all-to-all-start.5 = ((f32[8,32,8,256]{3,2,1,0:T(8,128)}), f32[8,32,8,256]{3,2,1,0:T(8,128)}, u32[]{:S(2)}, u32[]{:S(2)}) async-start(f32[8,32,8,256]{3,2,1,0:T(8,128)} %bitcast.15), calls=%async_computation.5 | async-start | bytes 4194304 | tf_op jit(solution)/shard_map/all_to_all | solution.py:230
  222.8 2.2 collective-permute-start.14
  225.0 5.9 %finish.2 = f32[2,16,64,256]{3,2,1,0:T(8,128)} custom-call(s32[2]{0:T(128)S(1)} %pad_add_fusion.ids, f32[8,32,8,256]{3,2,1,0:T(8,128)} %add.40.cur.own, f32[8,16,8,256]{3,2,1,0:T(8,128)S(1)} %collective-permute-done.15.other), custom_call_target="tpu_custom_call" | custom-call | tf_op jit(solution)/shard_map/finish/pallas_call | solution.py:180
  231.0 3.0 %collective-permute-done.14.far_mid = f32[2,32,8,256]{3,2,1,0:T(8,128)S(1)} collective-permute-done((f32[2,32,8,256]{3,2,1,0:T(8,128)S(1)}, f32[2,32,8,256]{3,2,1,0:T(8,128)S(1)}, u32[]{:S(2)}, u32[]{:S(2)}) %collective-permute-start.14) | collective-permute-done | bytes 524320 | tf_op jit(solution)/shard_map/ppermute | solution.py:217
  234.0 7.3 %local_terms.5 = f32[8,32,8,256]{3,2,1,0:T(8,128)} custom-call(s32[32]{0:T(128)S(1)} %dynamic_slice.12.ext, f32[34]{0:T(128)S(1)} %pad_maximum_fusion.coef, f32[8,32,8,256]{3,2,1,0:T(8,128)} %add.40.cur.own, f32[8,32,8,256]{3,2,1,0:T(8,128)S(1)} %collective-permute-done.11.near, f32[3,32,8,256]{3,2,1,0:T(8,128)S(1)} %copy-done.7, ...), custom_call_target="tpu_custom_call" | custom-call | flops 2000000000 | bytes 14000000 | tf_op jit(solution)/shard_map/local_terms/pallas_call | solution.py:126
  241.3 4.6 %all-to-all-done.5 = f32[8,32,8,256]{3,2,1,0:T(8,128)} async-done(((f32[8,32,8,256]{3,2,1,0:T(8,128)}), f32[8,32,8,256]{3,2,1,0:T(8,128)}, u32[]{:S(2)}, u32[]{:S(2)}) %all-to-all-start.5) | async-done | bytes 2097184 | tf_op jit(solution)/shard_map/all_to_all | solution.py:230
  245.9 2.5 add.41.own
  249.7 2.3 collective-permute-done.16.other
  252.0 3.5 %finish.3 = f32[2,16,64,256]{3,2,1,0:T(8,128)} custom-call(s32[2]{0:T(128)S(1)} %pad_add_fusion.ids, f32[8,32,8,256]{3,2,1,0:T(8,128)S(1)} %add.41.own, f32[8,16,8,256]{3,2,1,0:T(8,128)S(1)} %collective-permute-done.16.other), custom_call_target="tpu_custom_call" | custom-call | tf_op jit(solution)/shard_map/finish/pallas_call | solution.py:180
  (74 shorter events, 26.8 us)
Async XLA Ops:
  0.6 8.2 %copy-start.4 = (f32[2,16,64,256]{3,2,1,0:T(8,128)S(1)}, f32[2,16,64,256]{3,2,1,0:T(8,128)}, u32[]{:S(2)}) copy-start(f32[2,16,64,256]{3,2,1,0:T(8,128)} %own.1) | copy-start | bytes 6291460
  0.6 6.2 %copy-start.19 = (s32[2,256]{1,0:T(2,128)S(1)}, s32[2,256]{1,0:T(2,128)}, u32[]{:S(2)}) copy-start(s32[2,256]{1,0:T(2,128)} %param.8) | copy-start | bytes 6148
  3.1 5.7 %collective-permute-start.1 = (f32[16,64,256]{2,1,0:T(8,128)}, f32[16,64,256]{2,1,0:T(8,128)S(1)}, u32[]{:S(2)}, u32[]{:S(2)}) collective-permute-start(f32[16,64,256]{2,1,0:T(8,128)} %dynamic-slice_bitcast_fusion), channel_id=1, source_target_pairs={{0,1},{1,0},{2,3},{3,2},{4,5},{5,4},{6,7},{7,6},{8,9},{9,8},{10,11... | collective-permute-start | bytes 3145736 | tf_op jit(solution)/shard_map/ppermute | solution.py:206
  11.3 5.4 %copy-start = (f32[8,32,8,256]{3,2,1,0:T(8,128)S(1)}, f32[8,32,8,256]{3,2,1,0:T(8,128)}, u32[]{:S(2)}) copy-start(f32[8,32,8,256]{3,2,1,0:T(8,128)} %start.1.cur.rest_0_) | copy-start | bytes 6291460
  11.3 40.0 %collective-permute-start.2 = (f32[8,32,8,256]{3,2,1,0:T(8,128)}, f32[8,32,8,256]{3,2,1,0:T(8,128)}, u32[]{:S(2)}, u32[]{:S(2)}) collective-permute-start(f32[8,32,8,256]{3,2,1,0:T(8,128)} %start.1.cur.rest_0_), channel_id=1, source_target_pairs={{0,1},{1,0},{2,3},{3,2},{4,5},{5,4},{6,7},{7,6},{8,9},{9,8},{10,11... | collective-permute-start | bytes 6291464 | tf_op jit(solution)/shard_map/ppermute | solution.py:206
  11.7 39.6 %all-to-all-start = ((f32[8,32,8,256]{3,2,1,0:T(8,128)}), f32[8,32,8,256]{3,2,1,0:T(8,128)}, u32[]{:S(2)}, u32[]{:S(2)}) async-start(f32[8,32,8,256]{3,2,1,0:T(8,128)} %start.1.cur.rest_0_), calls=%async_computation | async-start | bytes 4194304 | tf_op jit(solution)/shard_map/all_to_all | solution.py:230
  16.7 8.6 %copy-start.8 = (f32[256,256]{1,0:T(8,128)S(1)}, f32[256,256]{1,0:T(8,128)}, u32[]{:S(2)}) copy-start(f32[256,256]{1,0:T(8,128)} %radial.1) | copy-start | bytes 786436
  16.7 8.6 %copy-start.10 = (f32[64,64]{1,0:T(8,128)S(1)}, f32[64,64]{1,0:T(8,128)}, u32[]{:S(2)}) copy-start(f32[64,64]{1,0:T(8,128)} %bond.1) | copy-start | bytes 49156
  18.0 14.1 %collective-permute-start.4 = (f32[3,32,8,256]{3,2,1,0:T(8,128)}, f32[3,32,8,256]{3,2,1,0:T(8,128)S(1)}, u32[]{:S(2)}, u32[]{:S(2)}) collective-permute-start(f32[3,32,8,256]{3,2,1,0:T(8,128)} %get-tuple-element.58), channel_id=1, source_target_pairs={{1,16},{3,18},{5,20},{7,22},{9,24},{11,26},{13,28},{15,30},{16,1},... | collective-permute-start | bytes 2359304 | tf_op jit(solution)/shard_map/ppermute | solution.py:217
  21.8 18.7 %collective-permute-start.3 = (f32[3,32,8,256]{3,2,1,0:T(8,128)}, f32[3,32,8,256]{3,2,1,0:T(8,128)}, u32[]{:S(2)}, u32[]{:S(2)}) collective-permute-start(f32[3,32,8,256]{3,2,1,0:T(8,128)} %get-tuple-element.59), channel_id=1, source_target_pairs={{1,16},{3,18},{5,20},{7,22},{9,24},{11,26},{13,28},{15,30},{16,1},... | collective-permute-start | bytes 2359304 | tf_op jit(solution)/shard_map/ppermute | solution.py:217
  25.3 1.0 copy-start.9
  27.1 5.0 %copy-start.11 = (bf16[256,256]{1,0:T(8,128)(2,1)}, bf16[256,256]{1,0:T(8,128)(2,1)S(1)}, u32[]{:S(2)}) copy-start(bf16[256,256]{1,0:T(8,128)(2,1)S(1)} %get-tuple-element.35.rad_h) | copy-start | bytes 393220
  27.1 5.0 %copy-start.14 = (bf16[256,256]{1,0:T(8,128)(2,1)}, bf16[256,256]{1,0:T(8,128)(2,1)S(1)}, u32[]{:S(2)}) copy-start(bf16[256,256]{1,0:T(8,128)(2,1)S(1)} %get-tuple-element.36.rad_l) | copy-start | bytes 393220
  51.3 0.9 copy-start.12
  52.2 0.9 copy-start.15
  56.9 8.6 %copy-start.18 = (f32[16]{0:T(128)S(1)}, f32[16]{0:T(128)}, u32[]{:S(2)}) copy-start(f32[16]{0:T(128)} %param.10) | copy-start | bytes 196
  56.9 35.2 %all-to-all-start.1 = ((f32[8,32,8,256]{3,2,1,0:T(8,128)}), f32[8,32,8,256]{3,2,1,0:T(8,128)}, u32[]{:S(2)}, u32[]{:S(2)}) async-start(f32[8,32,8,256]{3,2,1,0:T(8,128)} %bitcast.14), calls=%async_computation.1 | async-start | bytes 4194304 | tf_op jit(solution)/shard_map/all_to_all | solution.py:230
  61.4 6.7 %collective-permute-start.6 = (f32[16,64,256]{2,1,0:T(8,128)}, f32[16,64,256]{2,1,0:T(8,128)}, u32[]{:S(2)}, u32[]{:S(2)}) collective-permute-start(f32[16,64,256]{2,1,0:T(8,128)} %param.9), channel_id=1, source_target_pairs={{0,1},{1,0},{2,3},{3,2},{4,5},{5,4},{6,7},{7,6},{8,9},{9,8},{10,11... | collective-permute-start | bytes 3145736 | tf_op jit(solution)/shard_map/ppermute | solution.py:206
  63.6 11.1 %collective-permute-start.5 = (f32[2,32,8,256]{3,2,1,0:T(8,128)}, f32[2,32,8,256]{3,2,1,0:T(8,128)}, u32[]{:S(2)}, u32[]{:S(2)}) collective-permute-start(f32[2,32,8,256]{3,2,1,0:T(8,128)} %slice.35), channel_id=1, source_target_pairs={{1,16},{3,18},{5,20},{7,22},{9,24},{11,26},{13,28},{15,30},{16,1},... | collective-permute-start | bytes 1572872 | tf_op jit(solution)/shard_map/ppermute | solution.py:217
  65.5 2.5 collective-permute-start
  74.7 1.6 copy-start.1
  95.9 40.8 %collective-permute-start.7 = (f32[8,32,8,256]{3,2,1,0:T(8,128)}, f32[8,32,8,256]{3,2,1,0:T(8,128)}, u32[]{:S(2)}, u32[]{:S(2)}) collective-permute-start(f32[8,32,8,256]{3,2,1,0:T(8,128)} %add.39.cur.rest_0_), channel_id=1, source_target_pairs={{0,1},{1,0},{2,3},{3,2},{4,5},{5,4},{6,7},{7,6},{8,9},{9,8},{10,11... | collective-permute-start | bytes 6291464 | tf_op jit(solution)/shard_map/ppermute | solution.py:206
  98.1 38.5 %all-to-all-start.2 = ((f32[8,32,8,256]{3,2,1,0:T(8,128)}), f32[8,32,8,256]{3,2,1,0:T(8,128)}, u32[]{:S(2)}, u32[]{:S(2)}) async-start(f32[8,32,8,256]{3,2,1,0:T(8,128)} %local_terms.3), calls=%async_computation.2 | async-start | bytes 4194304 | tf_op jit(solution)/shard_map/all_to_all | solution.py:230
  102.5 34.2 %copy-start.13 = (bf16[256,256]{1,0:T(8,128)(2,1)S(1)}, bf16[256,256]{1,0:T(8,128)(2,1)}, u32[]{:S(2)}) copy-start(bf16[256,256]{1,0:T(8,128)(2,1)} %copy-done.11) | copy-start | bytes 393220
  105.2 31.4 %collective-permute-start.9 = (f32[3,32,8,256]{3,2,1,0:T(8,128)}, f32[3,32,8,256]{3,2,1,0:T(8,128)S(1)}, u32[]{:S(2)}, u32[]{:S(2)}) collective-permute-start(f32[3,32,8,256]{3,2,1,0:T(8,128)} %get-tuple-element.56), channel_id=1, source_target_pairs={{1,16},{3,18},{5,20},{7,22},{9,24},{11,26},{13,28},{15,30},{16,1},... | collective-permute-start | bytes 2359304 | tf_op jit(solution)/shard_map/ppermute | solution.py:217
  107.2 29.5 %collective-permute-start.8 = (f32[3,32,8,256]{3,2,1,0:T(8,128)}, f32[3,32,8,256]{3,2,1,0:T(8,128)}, u32[]{:S(2)}, u32[]{:S(2)}) collective-permute-start(f32[3,32,8,256]{3,2,1,0:T(8,128)} %get-tuple-element.57), channel_id=1, source_target_pairs={{1,16},{3,18},{5,20},{7,22},{9,24},{11,26},{13,28},{15,30},{16,1},... | collective-permute-start | bytes 2359304 | tf_op jit(solution)/shard_map/ppermute | solution.py:217
  136.7 1.6 copy-start.5
  138.3 0.9 copy-start.16
  143.3 30.6 %all-to-all-start.3 = ((f32[8,32,8,256]{3,2,1,0:T(8,128)}), f32[8,32,8,256]{3,2,1,0:T(8,128)}, u32[]{:S(2)}, u32[]{:S(2)}) async-start(f32[8,32,8,256]{3,2,1,0:T(8,128)} %bitcast.16), calls=%async_computation.3 | async-start | bytes 4194304 | tf_op jit(solution)/shard_map/all_to_all | solution.py:230
  148.8 10.9 %collective-permute-start.10 = (f32[2,32,8,256]{3,2,1,0:T(8,128)S(1)}, f32[2,32,8,256]{3,2,1,0:T(8,128)S(1)}, u32[]{:S(2)}, u32[]{:S(2)}) collective-permute-start(f32[2,32,8,256]{3,2,1,0:T(8,128)S(1)} %slice.38), channel_id=1, source_target_pairs={{1,16},{3,18},{5,20},{7,22},{9,24},{11,26},{13,28},{15,30},{16,1},... | collective-permute-start | bytes 1572872 | tf_op jit(solution)/shard_map/ppermute | solution.py:217
  159.7 1.6 copy-start.2
  177.7 32.0 %collective-permute-start.11 = (f32[8,32,8,256]{3,2,1,0:T(8,128)}, f32[8,32,8,256]{3,2,1,0:T(8,128)S(1)}, u32[]{:S(2)}, u32[]{:S(2)}) collective-permute-start(f32[8,32,8,256]{3,2,1,0:T(8,128)} %add.40.cur.own), channel_id=1, source_target_pairs={{0,1},{1,0},{2,3},{3,2},{4,5},{5,4},{6,7},{7,6},{8,9},{9,8},{10,11... | collective-permute-start | bytes 6291464 | tf_op jit(solution)/shard_map/ppermute | solution.py:206
  178.9 30.8 %all-to-all-start.4 = ((f32[8,32,8,256]{3,2,1,0:T(8,128)}), f32[8,32,8,256]{3,2,1,0:T(8,128)}, u32[]{:S(2)}, u32[]{:S(2)}) async-start(f32[8,32,8,256]{3,2,1,0:T(8,128)} %add.40.cur.own), calls=%async_computation.4 | async-start | bytes 4194304 | tf_op jit(solution)/shard_map/all_to_all | solution.py:230
  184.8 13.7 %collective-permute-start.13 = (f32[3,32,8,256]{3,2,1,0:T(8,128)S(1)}, f32[3,32,8,256]{3,2,1,0:T(8,128)S(1)}, u32[]{:S(2)}, u32[]{:S(2)}) collective-permute-start(f32[3,32,8,256]{3,2,1,0:T(8,128)S(1)} %get-tuple-element.54), channel_id=1, source_target_pairs={{1,16},{3,18},{5,20},{7,22},{9,24},{11,26},{13,28},{15,30},{16,1},... | collective-permute-start | bytes 2359304 | tf_op jit(solution)/shard_map/ppermute | solution.py:217
  186.7 20.2 %collective-permute-start.12 = (f32[3,32,8,256]{3,2,1,0:T(8,128)S(1)}, f32[3,32,8,256]{3,2,1,0:T(8,128)S(1)}, u32[]{:S(2)}, u32[]{:S(2)}) collective-permute-start(f32[3,32,8,256]{3,2,1,0:T(8,128)S(1)} %get-tuple-element.55), channel_id=1, source_target_pairs={{1,16},{3,18},{5,20},{7,22},{9,24},{11,26},{13,28},{15,30},{16,1},... | collective-permute-start | bytes 2359304 | tf_op jit(solution)/shard_map/ppermute | solution.py:217
  206.9 0.9 copy-start.6
  209.7 0.9 copy-start.17
  214.4 31.4 %all-to-all-start.5 = ((f32[8,32,8,256]{3,2,1,0:T(8,128)}), f32[8,32,8,256]{3,2,1,0:T(8,128)}, u32[]{:S(2)}, u32[]{:S(2)}) async-start(f32[8,32,8,256]{3,2,1,0:T(8,128)} %bitcast.15), calls=%async_computation.5 | async-start | bytes 4194304 | tf_op jit(solution)/shard_map/all_to_all | solution.py:230
  220.9 4.1 %collective-permute-start.15 = (f32[8,16,8,256]{3,2,1,0:T(8,128)S(1)}, f32[8,16,8,256]{3,2,1,0:T(8,128)S(1)}, u32[]{:S(2)}, u32[]{:S(2)}) collective-permute-start(f32[8,16,8,256]{3,2,1,0:T(8,128)S(1)} %slice.50), channel_id=1, source_target_pairs={{0,1},{1,0},{2,3},{3,2},{4,5},{5,4},{6,7},{7,6},{8,9},{9,8},{10,11... | collective-permute-start | bytes 3145736 | tf_op jit(solution)/shard_map/ppermute | solution.py:206
  222.8 11.2 %copy-start.3 = (f32[32,64,256]{2,1,0:T(8,128)S(1)}, f32[32,64,256]{2,1,0:T(8,128)}, u32[]{:S(2)}) copy-start(f32[32,64,256]{2,1,0:T(8,128)} %constant_dynamic-update-slice_fusion.pot) | copy-start | bytes 6291460
  222.8 11.2 %copy-start.7 = (f32[3,32,8,256]{3,2,1,0:T(8,128)S(1)}, f32[3,32,8,256]{3,2,1,0:T(8,128)}, u32[]{:S(2)}) copy-start(f32[3,32,8,256]{3,2,1,0:T(8,128)} %copy-done.6) | copy-start | bytes 2359300
  222.8 11.2 %collective-permute-start.14 = (f32[2,32,8,256]{3,2,1,0:T(8,128)S(1)}, f32[2,32,8,256]{3,2,1,0:T(8,128)S(1)}, u32[]{:S(2)}, u32[]{:S(2)}) collective-permute-start(f32[2,32,8,256]{3,2,1,0:T(8,128)S(1)} %slice.41), channel_id=1, source_target_pairs={{1,16},{3,18},{5,20},{7,22},{9,24},{11,26},{13,28},{15,30},{16,1},... | collective-permute-start | bytes 1572872 | tf_op jit(solution)/shard_map/ppermute | solution.py:217
  248.4 3.6 %collective-permute-start.16 = (f32[8,16,8,256]{3,2,1,0:T(8,128)S(1)}, f32[8,16,8,256]{3,2,1,0:T(8,128)S(1)}, u32[]{:S(2)}, u32[]{:S(2)}) collective-permute-start(f32[8,16,8,256]{3,2,1,0:T(8,128)S(1)} %slice.51), channel_id=1, source_target_pairs={{0,1},{1,0},{2,3},{3,2},{4,5},{5,4},{6,7},{7,6},{8,9},{9,8},{10,11... | collective-permute-start | bytes 3145736 | tf_op jit(solution)/shard_map/ppermute | solution.py:206

commit v3 on v2

v3 whole, which is shorter than its diff:
```python
import functools

import jax
import jax.numpy as jnp
from jax import lax
from jax.experimental import pallas as pl
from jax.experimental.pallas import tpu as pltpu
from jax.sharding import PartitionSpec as P

SHIFT = 4.0
SPREAD = 7.0
CHIPS = 8
OCT = 8
BOUNDS = ((0, 3), (3, 5), (5, 8))
F32 = jnp.float32
BF16 = jnp.bfloat16


def split(x):
    high = x.astype(BF16)
    return high, (x - high.astype(F32)).astype(BF16)


def mm(a, b):
    return jnp.dot(a, b, preferred_element_type=F32)


def params(mib=24):
    return pltpu.CompilerParams(vmem_limit_bytes=mib * 1024 * 1024)


def extent(ids, ext, r):
    return ext[ids[1], ids[0] * 32 + ((r // 16) ^ ids[1]) * 16 + r % 16]


def prep(ids, radial, bond, angle, extents):
    def kernel(ids, radial, bond, angle, extents, rad, bond_cat, ang, ext_col, tmp, tmp_col):
        def rows(ref):
            return jnp.concatenate(
                [ref[pl.ds(pl.multiple_of((i ^ ids[1]) * 16, 16), 16), :] for i in range(16)], 0
            )

        tmp[...] = rows(radial).T
        rad[0], rad[1] = split(rows(tmp) / SPREAD)
        high, low = split(bond[...] / SPREAD)
        bond_cat[...] = jnp.concatenate([high, high, low], 1)
        ang[0], ang[1] = split(angle[...].T / SPREAD)
        line = jnp.where(ids[1] == 0, extents[0:1], extents[1:2]).astype(F32)
        tmp_col[...] = jnp.broadcast_to(line, (128, 256)).T
        ext_col[...] = rows(tmp_col)

    big = jax.ShapeDtypeStruct((2, 256, 256), BF16)
    vm = pl.BlockSpec(memory_space=pltpu.VMEM)
    return pl.pallas_call(
        kernel,
        out_shape=(big, jax.ShapeDtypeStruct((64, 192), BF16), big, jax.ShapeDtypeStruct((256, 128), F32)),
        in_specs=[pl.BlockSpec(memory_space=pltpu.SMEM), vm, vm, vm, vm],
        out_specs=(vm,) * 4,
        scratch_shapes=[pltpu.VMEM((256, 256), F32), pltpu.VMEM((256, 128), F32)],
        compiler_params=params(),
        name="prep",
    )(ids, radial, bond, angle, extents)


def start(ids, ext, own, other):
    step = 8
    half = 16 // step

    def kernel(ids, ext, own, other, whole):
        i = pl.program_id(0)
        line = lax.broadcasted_iota(jnp.int32, (64, 256), 0)
        for r in range(step):
            x = jnp.where(i < half, own[0, r], other[r])
            whole[:, r] = jnp.where(line < extent(ids, ext, i * step + r), x, 0.0).reshape(CHIPS, OCT, 256)

    return pl.pallas_call(
        kernel,
        grid_spec=pltpu.PrefetchScalarGridSpec(
            num_scalar_prefetch=2,
            grid=(32 // step,),
            in_specs=[
                pl.BlockSpec((1, step, 64, 256), lambda i, ids, ext: (ids[1], jnp.minimum(i, half - 1), 0, 0)),
                pl.BlockSpec((step, 64, 256), lambda i, ids, ext: (jnp.maximum(i - half, 0), 0, 0)),
            ],
            out_specs=pl.BlockSpec((CHIPS, step, OCT, 256), lambda i, ids, ext: (0, i, 0, 0)),
        ),
        out_shape=pltpu.HBM((CHIPS, 32, OCT, 256), F32),
        compiler_params=params(),
        name="start",
    )(ids, ext, own, other)


def local_terms(ids, ext, coef, cur, near, far, far_mid, far_top, pot, bond_cat, ang, prev, sent):
    step = 4

    def kernel(ids, ext, coef, cur, near, far, far_mid, far_top, pot, bond_cat, ang, *rest):
        prev, out = (rest[0], rest[1]) if len(rest) > 1 else (None, rest[0])
        first = pl.program_id(0) * step
        line = lax.broadcasted_iota(jnp.int32, (64, 256), 0)
        xs = [cur[:, r].reshape(64, 256) for r in range(step)]
        high, low = split(jnp.concatenate(xs, 0))
        angle = mm(high, ang[0]) + mm(low, ang[0]) + mm(high, ang[1])
        for r in range(step):
            part = slice(r * 64, r * 64 + 64)
            stack = jnp.concatenate([high[part], low[part], high[part]], 0)
            total = angle[part] + mm(bond_cat[...], stack)
            total = total + (pot[r] - SHIFT) * (1.0 / SPREAD) * xs[r]
            weight = coef[2 + first + r] * (1.0 / SPREAD)
            total = total - (weight * coef[0]) * near[:, r].reshape(64, 256)
            total = total - (weight * coef[1]) * jnp.concatenate(
                [f[:, r].reshape(-1, 256) for f in (far, far_mid, far_top)], 0
            )
            total = jnp.where(line < extent(ids, ext, first + r), total, 0.0)
            if prev is not None:
                total = 2.0 * total - prev[:, r].reshape(64, 256)
            out[:, r] = total.reshape(CHIPS, OCT, 256)

    whole = pl.BlockSpec((CHIPS, step, OCT, 256), lambda i: (0, i, 0, 0))
    def crossed(count):
        return pl.BlockSpec((count, step, OCT, 256), lambda i: (0, (i + 16 // step) % (32 // step), 0, 0))

    smem = pl.BlockSpec(memory_space=pltpu.SMEM)
    args = [ids, ext, coef, cur, near, far, far_mid, far_top, pot, bond_cat, ang]
    specs = [smem, smem, smem, whole, crossed(CHIPS), *[crossed(hi - lo) for lo, hi in BOUNDS], pl.BlockSpec((step, 64, 256), lambda i: (i, 0, 0))]
    specs += [
        pl.BlockSpec((64, 192), lambda i: (0, 0)),
        pl.BlockSpec((2, 256, 256), lambda i: (0, 0, 0)),
    ]
    if prev is not None:
        args.append(prev)
        specs.append(whole)
    return pl.pallas_call(
        kernel,
        grid=(32 // step,),
        in_specs=specs,
        out_specs=whole,
        out_shape=(pltpu.HBM if sent else jax.ShapeDtypeStruct)((CHIPS, 32, OCT, 256), F32),
        compiler_params=params(),
        cost_estimate=pl.CostEstimate(flops=2_000_000_000, bytes_accessed=14_000_000, transcendentals=0),
        name="local_terms",
    )(*args)


def radial_term(ids, ext_col, rad, packet, scale, more=None):
    rows = CHIPS * 32 * OCT
    flat = [p.reshape(rows, 256) for p in ((packet,) if more is None else (packet, more))]
    count = len(flat)

    def kernel(ids, ext_col, rad, *refs):
        ins, out = refs[:count], refs[count]

        def column(q):
            at = pl.ds(q, 256, stride=OCT)
            return ins[0][at, :] + ins[1][at, :] if count > 1 else ins[0][at, :]

        for q in range(0, OCT, 2):
            high, low = split(jnp.concatenate([column(q), column(q + 1)], 1))
            total = mm(rad[0], high) + mm(rad[0], low) + mm(rad[1], high)
            for i in range(2):
                half = total[:, i * 128 : i * 128 + 128]
                half = jnp.where(ext_col[...] > (ids[0] * OCT + q + i).astype(F32), half * scale, 0.0)
                out[pl.ds(q + i, 256, stride=OCT), :] = half

    lanes = pl.BlockSpec((rows, 128), lambda i: (0, i))
    full = pl.BlockSpec((2, 256, 256), lambda i: (0, 0, 0))
    out = pl.pallas_call(
        kernel,
        grid=(2,),
        in_specs=[
            pl.BlockSpec(memory_space=pltpu.SMEM), pl.BlockSpec((256, 128), lambda i: (0, 0)), full
        ] + [lanes] * count,
        out_specs=lanes,
        out_shape=pltpu.HBM((rows, 256), F32),
        compiler_params=params(56),
        cost_estimate=pl.CostEstimate(flops=2_000_000_000, bytes_accessed=5_000_000, transcendentals=0),
        name="radial_term",
    )(ids, ext_col, rad, *flat)
    return out.reshape(CHIPS, 32, OCT, 256)


def finish(ids, own, other, more=None):
    step = 2
    ins = (own, other) if more is None else (own, other, more)

    def kernel(ids, own, other, *rest):
        out = rest[-1]
        for o in range(step):
            at = slice(o * OCT, o * OCT + OCT)
            out[ids[1], :, at, :] = own[o] + rest[0][o] if len(rest) > 1 else own[o]
            out[1 - ids[1], :, at, :] = other[o]

    return pl.pallas_call(
        kernel,
        grid_spec=pltpu.PrefetchScalarGridSpec(
            num_scalar_prefetch=1,
            grid=(CHIPS // step,),
            in_specs=[pl.BlockSpec((step, 16, OCT, 256), lambda j, ids: (j, 0, 0, 0))] * len(ins),
            out_specs=pl.BlockSpec((2, 16, step * OCT, 256), lambda j, ids: (0, 0, j, 0)),
        ),
        out_shape=jax.ShapeDtypeStruct((2, 16, 64, 256), F32),
        compiler_params=params(),
        name="finish",
    )(ids, *ins)


def shards(initial_packet, extents, potential, coriolis_weight, radial_kinetic, bond_kinetic, angle_kinetic):
    ka, ga = lax.axis_index("ka"), lax.axis_index("ga")
    chip, core = ga // 2, ga % 2
    ids = jnp.stack([chip, core]).astype(jnp.int32)
    groups = lax.axis_size("ka")
    members = lax.axis_size("ga")
    top = jnp.float32((2 * groups - 1) * (2 * groups))

    def swap_core(x):
        return lax.ppermute(x, "ga", [(g, g ^ 1) for g in range(members)])

    def swap_far(x, count):
        pairs = [
            (i * members + g, k * members + (g ^ 1))
            for i in range(count)
            for g in range(members)
            for k in (i + 1 if g % 2 else i - 1,)
            if 0 <= k < count
        ]
        return lax.ppermute(x, ("ka", "ga"), pairs)

    def halo(t, turned):
        low, mid, top = [t[lo:hi] for lo, hi in BOUNDS]
        low, top = swap_far(low, groups), swap_far(top, groups // 2)
        turned, low, top = lax.optimization_barrier((turned, low, top))
        t, mid, turned = lax.optimization_barrier((t, mid, turned))
        return turned, (swap_core(t), low, swap_far(mid, groups), top)

    same_core = [list(range(c, members, 2)) for c in range(2)]

    def turn(x):
        return lax.all_to_all(x, "ga", 0, 0, axis_index_groups=same_core, tiled=True)

    other = swap_core(lax.dynamic_index_in_dim(initial_packet, 1 - core, 0, keepdims=False))
    pot = jnp.concatenate([potential, swap_core(potential)], 0)
    weight = jnp.concatenate([coriolis_weight, swap_core(coriolis_weight)])
    kvalue = (2 * ka + core).astype(F32)
    upper = jnp.sqrt(top - kvalue * (kvalue + 1.0))
    lower = jnp.where(kvalue > 0.0, jnp.sqrt(top - kvalue * (kvalue - 1.0)), 0.0)
    coef = jnp.concatenate(
        [jnp.stack([jnp.where(core == 0, upper, lower), jnp.where(core == 0, lower, upper)]), weight]
    )
    rad, bond_cat, ang, ext_col = prep(ids, radial_kinetic, bond_kinetic, angle_kinetic, extents)
    other, rad, bond_cat, ang, ext_col = lax.optimization_barrier((other, rad, bond_cat, ang, ext_col))

    def local(cur, halos, prev=None, sent=True):
        return local_terms(ids, extents, coef, cur, *halos, pot, bond_cat, ang, prev, sent)

    def radial(packet, scale, more=None):
        return radial_term(ids, ext_col, rad, packet, scale, more)

    t0 = start(ids, extents, initial_packet, other)
    turned, h0 = halo(t0, turn(t0))
    b0 = radial(turned, 1.0)
    a0 = local(t0, h0)
    t1 = a0 + turn(b0)
    turned, h1 = halo(t1, turn(a0))
    b1 = radial(turned, 2.0, b0)
    c1 = local(t1, h1, t0)
    t2 = c1 + turn(b1)
    turned, h2 = halo(t2, turn(c1))
    b2 = radial(turned, 2.0, b1)
    c2 = local(t2, h2, t1, sent=False)
    former = finish(ids, t2, swap_core(t2[:, 16:]))
    c2, former = lax.optimization_barrier((c2, former))
    b2 = turn(b2)
    newest = finish(ids, c2, swap_core(c2[:, 16:] + b2[:, 16:]), b2)
    return newest, former


def solution(mesh):
    return jax.shard_map(
        shards,
        mesh=mesh,
        in_specs=(
            P("ka", "ga", None, None),
            P("ka", None),
            P("ga", None, None),
            P("ga"),
            P(),
            P(),
            P(),
        ),
        out_specs=(P("ka", "ga", None, None), P("ka", "ga", None, None)),
        check_vma=False,
    )
```

time: 257 us -> 246 us (0.957)
  waiting for transfers between devices: 106 us -> 113 us
  local copies, waits for them, and re-layouts: 30.1 us -> 23.8 us
  other arithmetic: 11.3 us -> 7.1 us
  Pallas kernels: 46.1 us -> 42.2 us
  starting transfers between devices: 61.3 us -> 57.7 us
    ppermute x9, waiting for transfers between devices: 45.2 us -> 67 us  [swap_far(): return lax.ppermute(x, ('ka', 'ga'), pairs)]
    all_to_all x6, waiting for transfers between devices: 57.1 us -> 43.3 us  [turn(): lax.all_to_all(x, 'ga', 0, 0, axis_index_groups=same_core, tiled=True)]
    slice x8 -> x7, local copies, waits for them, and re-layouts: 9.79 us -> 3.17 us  [the longest x6 3.07 us: halo(): low, mid, top = [t[lo:hi] for lo, hi in BOUNDS]]
    unnamed x41 -> x57, local copies, waits for them, and re-layouts: 12.6 us -> 15.8 us
    ppermute x8, starting transfers between devices: 10.6 us -> 7.44 us  [swap_core(): return lax.ppermute(x, 'ga', [(g, g ^ 1) for g in range(members)])]
    pallas_call x2, Pallas kernels: 9.48 us -> 6.65 us  [finish(): pl.pallas_call(kernel, grid_spec=pltpu.PrefetchScalarGridSpec(num_scalar_...]
  transfers between devices with their start and end apart: 23 -> 23, of which waited for: 15 -> 16; matrix products, arithmetic and copies ran while one was open for 7% -> 5% of each run, Pallas kernels for 11% -> 15%
where the time goes in v3:
time: 246 us; the launch traced here: 245 us
  waiting for transfers between devices  113 us (46%)
  starting transfers between devices  57.7 us (23%)
  Pallas kernels  42.2 us (17%)
  local copies, waits for them, and re-layouts  23.8 us (10%)
  other arithmetic  7.1 us (3%)
    ppermute x9, waiting for transfers between devices, swap_far(): return lax.ppermute(x, ('ka', 'ga'), pairs)  67 us
    all_to_all x6, waiting for transfers between devices, turn(): lax.all_to_all(x, 'ga', 0, 0, axis_index_groups=same_core, tiled=True)  43.3 us
    all_to_all x6, starting transfers between devices, turn(): lax.all_to_all(x, 'ga', 0, 0, axis_index_groups=same_core, tiled=True)  27.6 us
    ppermute x9, starting transfers between devices, swap_far(): return lax.ppermute(x, ('ka', 'ga'), pairs)  22.6 us
    pallas_call x3, Pallas kernels, local_terms(): pl.pallas_call(kernel, grid=(32 // step,), in_specs=specs, out_specs=whol...  19.8 us
    unnamed x57, local copies, waits for them, and re-layouts  15.8 us
    pallas_call x3, Pallas kernels, radial_term(): pl.pallas_call(kernel, grid=(2,), in_specs=[pl.BlockSpec(memory_space=plt...  12.4 us
    ppermute x8, starting transfers between devices, swap_core(): return lax.ppermute(x, 'ga', [(g, g ^ 1) for g in range(members)])  7.44 us
  transfers between devices with their start and end apart: 23, of which 16 were waited for; matrix products, arithmetic and copies ran while one was open for 5% of the time, Pallas kernels for 15%

profile of v3, /device:TPU:1, one launch (start us, length us, event | category | flops | bytes accessed | tf_op | source)
XLA Modules:
  0.0 244.6 jit_solution(15611857590441411257)
XLA Ops:
  0.7 2.4 dynamic-slice_bitcast_fusion
  3.1 3.2 %collective-permute-start.1 = (f32[16,64,256]{2,1,0:T(8,128)}, f32[16,64,256]{2,1,0:T(8,128)S(1)}, u32[]{:S(2)}, u32[]{:S(2)}) collective-permute-start(f32[16,64,256]{2,1,0:T(8,128)} %dynamic-slice_bitcast_fusion), channel_id=1, source_target_pairs={{0,1},{1,0},{2,3},{3,2},{4,5},{5,4},{6,7},{7,6},{8,9},{9,8},{10,11... | collective-permute-start | bytes 3145736 | tf_op jit(solution)/shard_map/ppermute | solution.py:215
  10.6 2.5 %start.1.cur.rest_0_ = f32[8,32,8,256]{3,2,1,0:T(8,128)} custom-call(s32[2]{0:T(128)S(1)} %pad_add_fusion.ids, s32[2,256]{1,0:T(2,128)S(1)} %copy-done.18, f32[2,16,64,256]{3,2,1,0:T(8,128)S(1)} %copy-done.9, f32[16,64,256]{2,1,0:T(8,128)S(1)} %collective-permute-done.1.other), custom_call_target="tpu_custom_call" | custom-call | tf_op jit(solution)/shard_map/start/pallas_call | solution.py:76
  13.1 5.0 %all-to-all-start = ((f32[8,32,8,256]{3,2,1,0:T(8,128)}), f32[8,32,8,256]{3,2,1,0:T(8,128)}, u32[]{:S(2)}, u32[]{:S(2)}) async-start(f32[8,32,8,256]{3,2,1,0:T(8,128)} %start.1.cur.rest_0_), calls=%async_computation | async-start | bytes 4194304 | tf_op jit(solution)/shard_map/all_to_all | solution.py:237
  18.4 3.7 %collective-permute-start.2 = (f32[3,32,8,256]{3,2,1,0:T(8,128)S(1)}, f32[3,32,8,256]{3,2,1,0:T(8,128)S(1)}, u32[]{:S(2)}, u32[]{:S(2)}) collective-permute-start(f32[3,32,8,256]{3,2,1,0:T(8,128)S(1)} %get-tuple-element.65), channel_id=1, source_target_pairs={{1,16},{3,18},{5,20},{7,22},{9,24},{11,26},{13,28},{15,30},{16,1},... | collective-permute-start | bytes 2359304 | tf_op jit(solution)/shard_map/ppermute | solution.py:225
  22.1 1.9 collective-permute-start.3
  24.9 7.3 %collective-permute-done.2.far = f32[3,32,8,256]{3,2,1,0:T(8,128)S(1)} collective-permute-done((f32[3,32,8,256]{3,2,1,0:T(8,128)S(1)}, f32[3,32,8,256]{3,2,1,0:T(8,128)S(1)}, u32[]{:S(2)}, u32[]{:S(2)}) %collective-permute-start.2) | collective-permute-done | bytes 786464 | tf_op jit(solution)/shard_map/ppermute | solution.py:225
  32.1 8.4 %collective-permute-done.3.far_top = f32[3,32,8,256]{3,2,1,0:T(8,128)S(1)} collective-permute-done((f32[3,32,8,256]{3,2,1,0:T(8,128)S(1)}, f32[3,32,8,256]{3,2,1,0:T(8,128)S(1)}, u32[]{:S(2)}, u32[]{:S(2)}) %collective-permute-start.3) | collective-permute-done | bytes 786464 | tf_op jit(solution)/shard_map/ppermute | solution.py:225
  41.5 11.4 %all-to-all-done = f32[8,32,8,256]{3,2,1,0:T(8,128)} async-done(((f32[8,32,8,256]{3,2,1,0:T(8,128)}), f32[8,32,8,256]{3,2,1,0:T(8,128)}, u32[]{:S(2)}, u32[]{:S(2)}) %all-to-all-start) | async-done | bytes 2097184 | tf_op jit(solution)/shard_map/all_to_all | solution.py:237
  54.0 3.7 %radial_term.3.refs_1_ = f32[2048,256]{1,0:T(8,128)} custom-call(s32[2]{0:T(128)} %copy-done.20, f32[256,128]{1,0:T(8,128)} %copy-done.25, bf16[2,256,256]{2,1,0:T(8,128)(2,1)} %copy-done.24, f32[2048,256]{1,0:T(8,128)} %bitcast.5.refs_0_), custom_call_target="tpu_custom_call" | custom-call | flops 2000000000 | bytes 5000000 | tf_op jit(solution)/shard_map/radial_term/pallas_call | solution.py:166
  57.7 4.5 %all-to-all-start.1 = ((f32[8,32,8,256]{3,2,1,0:T(8,128)}), f32[8,32,8,256]{3,2,1,0:T(8,128)}, u32[]{:S(2)}, u32[]{:S(2)}) async-start(f32[8,32,8,256]{3,2,1,0:T(8,128)} %bitcast.12), calls=%async_computation.1 | async-start | bytes 4194304 | tf_op jit(solution)/shard_map/all_to_all | solution.py:237
  62.3 1.9 collective-permute-start.5
  64.5 2.3 constant_dynamic-update-slice_fusion.1
  66.9 2.4 constant_dynamic-update-slice_fusion.pot
  69.2 4.2 %collective-permute-done.5.far_mid = f32[2,32,8,256]{3,2,1,0:T(8,128)} collective-permute-done((f32[2,32,8,256]{3,2,1,0:T(8,128)}, f32[2,32,8,256]{3,2,1,0:T(8,128)}, u32[]{:S(2)}, u32[]{:S(2)}) %collective-permute-start.5) | collective-permute-done | bytes 524320 | tf_op jit(solution)/shard_map/ppermute | solution.py:225
  75.0 6.9 %local_terms.3 = f32[8,32,8,256]{3,2,1,0:T(8,128)} custom-call(s32[2]{0:T(128)S(1)} %copy-done.21, s32[2,256]{1,0:T(2,128)S(1)} %copy-done.18, f32[34]{0:T(128)S(1)} %pad_maximum_fusion.coef, f32[8,32,8,256]{3,2,1,0:T(8,128)S(1)} %copy-done, f32[8,32,8,256]{3,2,1,0:T(8,128)} %collective-permute-done.4.near, ...), custom_call_target="tpu_custom_call" | custom-call | flops 2000000000 | bytes 14000000 | tf_op jit(solution)/shard_map/local_terms/pallas_call | solution.py:132
  81.9 13.3 %all-to-all-done.1 = f32[8,32,8,256]{3,2,1,0:T(8,128)} async-done(((f32[8,32,8,256]{3,2,1,0:T(8,128)}), f32[8,32,8,256]{3,2,1,0:T(8,128)}, u32[]{:S(2)}, u32[]{:S(2)}) %all-to-all-start.1) | async-done | bytes 2097184 | tf_op jit(solution)/shard_map/all_to_all | solution.py:237
  95.2 4.4 %all-to-all-start.2 = ((f32[8,32,8,256]{3,2,1,0:T(8,128)}), f32[8,32,8,256]{3,2,1,0:T(8,128)}, u32[]{:S(2)}, u32[]{:S(2)}) async-start(f32[8,32,8,256]{3,2,1,0:T(8,128)} %local_terms.3), calls=%async_computation.2 | async-start | bytes 4194304 | tf_op jit(solution)/shard_map/all_to_all | solution.py:237
  99.6 2.6 %add.30.cur.rest_0_ = f32[8,32,8,256]{3,2,1,0:T(8,128)S(1)} add(f32[8,32,8,256]{3,2,1,0:T(8,128)} %local_terms.3, f32[8,32,8,256]{3,2,1,0:T(8,128)} %all-to-all-done.1) | non-fusion elementwise | flops 524288 | bytes 6291456 | tf_op jit(solution)/shard_map/add | solution.py:261
  102.4 1.9 collective-permute-start.7
  104.3 3.6 %collective-permute-start.8 = (f32[3,32,8,256]{3,2,1,0:T(8,128)S(1)}, f32[3,32,8,256]{3,2,1,0:T(8,128)S(1)}, u32[]{:S(2)}, u32[]{:S(2)}) collective-permute-start(f32[3,32,8,256]{3,2,1,0:T(8,128)S(1)} %get-tuple-element.62), channel_id=1, source_target_pairs={{1,16},{3,18},{5,20},{7,22},{9,24},{11,26},{13,28},{15,30},{16,1},... | collective-permute-start | bytes 2359304 | tf_op jit(solution)/shard_map/ppermute | solution.py:225
  108.8 6.9 %collective-permute-done.7.far = f32[3,32,8,256]{3,2,1,0:T(8,128)S(1)} collective-permute-done((f32[3,32,8,256]{3,2,1,0:T(8,128)S(1)}, f32[3,32,8,256]{3,2,1,0:T(8,128)S(1)}, u32[]{:S(2)}, u32[]{:S(2)}) %collective-permute-start.7) | collective-permute-done | bytes 786464 | tf_op jit(solution)/shard_map/ppermute | solution.py:225
  115.7 8.8 %collective-permute-done.8.far_top = f32[3,32,8,256]{3,2,1,0:T(8,128)S(1)} collective-permute-done((f32[3,32,8,256]{3,2,1,0:T(8,128)S(1)}, f32[3,32,8,256]{3,2,1,0:T(8,128)S(1)}, u32[]{:S(2)}, u32[]{:S(2)}) %collective-permute-start.8) | collective-permute-done | bytes 786464 | tf_op jit(solution)/shard_map/ppermute | solution.py:225
  125.4 5.6 %all-to-all-done.2 = f32[8,32,8,256]{3,2,1,0:T(8,128)} async-done(((f32[8,32,8,256]{3,2,1,0:T(8,128)}), f32[8,32,8,256]{3,2,1,0:T(8,128)}, u32[]{:S(2)}, u32[]{:S(2)}) %all-to-all-start.2) | async-done | bytes 2097184 | tf_op jit(solution)/shard_map/all_to_all | solution.py:237
  131.5 4.3 %radial_term.4.refs_1_ = f32[2048,256]{1,0:T(8,128)} custom-call(s32[2]{0:T(128)} %copy-done.20, f32[256,128]{1,0:T(8,128)} %copy-done.25, bf16[2,256,256]{2,1,0:T(8,128)(2,1)} %copy-done.24, f32[2048,256]{1,0:T(8,128)} %bitcast.7.refs_0_, f32[2048,256]{1,0:T(8,128)} %radial_term.3.refs_1_), custom_call_target="tpu_custom_call" | custom-call | flops 2000000000 | bytes 5000000 | tf_op jit(solution)/shard_map/radial_term/pallas_call | solution.py:166
  135.9 4.5 %all-to-all-start.3 = ((f32[8,32,8,256]{3,2,1,0:T(8,128)}), f32[8,32,8,256]{3,2,1,0:T(8,128)}, u32[]{:S(2)}, u32[]{:S(2)}) async-start(f32[8,32,8,256]{3,2,1,0:T(8,128)} %bitcast.13), calls=%async_computation.3 | async-start | bytes 4194304 | tf_op jit(solution)/shard_map/all_to_all | solution.py:237
  140.4 1.9 collective-permute-start.10
  142.3 9.2 %collective-permute-done.10.far_mid = f32[2,32,8,256]{3,2,1,0:T(8,128)S(1)} collective-permute-done((f32[2,32,8,256]{3,2,1,0:T(8,128)}, f32[2,32,8,256]{3,2,1,0:T(8,128)S(1)}, u32[]{:S(2)}, u32[]{:S(2)}) %collective-permute-start.10) | collective-permute-done | bytes 524320 | tf_op jit(solution)/shard_map/ppermute | solution.py:225
  153.1 1.6 copy-done.5
  155.8 6.9 %local_terms.4 = f32[8,32,8,256]{3,2,1,0:T(8,128)} custom-call(s32[2]{0:T(128)S(1)} %copy-done.22, s32[2,256]{1,0:T(2,128)S(1)} %copy-done.18, f32[34]{0:T(128)S(1)} %pad_maximum_fusion.coef, f32[8,32,8,256]{3,2,1,0:T(8,128)S(1)} %copy-done.2, f32[8,32,8,256]{3,2,1,0:T(8,128)} %collective-permute-done.9.near, ...), custom_call_target="tpu_custom_call" | custom-call | flops 2000000000 | bytes 14000000 | tf_op jit(solution)/shard_map/local_terms/pallas_call | solution.py:132
  162.7 4.2 %all-to-all-done.3 = f32[8,32,8,256]{3,2,1,0:T(8,128)} async-done(((f32[8,32,8,256]{3,2,1,0:T(8,128)}), f32[8,32,8,256]{3,2,1,0:T(8,128)}, u32[]{:S(2)}, u32[]{:S(2)}) %all-to-all-start.3) | async-done | bytes 2097184 | tf_op jit(solution)/shard_map/all_to_all | solution.py:237
  166.9 4.9 %all-to-all-start.4 = ((f32[8,32,8,256]{3,2,1,0:T(8,128)}), f32[8,32,8,256]{3,2,1,0:T(8,128)}, u32[]{:S(2)}, u32[]{:S(2)}) async-start(f32[8,32,8,256]{3,2,1,0:T(8,128)} %local_terms.4), calls=%async_computation.4 | async-start | bytes 4194304 | tf_op jit(solution)/shard_map/all_to_all | solution.py:237
  171.8 2.6 %add.31.cur.own = f32[8,32,8,256]{3,2,1,0:T(8,128)S(1)} add(f32[8,32,8,256]{3,2,1,0:T(8,128)} %local_terms.4, f32[8,32,8,256]{3,2,1,0:T(8,128)} %all-to-all-done.3) | non-fusion elementwise | flops 524288 | bytes 6291456 | tf_op jit(solution)/shard_map/add | solution.py:265
  174.5 1.9 collective-permute-start.11
  176.5 3.6 %collective-permute-start.12 = (f32[3,32,8,256]{3,2,1,0:T(8,128)S(1)}, f32[3,32,8,256]{3,2,1,0:T(8,128)S(1)}, u32[]{:S(2)}, u32[]{:S(2)}) collective-permute-start(f32[3,32,8,256]{3,2,1,0:T(8,128)S(1)} %get-tuple-element.60), channel_id=1, source_target_pairs={{1,16},{3,18},{5,20},{7,22},{9,24},{11,26},{13,28},{15,30},{16,1},... | collective-permute-start | bytes 2359304 | tf_op jit(solution)/shard_map/ppermute | solution.py:225
  181.0 7.3 %collective-permute-done.11.far = f32[3,32,8,256]{3,2,1,0:T(8,128)S(1)} collective-permute-done((f32[3,32,8,256]{3,2,1,0:T(8,128)S(1)}, f32[3,32,8,256]{3,2,1,0:T(8,128)S(1)}, u32[]{:S(2)}, u32[]{:S(2)}) %collective-permute-start.11) | collective-permute-done | bytes 786464 | tf_op jit(solution)/shard_map/ppermute | solution.py:225
  188.2 8.4 %collective-permute-done.12.far_top = f32[3,32,8,256]{3,2,1,0:T(8,128)S(1)} collective-permute-done((f32[3,32,8,256]{3,2,1,0:T(8,128)S(1)}, f32[3,32,8,256]{3,2,1,0:T(8,128)S(1)}, u32[]{:S(2)}, u32[]{:S(2)}) %collective-permute-start.12) | collective-permute-done | bytes 786464 | tf_op jit(solution)/shard_map/ppermute | solution.py:225
  197.6 1.8 all-to-all-done.4
  200.1 4.4 %radial_term.5 = f32[2048,256]{1,0:T(8,128)} custom-call(s32[2]{0:T(128)} %copy-done.20, f32[256,128]{1,0:T(8,128)} %copy-done.25, bf16[2,256,256]{2,1,0:T(8,128)(2,1)} %copy-done.24, f32[2048,256]{1,0:T(8,128)} %bitcast.9.refs_0_, f32[2048,256]{1,0:T(8,128)} %radial_term.4.refs_1_), custom_call_target="tpu_custom_call" | custom-call | flops 2000000000 | bytes 5000000 | tf_op jit(solution)/shard_map/radial_term/pallas_call | solution.py:166
  204.5 4.3 %all-to-all-start.5 = ((f32[8,32,8,256]{3,2,1,0:T(8,128)}), f32[8,32,8,256]{3,2,1,0:T(8,128)}, u32[]{:S(2)}, u32[]{:S(2)}) async-start(f32[8,32,8,256]{3,2,1,0:T(8,128)} %bitcast.14), calls=%async_computation.5 | async-start | bytes 4194304 | tf_op jit(solution)/shard_map/all_to_all | solution.py:237
  209.9 2.0 collective-permute-start.14
  212.0 2.5 %finish.2 = f32[2,16,64,256]{3,2,1,0:T(8,128)} custom-call(s32[2]{0:T(128)S(1)} %copy-done.23, f32[8,32,8,256]{3,2,1,0:T(8,128)S(1)} %add.31.cur.own, f32[8,16,8,256]{3,2,1,0:T(8,128)S(1)} %collective-permute-done.15.other), custom_call_target="tpu_custom_call" | custom-call | tf_op jit(solution)/shard_map/finish/pallas_call | solution.py:192
  214.4 6.5 %collective-permute-done.14.far_mid = f32[2,32,8,256]{3,2,1,0:T(8,128)S(1)} collective-permute-done((f32[2,32,8,256]{3,2,1,0:T(8,128)S(1)}, f32[2,32,8,256]{3,2,1,0:T(8,128)S(1)}, u32[]{:S(2)}, u32[]{:S(2)}) %collective-permute-start.14) | collective-permute-done | bytes 524320 | tf_op jit(solution)/shard_map/ppermute | solution.py:225
  220.9 6.0 %local_terms.5.own = f32[8,32,8,256]{3,2,1,0:T(8,128)S(1)} custom-call(s32[2]{0:T(128)S(1)} %copy-done.23, s32[2,256]{1,0:T(2,128)S(1)} %copy-done.18, f32[34]{0:T(128)S(1)} %pad_maximum_fusion.coef, f32[8,32,8,256]{3,2,1,0:T(8,128)S(1)} %add.31.cur.own, f32[8,32,8,256]{3,2,1,0:T(8,128)} %collective-permute-done.13.near, ...), custom_call_target="tpu_custom_call" | custom-call | flops 2000000000 | bytes 14000000 | tf_op jit(solution)/shard_map/local_terms/pallas_call | solution.py:132
  228.3 7.0 %all-to-all-done.5.rest_0_ = f32[8,32,8,256]{3,2,1,0:T(8,128)} async-done(((f32[8,32,8,256]{3,2,1,0:T(8,128)}), f32[8,32,8,256]{3,2,1,0:T(8,128)}, u32[]{:S(2)}, u32[]{:S(2)}) %all-to-all-start.5) | async-done | bytes 2097184 | tf_op jit(solution)/shard_map/all_to_all | solution.py:237
  235.3 1.8 slice_add_fusion
  238.1 2.3 collective-permute-done.16.other
  240.4 4.2 %finish.3 = f32[2,16,64,256]{3,2,1,0:T(8,128)} custom-call(s32[2]{0:T(128)S(1)} %copy-done.23, f32[8,32,8,256]{3,2,1,0:T(8,128)S(1)} %copy-done.8, f32[8,16,8,256]{3,2,1,0:T(8,128)S(1)} %collective-permute-done.16.other, f32[8,32,8,256]{3,2,1,0:T(8,128)} %all-to-all-done.5.rest_0_), custom_call_target="tpu_custom_call" | custom-call | tf_op jit(solution)/shard_map/finish/pallas_call | solution.py:192
  (79 shorter events, 20.3 us)
Async XLA Ops:
  0.6 9.9 %copy-start.9 = (f32[2,16,64,256]{3,2,1,0:T(8,128)S(1)}, f32[2,16,64,256]{3,2,1,0:T(8,128)}, u32[]{:S(2)}) copy-start(f32[2,16,64,256]{3,2,1,0:T(8,128)} %own.1) | copy-start | bytes 6291460
  0.6 5.8 %copy-start.19 = (f32[64,64]{1,0:T(8,128)S(1)}, f32[64,64]{1,0:T(8,128)}, u32[]{:S(2)}) copy-start(f32[64,64]{1,0:T(8,128)} %bond.1) | copy-start | bytes 49156
  0.6 5.8 %copy-start.18 = (s32[2,256]{1,0:T(2,128)S(1)}, s32[2,256]{1,0:T(2,128)}, u32[]{:S(2)}) copy-start(s32[2,256]{1,0:T(2,128)} %ext.7) | copy-start | bytes 6148
  3.1 7.4 %collective-permute-start.1 = (f32[16,64,256]{2,1,0:T(8,128)}, f32[16,64,256]{2,1,0:T(8,128)S(1)}, u32[]{:S(2)}, u32[]{:S(2)}) collective-permute-start(f32[16,64,256]{2,1,0:T(8,128)} %dynamic-slice_bitcast_fusion), channel_id=1, source_target_pairs={{0,1},{1,0},{2,3},{3,2},{4,5},{5,4},{6,7},{7,6},{8,9},{9,8},{10,11... | collective-permute-start | bytes 3145736 | tf_op jit(solution)/shard_map/ppermute | solution.py:215
  6.4 1.0 copy-start.16
  7.4 0.9 copy-start.17
  8.3 4.8 %copy-start.20 = (s32[2]{0:T(128)}, s32[2]{0:T(128)S(1)}, u32[]{:S(2)}) copy-start(s32[2]{0:T(128)S(1)} %pad_add_fusion.ids) | copy-start | bytes 28
  13.1 5.1 %copy-start = (f32[8,32,8,256]{3,2,1,0:T(8,128)S(1)}, f32[8,32,8,256]{3,2,1,0:T(8,128)}, u32[]{:S(2)}) copy-start(f32[8,32,8,256]{3,2,1,0:T(8,128)} %start.1.cur.rest_0_) | copy-start | bytes 6291460
  13.1 39.8 %all-to-all-start = ((f32[8,32,8,256]{3,2,1,0:T(8,128)}), f32[8,32,8,256]{3,2,1,0:T(8,128)}, u32[]{:S(2)}, u32[]{:S(2)}) async-start(f32[8,32,8,256]{3,2,1,0:T(8,128)} %start.1.cur.rest_0_), calls=%async_computation | async-start | bytes 4194304 | tf_op jit(solution)/shard_map/all_to_all | solution.py:237
  18.4 13.8 %collective-permute-start.2 = (f32[3,32,8,256]{3,2,1,0:T(8,128)S(1)}, f32[3,32,8,256]{3,2,1,0:T(8,128)S(1)}, u32[]{:S(2)}, u32[]{:S(2)}) collective-permute-start(f32[3,32,8,256]{3,2,1,0:T(8,128)S(1)} %get-tuple-element.65), channel_id=1, source_target_pairs={{1,16},{3,18},{5,20},{7,22},{9,24},{11,26},{13,28},{15,30},{16,1},... | collective-permute-start | bytes 2359304 | tf_op jit(solution)/shard_map/ppermute | solution.py:225
  22.1 18.5 %collective-permute-start.3 = (f32[3,32,8,256]{3,2,1,0:T(8,128)S(1)}, f32[3,32,8,256]{3,2,1,0:T(8,128)S(1)}, u32[]{:S(2)}, u32[]{:S(2)}) collective-permute-start(f32[3,32,8,256]{3,2,1,0:T(8,128)S(1)} %get-tuple-element.64), channel_id=1, source_target_pairs={{1,16},{3,18},{5,20},{7,22},{9,24},{11,26},{13,28},{15,30},{16,1},... | collective-permute-start | bytes 2359304 | tf_op jit(solution)/shard_map/ppermute | solution.py:225
  40.6 0.9 copy-start.10
  52.9 20.6 %collective-permute-start.4 = (f32[8,32,8,256]{3,2,1,0:T(8,128)S(1)}, f32[8,32,8,256]{3,2,1,0:T(8,128)}, u32[]{:S(2)}, u32[]{:S(2)}) collective-permute-start(f32[8,32,8,256]{3,2,1,0:T(8,128)S(1)} %copy-done), channel_id=1, source_target_pairs={{0,1},{1,0},{2,3},{3,2},{4,5},{5,4},{6,7},{7,6},{8,9},{9,8},{10,11... | collective-permute-start | bytes 6291464 | tf_op jit(solution)/shard_map/ppermute | solution.py:215
  57.7 6.5 %copy-start.27 = (f32[16]{0:T(128)S(1)}, f32[16]{0:T(128)}, u32[]{:S(2)}) copy-start(f32[16]{0:T(128)} %param.10) | copy-start | bytes 196
  57.7 37.5 %all-to-all-start.1 = ((f32[8,32,8,256]{3,2,1,0:T(8,128)}), f32[8,32,8,256]{3,2,1,0:T(8,128)}, u32[]{:S(2)}, u32[]{:S(2)}) async-start(f32[8,32,8,256]{3,2,1,0:T(8,128)} %bitcast.12), calls=%async_computation.1 | async-start | bytes 4194304 | tf_op jit(solution)/shard_map/all_to_all | solution.py:237
  62.2 4.6 %collective-permute-start.6 = (f32[16,64,256]{2,1,0:T(8,128)}, f32[16,64,256]{2,1,0:T(8,128)}, u32[]{:S(2)}, u32[]{:S(2)}) collective-permute-start(f32[16,64,256]{2,1,0:T(8,128)} %param.9), channel_id=1, source_target_pairs={{0,1},{1,0},{2,3},{3,2},{4,5},{5,4},{6,7},{7,6},{8,9},{9,8},{10,11... | collective-permute-start | bytes 3145736 | tf_op jit(solution)/shard_map/ppermute | solution.py:215
  62.3 11.1 %collective-permute-start.5 = (f32[2,32,8,256]{3,2,1,0:T(8,128)}, f32[2,32,8,256]{3,2,1,0:T(8,128)}, u32[]{:S(2)}, u32[]{:S(2)}) collective-permute-start(f32[2,32,8,256]{3,2,1,0:T(8,128)} %slice.48), channel_id=1, source_target_pairs={{1,16},{3,18},{5,20},{7,22},{9,24},{11,26},{13,28},{15,30},{16,1},... | collective-permute-start | bytes 1572872 | tf_op jit(solution)/shard_map/ppermute | solution.py:225
  64.3 2.5 %collective-permute-start = (f32[16]{0:T(128)S(1)}, f32[16]{0:T(128)S(1)}, u32[]{:S(2)}, u32[]{:S(2)}) collective-permute-start(f32[16]{0:T(128)S(1)} %copy-done.27), channel_id=1, source_target_pairs={{0,1},{1,0},{2,3},{3,2},{4,5},{5,4},{6,7},{7,6},{8,9},{9,8},{10,11... | collective-permute-start | bytes 200 | tf_op jit(solution)/shard_map/ppermute | solution.py:215
  64.5 9.0 %copy-start.21 = (s32[2]{0:T(128)S(1)}, s32[2]{0:T(128)}, u32[]{:S(2)}) copy-start(s32[2]{0:T(128)} %copy-done.20) | copy-start | bytes 28
  66.8 6.7 %copy-start.11 = (f32[3,32,8,256]{3,2,1,0:T(8,128)S(1)}, f32[3,32,8,256]{3,2,1,0:T(8,128)}, u32[]{:S(2)}) copy-start(f32[3,32,8,256]{3,2,1,0:T(8,128)} %copy-done.10) | copy-start | bytes 2359300
  73.5 1.6 copy-start.4
  95.2 35.7 %all-to-all-start.2 = ((f32[8,32,8,256]{3,2,1,0:T(8,128)}), f32[8,32,8,256]{3,2,1,0:T(8,128)}, u32[]{:S(2)}, u32[]{:S(2)}) async-start(f32[8,32,8,256]{3,2,1,0:T(8,128)} %local_terms.3), calls=%async_computation.2 | async-start | bytes 4194304 | tf_op jit(solution)/shard_map/all_to_all | solution.py:237
  102.2 6.6 %copy-start.1 = (f32[8,32,8,256]{3,2,1,0:T(8,128)}, f32[8,32,8,256]{3,2,1,0:T(8,128)S(1)}, u32[]{:S(2)}) copy-start(f32[8,32,8,256]{3,2,1,0:T(8,128)S(1)} %add.30.cur.rest_0_) | copy-start | bytes 6291460
  102.4 13.3 %collective-permute-start.7 = (f32[3,32,8,256]{3,2,1,0:T(8,128)S(1)}, f32[3,32,8,256]{3,2,1,0:T(8,128)S(1)}, u32[]{:S(2)}, u32[]{:S(2)}) collective-permute-start(f32[3,32,8,256]{3,2,1,0:T(8,128)S(1)} %get-tuple-element.63), channel_id=1, source_target_pairs={{1,16},{3,18},{5,20},{7,22},{9,24},{11,26},{13,28},{15,30},{16,1},... | collective-permute-start | bytes 2359304 | tf_op jit(solution)/shard_map/ppermute | solution.py:225
  104.3 20.2 %collective-permute-start.8 = (f32[3,32,8,256]{3,2,1,0:T(8,128)S(1)}, f32[3,32,8,256]{3,2,1,0:T(8,128)S(1)}, u32[]{:S(2)}, u32[]{:S(2)}) collective-permute-start(f32[3,32,8,256]{3,2,1,0:T(8,128)S(1)} %get-tuple-element.62), channel_id=1, source_target_pairs={{1,16},{3,18},{5,20},{7,22},{9,24},{11,26},{13,28},{15,30},{16,1},... | collective-permute-start | bytes 2359304 | tf_op jit(solution)/shard_map/ppermute | solution.py:225
  131.0 20.5 %collective-permute-start.9 = (f32[8,32,8,256]{3,2,1,0:T(8,128)}, f32[8,32,8,256]{3,2,1,0:T(8,128)}, u32[]{:S(2)}, u32[]{:S(2)}) collective-permute-start(f32[8,32,8,256]{3,2,1,0:T(8,128)} %copy-done.1), channel_id=1, source_target_pairs={{0,1},{1,0},{2,3},{3,2},{4,5},{5,4},{6,7},{7,6},{8,9},{9,8},{10,11... | collective-permute-start | bytes 6291464 | tf_op jit(solution)/shard_map/ppermute | solution.py:215
  135.9 15.6 %copy-start.22 = (s32[2]{0:T(128)S(1)}, s32[2]{0:T(128)}, u32[]{:S(2)}) copy-start(s32[2]{0:T(128)} %copy-done.20) | copy-start | bytes 28
  135.9 31.0 %all-to-all-start.3 = ((f32[8,32,8,256]{3,2,1,0:T(8,128)}), f32[8,32,8,256]{3,2,1,0:T(8,128)}, u32[]{:S(2)}, u32[]{:S(2)}) async-start(f32[8,32,8,256]{3,2,1,0:T(8,128)} %bitcast.13), calls=%async_computation.3 | async-start | bytes 4194304 | tf_op jit(solution)/shard_map/all_to_all | solution.py:237
  140.4 11.1 %collective-permute-start.10 = (f32[2,32,8,256]{3,2,1,0:T(8,128)}, f32[2,32,8,256]{3,2,1,0:T(8,128)S(1)}, u32[]{:S(2)}, u32[]{:S(2)}) collective-permute-start(f32[2,32,8,256]{3,2,1,0:T(8,128)} %slice.51), channel_id=1, source_target_pairs={{1,16},{3,18},{5,20},{7,22},{9,24},{11,26},{13,28},{15,30},{16,1},... | collective-permute-start | bytes 1572872 | tf_op jit(solution)/shard_map/ppermute | solution.py:225
  151.5 1.6 copy-start.2
  153.1 1.6 copy-start.5
  154.7 1.1 copy-start.15
  166.9 32.5 %all-to-all-start.4 = ((f32[8,32,8,256]{3,2,1,0:T(8,128)}), f32[8,32,8,256]{3,2,1,0:T(8,128)}, u32[]{:S(2)}, u32[]{:S(2)}) async-start(f32[8,32,8,256]{3,2,1,0:T(8,128)} %local_terms.4), calls=%async_computation.4 | async-start | bytes 4194304 | tf_op jit(solution)/shard_map/all_to_all | solution.py:237
  174.5 13.7 %collective-permute-start.11 = (f32[3,32,8,256]{3,2,1,0:T(8,128)S(1)}, f32[3,32,8,256]{3,2,1,0:T(8,128)S(1)}, u32[]{:S(2)}, u32[]{:S(2)}) collective-permute-start(f32[3,32,8,256]{3,2,1,0:T(8,128)S(1)} %get-tuple-element.61), channel_id=1, source_target_pairs={{1,16},{3,18},{5,20},{7,22},{9,24},{11,26},{13,28},{15,30},{16,1},... | collective-permute-start | bytes 2359304 | tf_op jit(solution)/shard_map/ppermute | solution.py:225
  176.5 20.2 %collective-permute-start.12 = (f32[3,32,8,256]{3,2,1,0:T(8,128)S(1)}, f32[3,32,8,256]{3,2,1,0:T(8,128)S(1)}, u32[]{:S(2)}, u32[]{:S(2)}) collective-permute-start(f32[3,32,8,256]{3,2,1,0:T(8,128)S(1)} %get-tuple-element.60), channel_id=1, source_target_pairs={{1,16},{3,18},{5,20},{7,22},{9,24},{11,26},{13,28},{15,30},{16,1},... | collective-permute-start | bytes 2359304 | tf_op jit(solution)/shard_map/ppermute | solution.py:225
  196.7 0.9 copy-start.12
  199.4 21.5 %collective-permute-start.13 = (f32[8,32,8,256]{3,2,1,0:T(8,128)S(1)}, f32[8,32,8,256]{3,2,1,0:T(8,128)}, u32[]{:S(2)}, u32[]{:S(2)}) collective-permute-start(f32[8,32,8,256]{3,2,1,0:T(8,128)S(1)} %add.31.cur.own), channel_id=1, source_target_pairs={{0,1},{1,0},{2,3},{3,2},{4,5},{5,4},{6,7},{7,6},{8,9},{9,8},{10,11... | collective-permute-start | bytes 6291464 | tf_op jit(solution)/shard_map/ppermute | solution.py:215
  204.5 30.8 %all-to-all-start.5 = ((f32[8,32,8,256]{3,2,1,0:T(8,128)}), f32[8,32,8,256]{3,2,1,0:T(8,128)}, u32[]{:S(2)}, u32[]{:S(2)}) async-start(f32[8,32,8,256]{3,2,1,0:T(8,128)} %bitcast.14), calls=%async_computation.5 | async-start | bytes 4194304 | tf_op jit(solution)/shard_map/all_to_all | solution.py:237
  208.9 1.0 copy-start.26
  208.9 3.1 %copy-start.23 = (s32[2]{0:T(128)S(1)}, s32[2]{0:T(128)}, u32[]{:S(2)}) copy-start(s32[2]{0:T(128)} %copy-done.20) | copy-start | bytes 28
  209.0 11.9 %copy-start.3 = (f32[8,32,8,256]{3,2,1,0:T(8,128)S(1)}, f32[8,32,8,256]{3,2,1,0:T(8,128)}, u32[]{:S(2)}) copy-start(f32[8,32,8,256]{3,2,1,0:T(8,128)} %copy-done.1) | copy-start | bytes 6291460
  209.0 11.9 %copy-start.6 = (f32[32,64,256]{2,1,0:T(8,128)S(1)}, f32[32,64,256]{2,1,0:T(8,128)}, u32[]{:S(2)}) copy-start(f32[32,64,256]{2,1,0:T(8,128)} %constant_dynamic-update-slice_fusion.pot) | copy-start | bytes 6291460
  209.0 11.9 %copy-start.13 = (f32[3,32,8,256]{3,2,1,0:T(8,128)S(1)}, f32[3,32,8,256]{3,2,1,0:T(8,128)}, u32[]{:S(2)}) copy-start(f32[3,32,8,256]{3,2,1,0:T(8,128)} %copy-done.12) | copy-start | bytes 2359300
  209.0 2.9 %collective-permute-start.15 = (f32[8,16,8,256]{3,2,1,0:T(8,128)S(1)}, f32[8,16,8,256]{3,2,1,0:T(8,128)S(1)}, u32[]{:S(2)}, u32[]{:S(2)}) collective-permute-start(f32[8,16,8,256]{3,2,1,0:T(8,128)S(1)} %slice.57), channel_id=1, source_target_pairs={{0,1},{1,0},{2,3},{3,2},{4,5},{5,4},{6,7},{7,6},{8,9},{9,8},{10,11... | collective-permute-start | bytes 3145736 | tf_op jit(solution)/shard_map/ppermute | solution.py:215
  209.9 11.0 %collective-permute-start.14 = (f32[2,32,8,256]{3,2,1,0:T(8,128)S(1)}, f32[2,32,8,256]{3,2,1,0:T(8,128)S(1)}, u32[]{:S(2)}, u32[]{:S(2)}) collective-permute-start(f32[2,32,8,256]{3,2,1,0:T(8,128)S(1)} %copy-done.26), channel_id=1, source_target_pairs={{1,16},{3,18},{5,20},{7,22},{9,24},{11,26},{13,28},{15,30},{16,1},... | collective-permute-start | bytes 1572872 | tf_op jit(solution)/shard_map/ppermute | solution.py:225
  226.9 1.3 copy-start.7
  235.3 5.2 %copy-start.8 = (f32[8,32,8,256]{3,2,1,0:T(8,128)S(1)}, f32[8,32,8,256]{3,2,1,0:T(8,128)}, u32[]{:S(2)}) copy-start(f32[8,32,8,256]{3,2,1,0:T(8,128)} %copy-done.7) | copy-start | bytes 6291460
  237.1 3.3 %collective-permute-start.16 = (f32[8,16,8,256]{3,2,1,0:T(8,128)S(1)}, f32[8,16,8,256]{3,2,1,0:T(8,128)S(1)}, u32[]{:S(2)}, u32[]{:S(2)}) collective-permute-start(f32[8,16,8,256]{3,2,1,0:T(8,128)S(1)} %slice_add_fusion), channel_id=1, source_target_pairs={{0,1},{1,0},{2,3},{3,2},{4,5},{5,4},{6,7},{7,6},{8,9},{9,8},{10,11... | collective-permute-start | bytes 3145736 | tf_op jit(solution)/shard_map/ppermute | solution.py:215
  (3 other events, 2.2 us)

commit v4 on v3

--- a/solution.py
+++ b/solution.py
@@ -11,7 +11,7 @@
 SPREAD = 7.0
 CHIPS = 8
 OCT = 8
-BOUNDS = ((0, 3), (3, 5), (5, 8))
+BOUNDS = ((0, 2), (2, 5), (5, 8))
 F32 = jnp.float32
 BF16 = jnp.bfloat16
 

time: 246 us -> 247 us (level)
  transfers between devices with their start and end apart: 23 -> 23, of which waited for: 16 -> 13; matrix products, arithmetic and copies ran while one was open for 5% -> 5% of each run, Pallas kernels for 15% -> 15%
where the time goes in v4:
time: 247 us; the launch traced here: 245 us
  waiting for transfers between devices  113 us (46%)
  starting transfers between devices  57.2 us (23%)
  Pallas kernels  42.3 us (17%)
  local copies, waits for them, and re-layouts  24.3 us (10%)
  other arithmetic  7.1 us (3%)
    ppermute x9, waiting for transfers between devices, swap_far(): return lax.ppermute(x, ('ka', 'ga'), pairs)  69.4 us
    all_to_all x6, waiting for transfers between devices, turn(): lax.all_to_all(x, 'ga', 0, 0, axis_index_groups=same_core, tiled=True)  41.3 us
    all_to_all x6, starting transfers between devices, turn(): lax.all_to_all(x, 'ga', 0, 0, axis_index_groups=same_core, tiled=True)  27.8 us
    ppermute x9, starting transfers between devices, swap_far(): return lax.ppermute(x, ('ka', 'ga'), pairs)  22.6 us
    pallas_call x3, Pallas kernels, local_terms(): pl.pallas_call(kernel, grid=(32 // step,), in_specs=specs, out_specs=whol...  19.9 us
    unnamed x57, local copies, waits for them, and re-layouts  16 us
    pallas_call x3, Pallas kernels, radial_term(): pl.pallas_call(kernel, grid=(2,), in_specs=[pl.BlockSpec(memory_space=plt...  12.4 us
    ppermute x8, starting transfers between devices, swap_core(): return lax.ppermute(x, 'ga', [(g, g ^ 1) for g in range(members)])  6.74 us
  transfers between devices with their start and end apart: 23, of which 13 were waited for; matrix products, arithmetic and copies ran while one was open for 5% of the time, Pallas kernels for 15%

profile of v4, /device:TPU:1, one launch (start us, length us, event | category | flops | bytes accessed | tf_op | source)
XLA Modules:
  0.0 245.0 jit_solution(3540624984382746336)
XLA Ops:
  0.7 2.4 dynamic-slice_bitcast_fusion
  3.1 3.2 %collective-permute-start.1 = (f32[16,64,256]{2,1,0:T(8,128)}, f32[16,64,256]{2,1,0:T(8,128)S(1)}, u32[]{:S(2)}, u32[]{:S(2)}) collective-permute-start(f32[16,64,256]{2,1,0:T(8,128)} %dynamic-slice_bitcast_fusion), channel_id=1, source_target_pairs={{0,1},{1,0},{2,3},{3,2},{4,5},{5,4},{6,7},{7,6},{8,9},{9,8},{10,11... | collective-permute-start | bytes 3145736 | tf_op jit(solution)/shard_map/ppermute | solution.py:215
  10.6 2.5 %start.1.cur.rest_0_ = f32[8,32,8,256]{3,2,1,0:T(8,128)} custom-call(s32[2]{0:T(128)S(1)} %pad_add_fusion.ids, s32[2,256]{1,0:T(2,128)S(1)} %copy-done.18, f32[2,16,64,256]{3,2,1,0:T(8,128)S(1)} %copy-done.9, f32[16,64,256]{2,1,0:T(8,128)S(1)} %collective-permute-done.1.other), custom_call_target="tpu_custom_call" | custom-call | tf_op jit(solution)/shard_map/start/pallas_call | solution.py:76
  13.1 5.0 %all-to-all-start = ((f32[8,32,8,256]{3,2,1,0:T(8,128)}), f32[8,32,8,256]{3,2,1,0:T(8,128)}, u32[]{:S(2)}, u32[]{:S(2)}) async-start(f32[8,32,8,256]{3,2,1,0:T(8,128)} %start.1.cur.rest_0_), calls=%async_computation | async-start | bytes 4194304 | tf_op jit(solution)/shard_map/all_to_all | solution.py:237
  19.2 3.7 %collective-permute-start.3 = (f32[3,32,8,256]{3,2,1,0:T(8,128)S(1)}, f32[3,32,8,256]{3,2,1,0:T(8,128)S(1)}, u32[]{:S(2)}, u32[]{:S(2)}) collective-permute-start(f32[3,32,8,256]{3,2,1,0:T(8,128)S(1)} %get-tuple-element.64), channel_id=1, source_target_pairs={{1,16},{3,18},{5,20},{7,22},{9,24},{11,26},{13,28},{15,30},{16,1},... | collective-permute-start | bytes 2359304 | tf_op jit(solution)/shard_map/ppermute | solution.py:225
  23.0 1.9 collective-permute-start.2
  24.9 13.7 %collective-permute-done.2.far = f32[2,32,8,256]{3,2,1,0:T(8,128)S(1)} collective-permute-done((f32[2,32,8,256]{3,2,1,0:T(8,128)S(1)}, f32[2,32,8,256]{3,2,1,0:T(8,128)S(1)}, u32[]{:S(2)}, u32[]{:S(2)}) %collective-permute-start.2) | collective-permute-done | bytes 524320 | tf_op jit(solution)/shard_map/ppermute | solution.py:225
  39.4 10.6 %all-to-all-done = f32[8,32,8,256]{3,2,1,0:T(8,128)} async-done(((f32[8,32,8,256]{3,2,1,0:T(8,128)}), f32[8,32,8,256]{3,2,1,0:T(8,128)}, u32[]{:S(2)}, u32[]{:S(2)}) %all-to-all-start) | async-done | bytes 2097184 | tf_op jit(solution)/shard_map/all_to_all | solution.py:237
  51.2 3.7 %radial_term.3.refs_1_ = f32[2048,256]{1,0:T(8,128)} custom-call(s32[2]{0:T(128)} %copy-done.20, f32[256,128]{1,0:T(8,128)} %copy-done.25, bf16[2,256,256]{2,1,0:T(8,128)(2,1)} %copy-done.24, f32[2048,256]{1,0:T(8,128)} %bitcast.5.refs_0_), custom_call_target="tpu_custom_call" | custom-call | flops 2000000000 | bytes 5000000 | tf_op jit(solution)/shard_map/radial_term/pallas_call | solution.py:166
  54.9 4.5 %all-to-all-start.1 = ((f32[8,32,8,256]{3,2,1,0:T(8,128)}), f32[8,32,8,256]{3,2,1,0:T(8,128)}, u32[]{:S(2)}, u32[]{:S(2)}) async-start(f32[8,32,8,256]{3,2,1,0:T(8,128)} %bitcast.12), calls=%async_computation.1 | async-start | bytes 4194304 | tf_op jit(solution)/shard_map/all_to_all | solution.py:237
  59.5 1.9 collective-permute-start.5
  61.7 2.3 constant_dynamic-update-slice_fusion.1
  64.1 2.3 constant_dynamic-update-slice_fusion.pot
  66.4 7.0 %collective-permute-done.5.far_mid = f32[3,32,8,256]{3,2,1,0:T(8,128)} collective-permute-done((f32[3,32,8,256]{3,2,1,0:T(8,128)}, f32[3,32,8,256]{3,2,1,0:T(8,128)}, u32[]{:S(2)}, u32[]{:S(2)}) %collective-permute-start.5) | collective-permute-done | bytes 786464 | tf_op jit(solution)/shard_map/ppermute | solution.py:225
  73.5 1.6 copy-done.4
  75.0 7.0 %local_terms.3 = f32[8,32,8,256]{3,2,1,0:T(8,128)} custom-call(s32[2]{0:T(128)S(1)} %copy-done.21, s32[2,256]{1,0:T(2,128)S(1)} %copy-done.18, f32[34]{0:T(128)S(1)} %pad_maximum_fusion.coef, f32[8,32,8,256]{3,2,1,0:T(8,128)S(1)} %copy-done, f32[8,32,8,256]{3,2,1,0:T(8,128)} %collective-permute-done.4.near, f32[2,32,8,256]{3,2,1,0:T(8,128)S(1)} %copy-done.11, ...), custom_call_target="tpu_custom_call" | custom-call | flops 2000000000 | bytes 14000000 | tf_op jit(solution)/shard_map/local_terms/pallas_call | solution.py:132
  82.0 12.6 %all-to-all-done.1 = f32[8,32,8,256]{3,2,1,0:T(8,128)} async-done(((f32[8,32,8,256]{3,2,1,0:T(8,128)}), f32[8,32,8,256]{3,2,1,0:T(8,128)}, u32[]{:S(2)}, u32[]{:S(2)}) %all-to-all-start.1) | async-done | bytes 2097184 | tf_op jit(solution)/shard_map/all_to_all | solution.py:237
  94.7 4.4 %all-to-all-start.2 = ((f32[8,32,8,256]{3,2,1,0:T(8,128)}), f32[8,32,8,256]{3,2,1,0:T(8,128)}, u32[]{:S(2)}, u32[]{:S(2)}) async-start(f32[8,32,8,256]{3,2,1,0:T(8,128)} %local_terms.3), calls=%async_computation.2 | async-start | bytes 4194304 | tf_op jit(solution)/shard_map/all_to_all | solution.py:237
  99.0 2.6 %add.30.cur.rest_0_ = f32[8,32,8,256]{3,2,1,0:T(8,128)S(1)} add(f32[8,32,8,256]{3,2,1,0:T(8,128)} %local_terms.3, f32[8,32,8,256]{3,2,1,0:T(8,128)} %all-to-all-done.1) | non-fusion elementwise | flops 524288 | bytes 6291456 | tf_op jit(solution)/shard_map/add | solution.py:261
  102.8 1.9 collective-permute-start.8
  104.8 3.6 %collective-permute-start.7 = (f32[2,32,8,256]{3,2,1,0:T(8,128)S(1)}, f32[2,32,8,256]{3,2,1,0:T(8,128)S(1)}, u32[]{:S(2)}, u32[]{:S(2)}) collective-permute-start(f32[2,32,8,256]{3,2,1,0:T(8,128)S(1)} %slice.52), channel_id=1, source_target_pairs={{1,16},{3,18},{5,20},{7,22},{9,24},{11,26},{13,28},{15,30},{16,1},... | collective-permute-start | bytes 1572872 | tf_op jit(solution)/shard_map/ppermute | solution.py:225
  108.4 13.7 %collective-permute-done.7.far = f32[2,32,8,256]{3,2,1,0:T(8,128)S(1)} collective-permute-done((f32[2,32,8,256]{3,2,1,0:T(8,128)S(1)}, f32[2,32,8,256]{3,2,1,0:T(8,128)S(1)}, u32[]{:S(2)}, u32[]{:S(2)}) %collective-permute-start.7) | collective-permute-done | bytes 524320 | tf_op jit(solution)/shard_map/ppermute | solution.py:225
  122.9 7.7 %all-to-all-done.2 = f32[8,32,8,256]{3,2,1,0:T(8,128)} async-done(((f32[8,32,8,256]{3,2,1,0:T(8,128)}), f32[8,32,8,256]{3,2,1,0:T(8,128)}, u32[]{:S(2)}, u32[]{:S(2)}) %all-to-all-start.2) | async-done | bytes 2097184 | tf_op jit(solution)/shard_map/all_to_all | solution.py:237
  131.2 4.3 %radial_term.4.refs_1_ = f32[2048,256]{1,0:T(8,128)} custom-call(s32[2]{0:T(128)} %copy-done.20, f32[256,128]{1,0:T(8,128)} %copy-done.25, bf16[2,256,256]{2,1,0:T(8,128)(2,1)} %copy-done.24, f32[2048,256]{1,0:T(8,128)} %bitcast.7.refs_0_, f32[2048,256]{1,0:T(8,128)} %radial_term.3.refs_1_), custom_call_target="tpu_custom_call" | custom-call | flops 2000000000 | bytes 5000000 | tf_op jit(solution)/shard_map/radial_term/pallas_call | solution.py:166
  135.5 4.5 %all-to-all-start.3 = ((f32[8,32,8,256]{3,2,1,0:T(8,128)}), f32[8,32,8,256]{3,2,1,0:T(8,128)}, u32[]{:S(2)}, u32[]{:S(2)}) async-start(f32[8,32,8,256]{3,2,1,0:T(8,128)} %bitcast.13), calls=%async_computation.3 | async-start | bytes 4194304 | tf_op jit(solution)/shard_map/all_to_all | solution.py:237
  140.0 1.9 collective-permute-start.10
  142.0 12.0 %collective-permute-done.10.far_mid = f32[3,32,8,256]{3,2,1,0:T(8,128)S(1)} collective-permute-done((f32[3,32,8,256]{3,2,1,0:T(8,128)}, f32[3,32,8,256]{3,2,1,0:T(8,128)S(1)}, u32[]{:S(2)}, u32[]{:S(2)}) %collective-permute-start.10) | collective-permute-done | bytes 786464 | tf_op jit(solution)/shard_map/ppermute | solution.py:225
  154.0 1.6 copy-done.2
  155.6 1.6 copy-done.5
  158.2 6.9 %local_terms.4 = f32[8,32,8,256]{3,2,1,0:T(8,128)} custom-call(s32[2]{0:T(128)S(1)} %copy-done.22, s32[2,256]{1,0:T(2,128)S(1)} %copy-done.18, f32[34]{0:T(128)S(1)} %pad_maximum_fusion.coef, f32[8,32,8,256]{3,2,1,0:T(8,128)S(1)} %copy-done.2, f32[8,32,8,256]{3,2,1,0:T(8,128)} %collective-permute-done.9.near, f32[2,32,8,256]{3,2,1,0:T(8,128)S(1)} %copy-done.15, ...), custom_call_target="tpu_custom_call" | custom-call | flops 2000000000 | bytes 14000000 | tf_op jit(solution)/shard_map/local_terms/pallas_call | solution.py:132
  165.1 1.5 all-to-all-done.3
  166.6 5.1 %all-to-all-start.4 = ((f32[8,32,8,256]{3,2,1,0:T(8,128)}), f32[8,32,8,256]{3,2,1,0:T(8,128)}, u32[]{:S(2)}, u32[]{:S(2)}) async-start(f32[8,32,8,256]{3,2,1,0:T(8,128)} %local_terms.4), calls=%async_computation.4 | async-start | bytes 4194304 | tf_op jit(solution)/shard_map/all_to_all | solution.py:237
  171.6 2.6 %add.31.cur.own = f32[8,32,8,256]{3,2,1,0:T(8,128)S(1)} add(f32[8,32,8,256]{3,2,1,0:T(8,128)} %local_terms.4, f32[8,32,8,256]{3,2,1,0:T(8,128)} %all-to-all-done.3) | non-fusion elementwise | flops 524288 | bytes 6291456 | tf_op jit(solution)/shard_map/add | solution.py:265
  175.2 1.9 collective-permute-start.12
  177.2 3.6 %collective-permute-start.11 = (f32[2,32,8,256]{3,2,1,0:T(8,128)S(1)}, f32[2,32,8,256]{3,2,1,0:T(8,128)S(1)}, u32[]{:S(2)}, u32[]{:S(2)}) collective-permute-start(f32[2,32,8,256]{3,2,1,0:T(8,128)S(1)} %slice.55), channel_id=1, source_target_pairs={{1,16},{3,18},{5,20},{7,22},{9,24},{11,26},{13,28},{15,30},{16,1},... | collective-permute-start | bytes 1572872 | tf_op jit(solution)/shard_map/ppermute | solution.py:225
  180.8 13.7 %collective-permute-done.11.far = f32[2,32,8,256]{3,2,1,0:T(8,128)S(1)} collective-permute-done((f32[2,32,8,256]{3,2,1,0:T(8,128)S(1)}, f32[2,32,8,256]{3,2,1,0:T(8,128)S(1)}, u32[]{:S(2)}, u32[]{:S(2)}) %collective-permute-start.11) | collective-permute-done | bytes 524320 | tf_op jit(solution)/shard_map/ppermute | solution.py:225
  195.3 4.7 %all-to-all-done.4 = f32[8,32,8,256]{3,2,1,0:T(8,128)} async-done(((f32[8,32,8,256]{3,2,1,0:T(8,128)}), f32[8,32,8,256]{3,2,1,0:T(8,128)}, u32[]{:S(2)}, u32[]{:S(2)}) %all-to-all-start.4) | async-done | bytes 2097184 | tf_op jit(solution)/shard_map/all_to_all | solution.py:237
  200.6 4.4 %radial_term.5 = f32[2048,256]{1,0:T(8,128)} custom-call(s32[2]{0:T(128)} %copy-done.20, f32[256,128]{1,0:T(8,128)} %copy-done.25, bf16[2,256,256]{2,1,0:T(8,128)(2,1)} %copy-done.24, f32[2048,256]{1,0:T(8,128)} %bitcast.9.refs_0_, f32[2048,256]{1,0:T(8,128)} %radial_term.4.refs_1_), custom_call_target="tpu_custom_call" | custom-call | flops 2000000000 | bytes 5000000 | tf_op jit(solution)/shard_map/radial_term/pallas_call | solution.py:166
  204.9 4.3 %all-to-all-start.5 = ((f32[8,32,8,256]{3,2,1,0:T(8,128)}), f32[8,32,8,256]{3,2,1,0:T(8,128)}, u32[]{:S(2)}, u32[]{:S(2)}) async-start(f32[8,32,8,256]{3,2,1,0:T(8,128)} %bitcast.14), calls=%async_computation.5 | async-start | bytes 4194304 | tf_op jit(solution)/shard_map/all_to_all | solution.py:237
  210.4 2.0 collective-permute-start.14
  212.5 2.5 %finish.2 = f32[2,16,64,256]{3,2,1,0:T(8,128)} custom-call(s32[2]{0:T(128)S(1)} %copy-done.23, f32[8,32,8,256]{3,2,1,0:T(8,128)S(1)} %add.31.cur.own, f32[8,16,8,256]{3,2,1,0:T(8,128)S(1)} %collective-permute-done.15.other), custom_call_target="tpu_custom_call" | custom-call | tf_op jit(solution)/shard_map/finish/pallas_call | solution.py:192
  214.9 9.3 %collective-permute-done.14.far_mid = f32[3,32,8,256]{3,2,1,0:T(8,128)S(1)} collective-permute-done((f32[3,32,8,256]{3,2,1,0:T(8,128)S(1)}, f32[3,32,8,256]{3,2,1,0:T(8,128)S(1)}, u32[]{:S(2)}, u32[]{:S(2)}) %collective-permute-start.14) | collective-permute-done | bytes 786464 | tf_op jit(solution)/shard_map/ppermute | solution.py:225
  224.3 6.0 %local_terms.5.own = f32[8,32,8,256]{3,2,1,0:T(8,128)S(1)} custom-call(s32[2]{0:T(128)S(1)} %copy-done.23, s32[2,256]{1,0:T(2,128)S(1)} %copy-done.18, f32[34]{0:T(128)S(1)} %pad_maximum_fusion.coef, f32[8,32,8,256]{3,2,1,0:T(8,128)S(1)} %add.31.cur.own, f32[8,32,8,256]{3,2,1,0:T(8,128)} %collective-permute-done.13.near, f32[2,32,8,256]{3,2,1,0:T(8,128)S(1)} %copy-done.13, ...), custom_call_target="tpu_custom_call" | custom-call | flops 2000000000 | bytes 14000000 | tf_op jit(solution)/shard_map/local_terms/pallas_call | solution.py:132
  230.3 1.3 copy-done.7
  231.6 4.2 %all-to-all-done.5.rest_0_ = f32[8,32,8,256]{3,2,1,0:T(8,128)} async-done(((f32[8,32,8,256]{3,2,1,0:T(8,128)}), f32[8,32,8,256]{3,2,1,0:T(8,128)}, u32[]{:S(2)}, u32[]{:S(2)}) %all-to-all-start.5) | async-done | bytes 2097184 | tf_op jit(solution)/shard_map/all_to_all | solution.py:237
  235.7 1.8 slice_add_fusion
  238.6 2.3 collective-permute-done.16.other
  240.8 4.2 %finish.3 = f32[2,16,64,256]{3,2,1,0:T(8,128)} custom-call(s32[2]{0:T(128)S(1)} %copy-done.23, f32[8,32,8,256]{3,2,1,0:T(8,128)S(1)} %copy-done.8, f32[8,16,8,256]{3,2,1,0:T(8,128)S(1)} %collective-permute-done.16.other, f32[8,32,8,256]{3,2,1,0:T(8,128)} %all-to-all-done.5.rest_0_), custom_call_target="tpu_custom_call" | custom-call | tf_op jit(solution)/shard_map/finish/pallas_call | solution.py:192
  (79 shorter events, 15.7 us)
Async XLA Ops:
  0.6 9.9 %copy-start.9 = (f32[2,16,64,256]{3,2,1,0:T(8,128)S(1)}, f32[2,16,64,256]{3,2,1,0:T(8,128)}, u32[]{:S(2)}) copy-start(f32[2,16,64,256]{3,2,1,0:T(8,128)} %own.1) | copy-start | bytes 6291460
  0.6 5.8 %copy-start.19 = (f32[64,64]{1,0:T(8,128)S(1)}, f32[64,64]{1,0:T(8,128)}, u32[]{:S(2)}) copy-start(f32[64,64]{1,0:T(8,128)} %bond.1) | copy-start | bytes 49156
  0.6 5.8 %copy-start.18 = (s32[2,256]{1,0:T(2,128)S(1)}, s32[2,256]{1,0:T(2,128)}, u32[]{:S(2)}) copy-start(s32[2,256]{1,0:T(2,128)} %ext.7) | copy-start | bytes 6148
  3.1 7.4 %collective-permute-start.1 = (f32[16,64,256]{2,1,0:T(8,128)}, f32[16,64,256]{2,1,0:T(8,128)S(1)}, u32[]{:S(2)}, u32[]{:S(2)}) collective-permute-start(f32[16,64,256]{2,1,0:T(8,128)} %dynamic-slice_bitcast_fusion), channel_id=1, source_target_pairs={{0,1},{1,0},{2,3},{3,2},{4,5},{5,4},{6,7},{7,6},{8,9},{9,8},{10,11... | collective-permute-start | bytes 3145736 | tf_op jit(solution)/shard_map/ppermute | solution.py:215
  6.4 1.0 copy-start.16
  7.4 0.9 copy-start.17
  8.3 4.8 %copy-start.20 = (s32[2]{0:T(128)}, s32[2]{0:T(128)S(1)}, u32[]{:S(2)}) copy-start(s32[2]{0:T(128)S(1)} %pad_add_fusion.ids) | copy-start | bytes 28
  13.1 5.1 %copy-start = (f32[8,32,8,256]{3,2,1,0:T(8,128)S(1)}, f32[8,32,8,256]{3,2,1,0:T(8,128)}, u32[]{:S(2)}) copy-start(f32[8,32,8,256]{3,2,1,0:T(8,128)} %start.1.cur.rest_0_) | copy-start | bytes 6291460
  13.1 37.0 %all-to-all-start = ((f32[8,32,8,256]{3,2,1,0:T(8,128)}), f32[8,32,8,256]{3,2,1,0:T(8,128)}, u32[]{:S(2)}, u32[]{:S(2)}) async-start(f32[8,32,8,256]{3,2,1,0:T(8,128)} %start.1.cur.rest_0_), calls=%async_computation | async-start | bytes 4194304 | tf_op jit(solution)/shard_map/all_to_all | solution.py:237
  19.2 20.2 %collective-permute-start.3 = (f32[3,32,8,256]{3,2,1,0:T(8,128)S(1)}, f32[3,32,8,256]{3,2,1,0:T(8,128)S(1)}, u32[]{:S(2)}, u32[]{:S(2)}) collective-permute-start(f32[3,32,8,256]{3,2,1,0:T(8,128)S(1)} %get-tuple-element.64), channel_id=1, source_target_pairs={{1,16},{3,18},{5,20},{7,22},{9,24},{11,26},{13,28},{15,30},{16,1},... | collective-permute-start | bytes 2359304 | tf_op jit(solution)/shard_map/ppermute | solution.py:225
  23.0 15.6 %collective-permute-start.2 = (f32[2,32,8,256]{3,2,1,0:T(8,128)S(1)}, f32[2,32,8,256]{3,2,1,0:T(8,128)S(1)}, u32[]{:S(2)}, u32[]{:S(2)}) collective-permute-start(f32[2,32,8,256]{3,2,1,0:T(8,128)S(1)} %slice.49), channel_id=1, source_target_pairs={{1,16},{3,18},{5,20},{7,22},{9,24},{11,26},{13,28},{15,30},{16,1},... | collective-permute-start | bytes 1572872 | tf_op jit(solution)/shard_map/ppermute | solution.py:225
  50.1 23.4 %collective-permute-start.4 = (f32[8,32,8,256]{3,2,1,0:T(8,128)S(1)}, f32[8,32,8,256]{3,2,1,0:T(8,128)}, u32[]{:S(2)}, u32[]{:S(2)}) collective-permute-start(f32[8,32,8,256]{3,2,1,0:T(8,128)S(1)} %copy-done), channel_id=1, source_target_pairs={{0,1},{1,0},{2,3},{3,2},{4,5},{5,4},{6,7},{7,6},{8,9},{9,8},{10,11... | collective-permute-start | bytes 6291464 | tf_op jit(solution)/shard_map/ppermute | solution.py:215
  54.9 6.5 %copy-start.27 = (f32[16]{0:T(128)S(1)}, f32[16]{0:T(128)}, u32[]{:S(2)}) copy-start(f32[16]{0:T(128)} %param.10) | copy-start | bytes 196
  54.9 39.7 %all-to-all-start.1 = ((f32[8,32,8,256]{3,2,1,0:T(8,128)}), f32[8,32,8,256]{3,2,1,0:T(8,128)}, u32[]{:S(2)}, u32[]{:S(2)}) async-start(f32[8,32,8,256]{3,2,1,0:T(8,128)} %bitcast.12), calls=%async_computation.1 | async-start | bytes 4194304 | tf_op jit(solution)/shard_map/all_to_all | solution.py:237
  59.4 4.7 %collective-permute-start.6 = (f32[16,64,256]{2,1,0:T(8,128)}, f32[16,64,256]{2,1,0:T(8,128)}, u32[]{:S(2)}, u32[]{:S(2)}) collective-permute-start(f32[16,64,256]{2,1,0:T(8,128)} %param.9), channel_id=1, source_target_pairs={{0,1},{1,0},{2,3},{3,2},{4,5},{5,4},{6,7},{7,6},{8,9},{9,8},{10,11... | collective-permute-start | bytes 3145736 | tf_op jit(solution)/shard_map/ppermute | solution.py:215
  59.5 13.9 %collective-permute-start.5 = (f32[3,32,8,256]{3,2,1,0:T(8,128)}, f32[3,32,8,256]{3,2,1,0:T(8,128)}, u32[]{:S(2)}, u32[]{:S(2)}) collective-permute-start(f32[3,32,8,256]{3,2,1,0:T(8,128)} %get-tuple-element.39), channel_id=1, source_target_pairs={{1,16},{3,18},{5,20},{7,22},{9,24},{11,26},{13,28},{15,30},{16,1},... | collective-permute-start | bytes 2359304 | tf_op jit(solution)/shard_map/ppermute | solution.py:225
  61.5 2.5 %collective-permute-start = (f32[16]{0:T(128)S(1)}, f32[16]{0:T(128)S(1)}, u32[]{:S(2)}, u32[]{:S(2)}) collective-permute-start(f32[16]{0:T(128)S(1)} %copy-done.27), channel_id=1, source_target_pairs={{0,1},{1,0},{2,3},{3,2},{4,5},{5,4},{6,7},{7,6},{8,9},{9,8},{10,11... | collective-permute-start | bytes 200 | tf_op jit(solution)/shard_map/ppermute | solution.py:215
  61.7 11.8 %copy-start.21 = (s32[2]{0:T(128)S(1)}, s32[2]{0:T(128)}, u32[]{:S(2)}) copy-start(s32[2]{0:T(128)} %copy-done.20) | copy-start | bytes 28
  64.0 9.5 %copy-start.11 = (f32[2,32,8,256]{3,2,1,0:T(8,128)S(1)}, f32[2,32,8,256]{3,2,1,0:T(8,128)}, u32[]{:S(2)}) copy-start(f32[2,32,8,256]{3,2,1,0:T(8,128)} %copy-done.10) | copy-start | bytes 1572868
  73.4 1.6 copy-start.4
  94.7 36.0 %all-to-all-start.2 = ((f32[8,32,8,256]{3,2,1,0:T(8,128)}), f32[8,32,8,256]{3,2,1,0:T(8,128)}, u32[]{:S(2)}, u32[]{:S(2)}) async-start(f32[8,32,8,256]{3,2,1,0:T(8,128)} %local_terms.3), calls=%async_computation.2 | async-start | bytes 4194304 | tf_op jit(solution)/shard_map/all_to_all | solution.py:237
  101.6 3.2 %copy-start.1 = (f32[8,32,8,256]{3,2,1,0:T(8,128)}, f32[8,32,8,256]{3,2,1,0:T(8,128)S(1)}, u32[]{:S(2)}) copy-start(f32[8,32,8,256]{3,2,1,0:T(8,128)S(1)} %add.30.cur.rest_0_) | copy-start | bytes 6291460
  102.8 20.1 %collective-permute-start.8 = (f32[3,32,8,256]{3,2,1,0:T(8,128)S(1)}, f32[3,32,8,256]{3,2,1,0:T(8,128)S(1)}, u32[]{:S(2)}, u32[]{:S(2)}) collective-permute-start(f32[3,32,8,256]{3,2,1,0:T(8,128)S(1)} %get-tuple-element.62), channel_id=1, source_target_pairs={{1,16},{3,18},{5,20},{7,22},{9,24},{11,26},{13,28},{15,30},{16,1},... | collective-permute-start | bytes 2359304 | tf_op jit(solution)/shard_map/ppermute | solution.py:225
  104.8 17.3 %collective-permute-start.7 = (f32[2,32,8,256]{3,2,1,0:T(8,128)S(1)}, f32[2,32,8,256]{3,2,1,0:T(8,128)S(1)}, u32[]{:S(2)}, u32[]{:S(2)}) collective-permute-start(f32[2,32,8,256]{3,2,1,0:T(8,128)S(1)} %slice.52), channel_id=1, source_target_pairs={{1,16},{3,18},{5,20},{7,22},{9,24},{11,26},{13,28},{15,30},{16,1},... | collective-permute-start | bytes 1572872 | tf_op jit(solution)/shard_map/ppermute | solution.py:225
  122.1 0.8 copy-start.14
  130.6 23.3 %collective-permute-start.9 = (f32[8,32,8,256]{3,2,1,0:T(8,128)}, f32[8,32,8,256]{3,2,1,0:T(8,128)}, u32[]{:S(2)}, u32[]{:S(2)}) collective-permute-start(f32[8,32,8,256]{3,2,1,0:T(8,128)} %copy-done.1), channel_id=1, source_target_pairs={{0,1},{1,0},{2,3},{3,2},{4,5},{5,4},{6,7},{7,6},{8,9},{9,8},{10,11... | collective-permute-start | bytes 6291464 | tf_op jit(solution)/shard_map/ppermute | solution.py:215
  135.5 18.4 %copy-start.22 = (s32[2]{0:T(128)S(1)}, s32[2]{0:T(128)}, u32[]{:S(2)}) copy-start(s32[2]{0:T(128)} %copy-done.20) | copy-start | bytes 28
  135.5 31.0 %all-to-all-start.3 = ((f32[8,32,8,256]{3,2,1,0:T(8,128)}), f32[8,32,8,256]{3,2,1,0:T(8,128)}, u32[]{:S(2)}, u32[]{:S(2)}) async-start(f32[8,32,8,256]{3,2,1,0:T(8,128)} %bitcast.13), calls=%async_computation.3 | async-start | bytes 4194304 | tf_op jit(solution)/shard_map/all_to_all | solution.py:237
  140.0 13.9 %collective-permute-start.10 = (f32[3,32,8,256]{3,2,1,0:T(8,128)}, f32[3,32,8,256]{3,2,1,0:T(8,128)S(1)}, u32[]{:S(2)}, u32[]{:S(2)}) collective-permute-start(f32[3,32,8,256]{3,2,1,0:T(8,128)} %get-tuple-element.49), channel_id=1, source_target_pairs={{1,16},{3,18},{5,20},{7,22},{9,24},{11,26},{13,28},{15,30},{16,1},... | collective-permute-start | bytes 2359304 | tf_op jit(solution)/shard_map/ppermute | solution.py:225
  154.0 1.6 copy-start.2
  155.6 1.6 copy-start.5
  157.2 1.0 copy-start.15
  166.6 33.4 %all-to-all-start.4 = ((f32[8,32,8,256]{3,2,1,0:T(8,128)}), f32[8,32,8,256]{3,2,1,0:T(8,128)}, u32[]{:S(2)}, u32[]{:S(2)}) async-start(f32[8,32,8,256]{3,2,1,0:T(8,128)} %local_terms.4), calls=%async_computation.4 | async-start | bytes 4194304 | tf_op jit(solution)/shard_map/all_to_all | solution.py:237
  175.2 20.1 %collective-permute-start.12 = (f32[3,32,8,256]{3,2,1,0:T(8,128)S(1)}, f32[3,32,8,256]{3,2,1,0:T(8,128)S(1)}, u32[]{:S(2)}, u32[]{:S(2)}) collective-permute-start(f32[3,32,8,256]{3,2,1,0:T(8,128)S(1)} %get-tuple-element.60), channel_id=1, source_target_pairs={{1,16},{3,18},{5,20},{7,22},{9,24},{11,26},{13,28},{15,30},{16,1},... | collective-permute-start | bytes 2359304 | tf_op jit(solution)/shard_map/ppermute | solution.py:225
  177.2 17.4 %collective-permute-start.11 = (f32[2,32,8,256]{3,2,1,0:T(8,128)S(1)}, f32[2,32,8,256]{3,2,1,0:T(8,128)S(1)}, u32[]{:S(2)}, u32[]{:S(2)}) collective-permute-start(f32[2,32,8,256]{3,2,1,0:T(8,128)S(1)} %slice.55), channel_id=1, source_target_pairs={{1,16},{3,18},{5,20},{7,22},{9,24},{11,26},{13,28},{15,30},{16,1},... | collective-permute-start | bytes 1572872 | tf_op jit(solution)/shard_map/ppermute | solution.py:225
  194.5 0.8 copy-start.12
  200.0 24.2 %collective-permute-start.13 = (f32[8,32,8,256]{3,2,1,0:T(8,128)S(1)}, f32[8,32,8,256]{3,2,1,0:T(8,128)}, u32[]{:S(2)}, u32[]{:S(2)}) collective-permute-start(f32[8,32,8,256]{3,2,1,0:T(8,128)S(1)} %add.31.cur.own), channel_id=1, source_target_pairs={{0,1},{1,0},{2,3},{3,2},{4,5},{5,4},{6,7},{7,6},{8,9},{9,8},{10,11... | collective-permute-start | bytes 6291464 | tf_op jit(solution)/shard_map/ppermute | solution.py:215
  204.9 30.8 %all-to-all-start.5 = ((f32[8,32,8,256]{3,2,1,0:T(8,128)}), f32[8,32,8,256]{3,2,1,0:T(8,128)}, u32[]{:S(2)}, u32[]{:S(2)}) async-start(f32[8,32,8,256]{3,2,1,0:T(8,128)} %bitcast.14), calls=%async_computation.5 | async-start | bytes 4194304 | tf_op jit(solution)/shard_map/all_to_all | solution.py:237
  209.3 1.1 copy-start.26
  209.3 3.2 %copy-start.23 = (s32[2]{0:T(128)S(1)}, s32[2]{0:T(128)}, u32[]{:S(2)}) copy-start(s32[2]{0:T(128)} %copy-done.20) | copy-start | bytes 28
  209.4 14.8 %copy-start.3 = (f32[8,32,8,256]{3,2,1,0:T(8,128)S(1)}, f32[8,32,8,256]{3,2,1,0:T(8,128)}, u32[]{:S(2)}) copy-start(f32[8,32,8,256]{3,2,1,0:T(8,128)} %copy-done.1) | copy-start | bytes 6291460
  209.4 14.8 %copy-start.6 = (f32[32,64,256]{2,1,0:T(8,128)S(1)}, f32[32,64,256]{2,1,0:T(8,128)}, u32[]{:S(2)}) copy-start(f32[32,64,256]{2,1,0:T(8,128)} %constant_dynamic-update-slice_fusion.pot) | copy-start | bytes 6291460
  209.4 14.8 %copy-start.13 = (f32[2,32,8,256]{3,2,1,0:T(8,128)S(1)}, f32[2,32,8,256]{3,2,1,0:T(8,128)}, u32[]{:S(2)}) copy-start(f32[2,32,8,256]{3,2,1,0:T(8,128)} %copy-done.12) | copy-start | bytes 1572868
  209.4 3.0 %collective-permute-start.15 = (f32[8,16,8,256]{3,2,1,0:T(8,128)S(1)}, f32[8,16,8,256]{3,2,1,0:T(8,128)S(1)}, u32[]{:S(2)}, u32[]{:S(2)}) collective-permute-start(f32[8,16,8,256]{3,2,1,0:T(8,128)S(1)} %slice.57), channel_id=1, source_target_pairs={{0,1},{1,0},{2,3},{3,2},{4,5},{5,4},{6,7},{7,6},{8,9},{9,8},{10,11... | collective-permute-start | bytes 3145736 | tf_op jit(solution)/shard_map/ppermute | solution.py:215
  210.4 13.8 %collective-permute-start.14 = (f32[3,32,8,256]{3,2,1,0:T(8,128)S(1)}, f32[3,32,8,256]{3,2,1,0:T(8,128)S(1)}, u32[]{:S(2)}, u32[]{:S(2)}) collective-permute-start(f32[3,32,8,256]{3,2,1,0:T(8,128)S(1)} %copy-done.26), channel_id=1, source_target_pairs={{1,16},{3,18},{5,20},{7,22},{9,24},{11,26},{13,28},{15,30},{16,1},... | collective-permute-start | bytes 2359304 | tf_op jit(solution)/shard_map/ppermute | solution.py:225
  230.3 1.3 copy-start.7
  235.7 5.1 %copy-start.8 = (f32[8,32,8,256]{3,2,1,0:T(8,128)S(1)}, f32[8,32,8,256]{3,2,1,0:T(8,128)}, u32[]{:S(2)}) copy-start(f32[8,32,8,256]{3,2,1,0:T(8,128)} %copy-done.7) | copy-start | bytes 6291460
  237.6 3.3 %collective-permute-start.16 = (f32[8,16,8,256]{3,2,1,0:T(8,128)S(1)}, f32[8,16,8,256]{3,2,1,0:T(8,128)S(1)}, u32[]{:S(2)}, u32[]{:S(2)}) collective-permute-start(f32[8,16,8,256]{3,2,1,0:T(8,128)S(1)} %slice_add_fusion), channel_id=1, source_target_pairs={{0,1},{1,0},{2,3},{3,2},{4,5},{5,4},{6,7},{7,6},{8,9},{9,8},{10,11... | collective-permute-start | bytes 3145736 | tf_op jit(solution)/shard_map/ppermute | solution.py:215
  (3 other events, 2.2 us)

commit v5 on v3

--- a/solution.py
+++ b/solution.py
@@ -99,7 +99,9 @@
         line = lax.broadcasted_iota(jnp.int32, (64, 256), 0)
         xs = [cur[:, r].reshape(64, 256) for r in range(step)]
         high, low = split(jnp.concatenate(xs, 0))
-        angle = mm(high, ang[0]) + mm(low, ang[0]) + mm(high, ang[1])
+        angle = mm(
+            jnp.concatenate([high, low, high], 1), jnp.concatenate([ang[0], ang[0], ang[1]], 0)
+        )
         for r in range(step):
             part = slice(r * 64, r * 64 + 64)
             stack = jnp.concatenate([high[part], low[part], high[part]], 0)
@@ -153,9 +155,10 @@
             at = pl.ds(q, 256, stride=OCT)
             return ins[0][at, :] + ins[1][at, :] if count > 1 else ins[0][at, :]
 
+        matrix = jnp.concatenate([rad[0], rad[0], rad[1]], 1)
         for q in range(0, OCT, 2):
             high, low = split(jnp.concatenate([column(q), column(q + 1)], 1))
-            total = mm(rad[0], high) + mm(rad[0], low) + mm(rad[1], high)
+            total = mm(matrix, jnp.concatenate([high, low, high], 0))
             for i in range(2):
                 half = total[:, i * 128 : i * 128 + 128]
                 half = jnp.where(ext_col[...] > (ids[0] * OCT + q + i).astype(F32), half * scale, 0.0)

time: 246 us -> 246 us (level)
  no operation moved by 1% of the time
where the time goes in v5:
time: 246 us; the launch traced here: 245 us
  waiting for transfers between devices  113 us (46%)
  starting transfers between devices  57.7 us (23%)
  Pallas kernels  42.6 us (17%)
  local copies, waits for them, and re-layouts  23.8 us (10%)
  other arithmetic  7.1 us (3%)
    ppermute x9, waiting for transfers between devices, swap_far(): return lax.ppermute(x, ('ka', 'ga'), pairs)  67 us
    all_to_all x6, waiting for transfers between devices, turn(): lax.all_to_all(x, 'ga', 0, 0, axis_index_groups=same_core, tiled=True)  43.3 us
    all_to_all x6, starting transfers between devices, turn(): lax.all_to_all(x, 'ga', 0, 0, axis_index_groups=same_core, tiled=True)  27.6 us
    ppermute x9, starting transfers between devices, swap_far(): return lax.ppermute(x, ('ka', 'ga'), pairs)  22.6 us
    pallas_call x3, Pallas kernels, local_terms(): pl.pallas_call(kernel, grid=(32 // step,), in_specs=specs, out_specs=whol...  19.8 us
    unnamed x57, local copies, waits for them, and re-layouts  15.8 us
    pallas_call x3, Pallas kernels, radial_term(): pl.pallas_call(kernel, grid=(2,), in_specs=[pl.BlockSpec(memory_space=plt...  12.8 us
    ppermute x8, starting transfers between devices, swap_core(): return lax.ppermute(x, 'ga', [(g, g ^ 1) for g in range(members)])  7.45 us
  transfers between devices with their start and end apart: 23, of which 16 were waited for; matrix products, arithmetic and copies ran while one was open for 5% of the time, Pallas kernels for 15%

profile of v5, /device:TPU:1, one launch (start us, length us, event | category | flops | bytes accessed | tf_op | source)
XLA Modules:
  0.0 245.0 jit_solution(5872900515154486102)
XLA Ops:
  0.7 2.4 dynamic-slice_bitcast_fusion
  3.1 3.2 %collective-permute-start.1 = (f32[16,64,256]{2,1,0:T(8,128)}, f32[16,64,256]{2,1,0:T(8,128)S(1)}, u32[]{:S(2)}, u32[]{:S(2)}) collective-permute-start(f32[16,64,256]{2,1,0:T(8,128)} %dynamic-slice_bitcast_fusion), channel_id=1, source_target_pairs={{0,1},{1,0},{2,3},{3,2},{4,5},{5,4},{6,7},{7,6},{8,9},{9,8},{10,11... | collective-permute-start | bytes 3145736 | tf_op jit(solution)/shard_map/ppermute | solution.py:218
  10.6 2.5 %start.1.cur.rest_0_ = f32[8,32,8,256]{3,2,1,0:T(8,128)} custom-call(s32[2]{0:T(128)S(1)} %pad_add_fusion.ids, s32[2,256]{1,0:T(2,128)S(1)} %copy-done.18, f32[2,16,64,256]{3,2,1,0:T(8,128)S(1)} %copy-done.9, f32[16,64,256]{2,1,0:T(8,128)S(1)} %collective-permute-done.1.other), custom_call_target="tpu_custom_call" | custom-call | tf_op jit(solution)/shard_map/start/pallas_call | solution.py:76
  13.1 5.0 %all-to-all-start = ((f32[8,32,8,256]{3,2,1,0:T(8,128)}), f32[8,32,8,256]{3,2,1,0:T(8,128)}, u32[]{:S(2)}, u32[]{:S(2)}) async-start(f32[8,32,8,256]{3,2,1,0:T(8,128)} %start.1.cur.rest_0_), calls=%async_computation | async-start | bytes 4194304 | tf_op jit(solution)/shard_map/all_to_all | solution.py:240
  18.4 3.7 %collective-permute-start.2 = (f32[3,32,8,256]{3,2,1,0:T(8,128)S(1)}, f32[3,32,8,256]{3,2,1,0:T(8,128)S(1)}, u32[]{:S(2)}, u32[]{:S(2)}) collective-permute-start(f32[3,32,8,256]{3,2,1,0:T(8,128)S(1)} %get-tuple-element.65), channel_id=1, source_target_pairs={{1,16},{3,18},{5,20},{7,22},{9,24},{11,26},{13,28},{15,30},{16,1},... | collective-permute-start | bytes 2359304 | tf_op jit(solution)/shard_map/ppermute | solution.py:228
  22.1 1.9 collective-permute-start.3
  24.9 7.3 %collective-permute-done.2.far = f32[3,32,8,256]{3,2,1,0:T(8,128)S(1)} collective-permute-done((f32[3,32,8,256]{3,2,1,0:T(8,128)S(1)}, f32[3,32,8,256]{3,2,1,0:T(8,128)S(1)}, u32[]{:S(2)}, u32[]{:S(2)}) %collective-permute-start.2) | collective-permute-done | bytes 786464 | tf_op jit(solution)/shard_map/ppermute | solution.py:228
  32.1 8.4 %collective-permute-done.3.far_top = f32[3,32,8,256]{3,2,1,0:T(8,128)S(1)} collective-permute-done((f32[3,32,8,256]{3,2,1,0:T(8,128)S(1)}, f32[3,32,8,256]{3,2,1,0:T(8,128)S(1)}, u32[]{:S(2)}, u32[]{:S(2)}) %collective-permute-start.3) | collective-permute-done | bytes 786464 | tf_op jit(solution)/shard_map/ppermute | solution.py:228
  41.5 11.4 %all-to-all-done = f32[8,32,8,256]{3,2,1,0:T(8,128)} async-done(((f32[8,32,8,256]{3,2,1,0:T(8,128)}), f32[8,32,8,256]{3,2,1,0:T(8,128)}, u32[]{:S(2)}, u32[]{:S(2)}) %all-to-all-start) | async-done | bytes 2097184 | tf_op jit(solution)/shard_map/all_to_all | solution.py:240
  54.0 3.8 %radial_term.3.refs_1_ = f32[2048,256]{1,0:T(8,128)} custom-call(s32[2]{0:T(128)} %copy-done.20, f32[256,128]{1,0:T(8,128)} %copy-done.25, bf16[2,256,256]{2,1,0:T(8,128)(2,1)} %copy-done.24, f32[2048,256]{1,0:T(8,128)} %bitcast.5.refs_0_), custom_call_target="tpu_custom_call" | custom-call | flops 2000000000 | bytes 5000000 | tf_op jit(solution)/shard_map/radial_term/pallas_call | solution.py:169
  57.8 4.5 %all-to-all-start.1 = ((f32[8,32,8,256]{3,2,1,0:T(8,128)}), f32[8,32,8,256]{3,2,1,0:T(8,128)}, u32[]{:S(2)}, u32[]{:S(2)}) async-start(f32[8,32,8,256]{3,2,1,0:T(8,128)} %bitcast.12), calls=%async_computation.1 | async-start | bytes 4194304 | tf_op jit(solution)/shard_map/all_to_all | solution.py:240
  62.4 1.9 collective-permute-start.5
  64.6 2.3 constant_dynamic-update-slice_fusion.1
  66.9 2.4 constant_dynamic-update-slice_fusion.pot
  69.3 4.2 %collective-permute-done.5.far_mid = f32[2,32,8,256]{3,2,1,0:T(8,128)} collective-permute-done((f32[2,32,8,256]{3,2,1,0:T(8,128)}, f32[2,32,8,256]{3,2,1,0:T(8,128)}, u32[]{:S(2)}, u32[]{:S(2)}) %collective-permute-start.5) | collective-permute-done | bytes 524320 | tf_op jit(solution)/shard_map/ppermute | solution.py:228
  75.1 6.9 %local_terms.3 = f32[8,32,8,256]{3,2,1,0:T(8,128)} custom-call(s32[2]{0:T(128)S(1)} %copy-done.21, s32[2,256]{1,0:T(2,128)S(1)} %copy-done.18, f32[34]{0:T(128)S(1)} %pad_maximum_fusion.coef, f32[8,32,8,256]{3,2,1,0:T(8,128)S(1)} %copy-done, f32[8,32,8,256]{3,2,1,0:T(8,128)} %collective-permute-done.4.near, ...), custom_call_target="tpu_custom_call" | custom-call | flops 2000000000 | bytes 14000000 | tf_op jit(solution)/shard_map/local_terms/pallas_call | solution.py:134
  82.0 13.3 %all-to-all-done.1 = f32[8,32,8,256]{3,2,1,0:T(8,128)} async-done(((f32[8,32,8,256]{3,2,1,0:T(8,128)}), f32[8,32,8,256]{3,2,1,0:T(8,128)}, u32[]{:S(2)}, u32[]{:S(2)}) %all-to-all-start.1) | async-done | bytes 2097184 | tf_op jit(solution)/shard_map/all_to_all | solution.py:240
  95.3 4.4 %all-to-all-start.2 = ((f32[8,32,8,256]{3,2,1,0:T(8,128)}), f32[8,32,8,256]{3,2,1,0:T(8,128)}, u32[]{:S(2)}, u32[]{:S(2)}) async-start(f32[8,32,8,256]{3,2,1,0:T(8,128)} %local_terms.3), calls=%async_computation.2 | async-start | bytes 4194304 | tf_op jit(solution)/shard_map/all_to_all | solution.py:240
  99.7 2.6 %add.30.cur.rest_0_ = f32[8,32,8,256]{3,2,1,0:T(8,128)S(1)} add(f32[8,32,8,256]{3,2,1,0:T(8,128)} %local_terms.3, f32[8,32,8,256]{3,2,1,0:T(8,128)} %all-to-all-done.1) | non-fusion elementwise | flops 524288 | bytes 6291456 | tf_op jit(solution)/shard_map/add | solution.py:264
  102.5 1.9 collective-permute-start.7
  104.4 3.6 %collective-permute-start.8 = (f32[3,32,8,256]{3,2,1,0:T(8,128)S(1)}, f32[3,32,8,256]{3,2,1,0:T(8,128)S(1)}, u32[]{:S(2)}, u32[]{:S(2)}) collective-permute-start(f32[3,32,8,256]{3,2,1,0:T(8,128)S(1)} %get-tuple-element.62), channel_id=1, source_target_pairs={{1,16},{3,18},{5,20},{7,22},{9,24},{11,26},{13,28},{15,30},{16,1},... | collective-permute-start | bytes 2359304 | tf_op jit(solution)/shard_map/ppermute | solution.py:228
  108.9 6.9 %collective-permute-done.7.far = f32[3,32,8,256]{3,2,1,0:T(8,128)S(1)} collective-permute-done((f32[3,32,8,256]{3,2,1,0:T(8,128)S(1)}, f32[3,32,8,256]{3,2,1,0:T(8,128)S(1)}, u32[]{:S(2)}, u32[]{:S(2)}) %collective-permute-start.7) | collective-permute-done | bytes 786464 | tf_op jit(solution)/shard_map/ppermute | solution.py:228
  115.8 8.8 %collective-permute-done.8.far_top = f32[3,32,8,256]{3,2,1,0:T(8,128)S(1)} collective-permute-done((f32[3,32,8,256]{3,2,1,0:T(8,128)S(1)}, f32[3,32,8,256]{3,2,1,0:T(8,128)S(1)}, u32[]{:S(2)}, u32[]{:S(2)}) %collective-permute-start.8) | collective-permute-done | bytes 786464 | tf_op jit(solution)/shard_map/ppermute | solution.py:228
  125.5 5.6 %all-to-all-done.2 = f32[8,32,8,256]{3,2,1,0:T(8,128)} async-done(((f32[8,32,8,256]{3,2,1,0:T(8,128)}), f32[8,32,8,256]{3,2,1,0:T(8,128)}, u32[]{:S(2)}, u32[]{:S(2)}) %all-to-all-start.2) | async-done | bytes 2097184 | tf_op jit(solution)/shard_map/all_to_all | solution.py:240
  131.6 4.5 %radial_term.4.refs_1_ = f32[2048,256]{1,0:T(8,128)} custom-call(s32[2]{0:T(128)} %copy-done.20, f32[256,128]{1,0:T(8,128)} %copy-done.25, bf16[2,256,256]{2,1,0:T(8,128)(2,1)} %copy-done.24, f32[2048,256]{1,0:T(8,128)} %bitcast.7.refs_0_, f32[2048,256]{1,0:T(8,128)} %radial_term.3.refs_1_), custom_call_target="tpu_custom_call" | custom-call | flops 2000000000 | bytes 5000000 | tf_op jit(solution)/shard_map/radial_term/pallas_call | solution.py:169
  136.1 4.5 %all-to-all-start.3 = ((f32[8,32,8,256]{3,2,1,0:T(8,128)}), f32[8,32,8,256]{3,2,1,0:T(8,128)}, u32[]{:S(2)}, u32[]{:S(2)}) async-start(f32[8,32,8,256]{3,2,1,0:T(8,128)} %bitcast.13), calls=%async_computation.3 | async-start | bytes 4194304 | tf_op jit(solution)/shard_map/all_to_all | solution.py:240
  140.6 1.9 collective-permute-start.10
  142.5 9.2 %collective-permute-done.10.far_mid = f32[2,32,8,256]{3,2,1,0:T(8,128)S(1)} collective-permute-done((f32[2,32,8,256]{3,2,1,0:T(8,128)}, f32[2,32,8,256]{3,2,1,0:T(8,128)S(1)}, u32[]{:S(2)}, u32[]{:S(2)}) %collective-permute-start.10) | collective-permute-done | bytes 524320 | tf_op jit(solution)/shard_map/ppermute | solution.py:228
  153.3 1.6 copy-done.5
  156.1 6.9 %local_terms.4 = f32[8,32,8,256]{3,2,1,0:T(8,128)} custom-call(s32[2]{0:T(128)S(1)} %copy-done.22, s32[2,256]{1,0:T(2,128)S(1)} %copy-done.18, f32[34]{0:T(128)S(1)} %pad_maximum_fusion.coef, f32[8,32,8,256]{3,2,1,0:T(8,128)S(1)} %copy-done.2, f32[8,32,8,256]{3,2,1,0:T(8,128)} %collective-permute-done.9.near, ...), custom_call_target="tpu_custom_call" | custom-call | flops 2000000000 | bytes 14000000 | tf_op jit(solution)/shard_map/local_terms/pallas_call | solution.py:134
  162.9 4.2 %all-to-all-done.3 = f32[8,32,8,256]{3,2,1,0:T(8,128)} async-done(((f32[8,32,8,256]{3,2,1,0:T(8,128)}), f32[8,32,8,256]{3,2,1,0:T(8,128)}, u32[]{:S(2)}, u32[]{:S(2)}) %all-to-all-start.3) | async-done | bytes 2097184 | tf_op jit(solution)/shard_map/all_to_all | solution.py:240
  167.1 4.9 %all-to-all-start.4 = ((f32[8,32,8,256]{3,2,1,0:T(8,128)}), f32[8,32,8,256]{3,2,1,0:T(8,128)}, u32[]{:S(2)}, u32[]{:S(2)}) async-start(f32[8,32,8,256]{3,2,1,0:T(8,128)} %local_terms.4), calls=%async_computation.4 | async-start | bytes 4194304 | tf_op jit(solution)/shard_map/all_to_all | solution.py:240
  172.0 2.6 %add.31.cur.own = f32[8,32,8,256]{3,2,1,0:T(8,128)S(1)} add(f32[8,32,8,256]{3,2,1,0:T(8,128)} %local_terms.4, f32[8,32,8,256]{3,2,1,0:T(8,128)} %all-to-all-done.3) | non-fusion elementwise | flops 524288 | bytes 6291456 | tf_op jit(solution)/shard_map/add | solution.py:268
  174.8 1.9 collective-permute-start.11
  176.7 3.6 %collective-permute-start.12 = (f32[3,32,8,256]{3,2,1,0:T(8,128)S(1)}, f32[3,32,8,256]{3,2,1,0:T(8,128)S(1)}, u32[]{:S(2)}, u32[]{:S(2)}) collective-permute-start(f32[3,32,8,256]{3,2,1,0:T(8,128)S(1)} %get-tuple-element.60), channel_id=1, source_target_pairs={{1,16},{3,18},{5,20},{7,22},{9,24},{11,26},{13,28},{15,30},{16,1},... | collective-permute-start | bytes 2359304 | tf_op jit(solution)/shard_map/ppermute | solution.py:228
  181.2 7.3 %collective-permute-done.11.far = f32[3,32,8,256]{3,2,1,0:T(8,128)S(1)} collective-permute-done((f32[3,32,8,256]{3,2,1,0:T(8,128)S(1)}, f32[3,32,8,256]{3,2,1,0:T(8,128)S(1)}, u32[]{:S(2)}, u32[]{:S(2)}) %collective-permute-start.11) | collective-permute-done | bytes 786464 | tf_op jit(solution)/shard_map/ppermute | solution.py:228
  188.5 8.4 %collective-permute-done.12.far_top = f32[3,32,8,256]{3,2,1,0:T(8,128)S(1)} collective-permute-done((f32[3,32,8,256]{3,2,1,0:T(8,128)S(1)}, f32[3,32,8,256]{3,2,1,0:T(8,128)S(1)}, u32[]{:S(2)}, u32[]{:S(2)}) %collective-permute-start.12) | collective-permute-done | bytes 786464 | tf_op jit(solution)/shard_map/ppermute | solution.py:228
  197.8 1.8 all-to-all-done.4
  200.4 4.5 %radial_term.5 = f32[2048,256]{1,0:T(8,128)} custom-call(s32[2]{0:T(128)} %copy-done.20, f32[256,128]{1,0:T(8,128)} %copy-done.25, bf16[2,256,256]{2,1,0:T(8,128)(2,1)} %copy-done.24, f32[2048,256]{1,0:T(8,128)} %bitcast.9.refs_0_, f32[2048,256]{1,0:T(8,128)} %radial_term.4.refs_1_), custom_call_target="tpu_custom_call" | custom-call | flops 2000000000 | bytes 5000000 | tf_op jit(solution)/shard_map/radial_term/pallas_call | solution.py:169
  204.9 4.3 %all-to-all-start.5 = ((f32[8,32,8,256]{3,2,1,0:T(8,128)}), f32[8,32,8,256]{3,2,1,0:T(8,128)}, u32[]{:S(2)}, u32[]{:S(2)}) async-start(f32[8,32,8,256]{3,2,1,0:T(8,128)} %bitcast.14), calls=%async_computation.5 | async-start | bytes 4194304 | tf_op jit(solution)/shard_map/all_to_all | solution.py:240
  210.3 2.0 collective-permute-start.14
  212.3 2.5 %finish.2 = f32[2,16,64,256]{3,2,1,0:T(8,128)} custom-call(s32[2]{0:T(128)S(1)} %copy-done.23, f32[8,32,8,256]{3,2,1,0:T(8,128)S(1)} %add.31.cur.own, f32[8,16,8,256]{3,2,1,0:T(8,128)S(1)} %collective-permute-done.15.other), custom_call_target="tpu_custom_call" | custom-call | tf_op jit(solution)/shard_map/finish/pallas_call | solution.py:195
  214.8 6.5 %collective-permute-done.14.far_mid = f32[2,32,8,256]{3,2,1,0:T(8,128)S(1)} collective-permute-done((f32[2,32,8,256]{3,2,1,0:T(8,128)S(1)}, f32[2,32,8,256]{3,2,1,0:T(8,128)S(1)}, u32[]{:S(2)}, u32[]{:S(2)}) %collective-permute-start.14) | collective-permute-done | bytes 524320 | tf_op jit(solution)/shard_map/ppermute | solution.py:228
  221.3 6.0 %local_terms.5.own = f32[8,32,8,256]{3,2,1,0:T(8,128)S(1)} custom-call(s32[2]{0:T(128)S(1)} %copy-done.23, s32[2,256]{1,0:T(2,128)S(1)} %copy-done.18, f32[34]{0:T(128)S(1)} %pad_maximum_fusion.coef, f32[8,32,8,256]{3,2,1,0:T(8,128)S(1)} %add.31.cur.own, f32[8,32,8,256]{3,2,1,0:T(8,128)} %collective-permute-done.13.near, ...), custom_call_target="tpu_custom_call" | custom-call | flops 2000000000 | bytes 14000000 | tf_op jit(solution)/shard_map/local_terms/pallas_call | solution.py:134
  228.6 7.0 %all-to-all-done.5.rest_0_ = f32[8,32,8,256]{3,2,1,0:T(8,128)} async-done(((f32[8,32,8,256]{3,2,1,0:T(8,128)}), f32[8,32,8,256]{3,2,1,0:T(8,128)}, u32[]{:S(2)}, u32[]{:S(2)}) %all-to-all-start.5) | async-done | bytes 2097184 | tf_op jit(solution)/shard_map/all_to_all | solution.py:240
  235.6 1.8 slice_add_fusion
  238.5 2.3 collective-permute-done.16.other
  240.8 4.2 %finish.3 = f32[2,16,64,256]{3,2,1,0:T(8,128)} custom-call(s32[2]{0:T(128)S(1)} %copy-done.23, f32[8,32,8,256]{3,2,1,0:T(8,128)S(1)} %copy-done.8, f32[8,16,8,256]{3,2,1,0:T(8,128)S(1)} %collective-permute-done.16.other, f32[8,32,8,256]{3,2,1,0:T(8,128)} %all-to-all-done.5.rest_0_), custom_call_target="tpu_custom_call" | custom-call | tf_op jit(solution)/shard_map/finish/pallas_call | solution.py:195
  (79 shorter events, 20.3 us)
Async XLA Ops:
  0.6 9.9 %copy-start.9 = (f32[2,16,64,256]{3,2,1,0:T(8,128)S(1)}, f32[2,16,64,256]{3,2,1,0:T(8,128)}, u32[]{:S(2)}) copy-start(f32[2,16,64,256]{3,2,1,0:T(8,128)} %own.1) | copy-start | bytes 6291460
  0.6 5.8 %copy-start.19 = (f32[64,64]{1,0:T(8,128)S(1)}, f32[64,64]{1,0:T(8,128)}, u32[]{:S(2)}) copy-start(f32[64,64]{1,0:T(8,128)} %bond.1) | copy-start | bytes 49156
  0.6 5.8 %copy-start.18 = (s32[2,256]{1,0:T(2,128)S(1)}, s32[2,256]{1,0:T(2,128)}, u32[]{:S(2)}) copy-start(s32[2,256]{1,0:T(2,128)} %ext.7) | copy-start | bytes 6148
  3.1 7.4 %collective-permute-start.1 = (f32[16,64,256]{2,1,0:T(8,128)}, f32[16,64,256]{2,1,0:T(8,128)S(1)}, u32[]{:S(2)}, u32[]{:S(2)}) collective-permute-start(f32[16,64,256]{2,1,0:T(8,128)} %dynamic-slice_bitcast_fusion), channel_id=1, source_target_pairs={{0,1},{1,0},{2,3},{3,2},{4,5},{5,4},{6,7},{7,6},{8,9},{9,8},{10,11... | collective-permute-start | bytes 3145736 | tf_op jit(solution)/shard_map/ppermute | solution.py:218
  6.4 1.0 copy-start.16
  7.4 0.9 copy-start.17
  8.3 4.8 %copy-start.20 = (s32[2]{0:T(128)}, s32[2]{0:T(128)S(1)}, u32[]{:S(2)}) copy-start(s32[2]{0:T(128)S(1)} %pad_add_fusion.ids) | copy-start | bytes 28
  13.1 5.1 %copy-start = (f32[8,32,8,256]{3,2,1,0:T(8,128)S(1)}, f32[8,32,8,256]{3,2,1,0:T(8,128)}, u32[]{:S(2)}) copy-start(f32[8,32,8,256]{3,2,1,0:T(8,128)} %start.1.cur.rest_0_) | copy-start | bytes 6291460
  13.1 39.8 %all-to-all-start = ((f32[8,32,8,256]{3,2,1,0:T(8,128)}), f32[8,32,8,256]{3,2,1,0:T(8,128)}, u32[]{:S(2)}, u32[]{:S(2)}) async-start(f32[8,32,8,256]{3,2,1,0:T(8,128)} %start.1.cur.rest_0_), calls=%async_computation | async-start | bytes 4194304 | tf_op jit(solution)/shard_map/all_to_all | solution.py:240
  18.4 13.8 %collective-permute-start.2 = (f32[3,32,8,256]{3,2,1,0:T(8,128)S(1)}, f32[3,32,8,256]{3,2,1,0:T(8,128)S(1)}, u32[]{:S(2)}, u32[]{:S(2)}) collective-permute-start(f32[3,32,8,256]{3,2,1,0:T(8,128)S(1)} %get-tuple-element.65), channel_id=1, source_target_pairs={{1,16},{3,18},{5,20},{7,22},{9,24},{11,26},{13,28},{15,30},{16,1},... | collective-permute-start | bytes 2359304 | tf_op jit(solution)/shard_map/ppermute | solution.py:228
  22.1 18.5 %collective-permute-start.3 = (f32[3,32,8,256]{3,2,1,0:T(8,128)S(1)}, f32[3,32,8,256]{3,2,1,0:T(8,128)S(1)}, u32[]{:S(2)}, u32[]{:S(2)}) collective-permute-start(f32[3,32,8,256]{3,2,1,0:T(8,128)S(1)} %get-tuple-element.64), channel_id=1, source_target_pairs={{1,16},{3,18},{5,20},{7,22},{9,24},{11,26},{13,28},{15,30},{16,1},... | collective-permute-start | bytes 2359304 | tf_op jit(solution)/shard_map/ppermute | solution.py:228
  40.6 0.9 copy-start.10
  52.9 20.6 %collective-permute-start.4 = (f32[8,32,8,256]{3,2,1,0:T(8,128)S(1)}, f32[8,32,8,256]{3,2,1,0:T(8,128)}, u32[]{:S(2)}, u32[]{:S(2)}) collective-permute-start(f32[8,32,8,256]{3,2,1,0:T(8,128)S(1)} %copy-done), channel_id=1, source_target_pairs={{0,1},{1,0},{2,3},{3,2},{4,5},{5,4},{6,7},{7,6},{8,9},{9,8},{10,11... | collective-permute-start | bytes 6291464 | tf_op jit(solution)/shard_map/ppermute | solution.py:218
  57.8 6.5 %copy-start.27 = (f32[16]{0:T(128)S(1)}, f32[16]{0:T(128)}, u32[]{:S(2)}) copy-start(f32[16]{0:T(128)} %param.10) | copy-start | bytes 196
  57.8 37.5 %all-to-all-start.1 = ((f32[8,32,8,256]{3,2,1,0:T(8,128)}), f32[8,32,8,256]{3,2,1,0:T(8,128)}, u32[]{:S(2)}, u32[]{:S(2)}) async-start(f32[8,32,8,256]{3,2,1,0:T(8,128)} %bitcast.12), calls=%async_computation.1 | async-start | bytes 4194304 | tf_op jit(solution)/shard_map/all_to_all | solution.py:240
  62.3 4.6 %collective-permute-start.6 = (f32[16,64,256]{2,1,0:T(8,128)}, f32[16,64,256]{2,1,0:T(8,128)}, u32[]{:S(2)}, u32[]{:S(2)}) collective-permute-start(f32[16,64,256]{2,1,0:T(8,128)} %param.9), channel_id=1, source_target_pairs={{0,1},{1,0},{2,3},{3,2},{4,5},{5,4},{6,7},{7,6},{8,9},{9,8},{10,11... | collective-permute-start | bytes 3145736 | tf_op jit(solution)/shard_map/ppermute | solution.py:218
  62.4 11.1 %collective-permute-start.5 = (f32[2,32,8,256]{3,2,1,0:T(8,128)}, f32[2,32,8,256]{3,2,1,0:T(8,128)}, u32[]{:S(2)}, u32[]{:S(2)}) collective-permute-start(f32[2,32,8,256]{3,2,1,0:T(8,128)} %slice.48), channel_id=1, source_target_pairs={{1,16},{3,18},{5,20},{7,22},{9,24},{11,26},{13,28},{15,30},{16,1},... | collective-permute-start | bytes 1572872 | tf_op jit(solution)/shard_map/ppermute | solution.py:228
  64.3 2.5 %collective-permute-start = (f32[16]{0:T(128)S(1)}, f32[16]{0:T(128)S(1)}, u32[]{:S(2)}, u32[]{:S(2)}) collective-permute-start(f32[16]{0:T(128)S(1)} %copy-done.27), channel_id=1, source_target_pairs={{0,1},{1,0},{2,3},{3,2},{4,5},{5,4},{6,7},{7,6},{8,9},{9,8},{10,11... | collective-permute-start | bytes 200 | tf_op jit(solution)/shard_map/ppermute | solution.py:218
  64.6 9.0 %copy-start.21 = (s32[2]{0:T(128)S(1)}, s32[2]{0:T(128)}, u32[]{:S(2)}) copy-start(s32[2]{0:T(128)} %copy-done.20) | copy-start | bytes 28
  66.9 6.7 %copy-start.11 = (f32[3,32,8,256]{3,2,1,0:T(8,128)S(1)}, f32[3,32,8,256]{3,2,1,0:T(8,128)}, u32[]{:S(2)}) copy-start(f32[3,32,8,256]{3,2,1,0:T(8,128)} %copy-done.10) | copy-start | bytes 2359300
  73.5 1.6 copy-start.4
  95.3 35.8 %all-to-all-start.2 = ((f32[8,32,8,256]{3,2,1,0:T(8,128)}), f32[8,32,8,256]{3,2,1,0:T(8,128)}, u32[]{:S(2)}, u32[]{:S(2)}) async-start(f32[8,32,8,256]{3,2,1,0:T(8,128)} %local_terms.3), calls=%async_computation.2 | async-start | bytes 4194304 | tf_op jit(solution)/shard_map/all_to_all | solution.py:240
  102.3 6.6 %copy-start.1 = (f32[8,32,8,256]{3,2,1,0:T(8,128)}, f32[8,32,8,256]{3,2,1,0:T(8,128)S(1)}, u32[]{:S(2)}) copy-start(f32[8,32,8,256]{3,2,1,0:T(8,128)S(1)} %add.30.cur.rest_0_) | copy-start | bytes 6291460
  102.5 13.3 %collective-permute-start.7 = (f32[3,32,8,256]{3,2,1,0:T(8,128)S(1)}, f32[3,32,8,256]{3,2,1,0:T(8,128)S(1)}, u32[]{:S(2)}, u32[]{:S(2)}) collective-permute-start(f32[3,32,8,256]{3,2,1,0:T(8,128)S(1)} %get-tuple-element.63), channel_id=1, source_target_pairs={{1,16},{3,18},{5,20},{7,22},{9,24},{11,26},{13,28},{15,30},{16,1},... | collective-permute-start | bytes 2359304 | tf_op jit(solution)/shard_map/ppermute | solution.py:228
  104.4 20.2 %collective-permute-start.8 = (f32[3,32,8,256]{3,2,1,0:T(8,128)S(1)}, f32[3,32,8,256]{3,2,1,0:T(8,128)S(1)}, u32[]{:S(2)}, u32[]{:S(2)}) collective-permute-start(f32[3,32,8,256]{3,2,1,0:T(8,128)S(1)} %get-tuple-element.62), channel_id=1, source_target_pairs={{1,16},{3,18},{5,20},{7,22},{9,24},{11,26},{13,28},{15,30},{16,1},... | collective-permute-start | bytes 2359304 | tf_op jit(solution)/shard_map/ppermute | solution.py:228
  124.6 0.9 copy-start.14
  131.1 20.7 %collective-permute-start.9 = (f32[8,32,8,256]{3,2,1,0:T(8,128)}, f32[8,32,8,256]{3,2,1,0:T(8,128)}, u32[]{:S(2)}, u32[]{:S(2)}) collective-permute-start(f32[8,32,8,256]{3,2,1,0:T(8,128)} %copy-done.1), channel_id=1, source_target_pairs={{0,1},{1,0},{2,3},{3,2},{4,5},{5,4},{6,7},{7,6},{8,9},{9,8},{10,11... | collective-permute-start | bytes 6291464 | tf_op jit(solution)/shard_map/ppermute | solution.py:218
  136.1 15.6 %copy-start.22 = (s32[2]{0:T(128)S(1)}, s32[2]{0:T(128)}, u32[]{:S(2)}) copy-start(s32[2]{0:T(128)} %copy-done.20) | copy-start | bytes 28
  136.1 31.0 %all-to-all-start.3 = ((f32[8,32,8,256]{3,2,1,0:T(8,128)}), f32[8,32,8,256]{3,2,1,0:T(8,128)}, u32[]{:S(2)}, u32[]{:S(2)}) async-start(f32[8,32,8,256]{3,2,1,0:T(8,128)} %bitcast.13), calls=%async_computation.3 | async-start | bytes 4194304 | tf_op jit(solution)/shard_map/all_to_all | solution.py:240
  140.6 11.1 %collective-permute-start.10 = (f32[2,32,8,256]{3,2,1,0:T(8,128)}, f32[2,32,8,256]{3,2,1,0:T(8,128)S(1)}, u32[]{:S(2)}, u32[]{:S(2)}) collective-permute-start(f32[2,32,8,256]{3,2,1,0:T(8,128)} %slice.51), channel_id=1, source_target_pairs={{1,16},{3,18},{5,20},{7,22},{9,24},{11,26},{13,28},{15,30},{16,1},... | collective-permute-start | bytes 1572872 | tf_op jit(solution)/shard_map/ppermute | solution.py:228
  151.7 1.6 copy-start.2
  153.3 1.6 copy-start.5
  154.9 1.1 copy-start.15
  167.1 32.5 %all-to-all-start.4 = ((f32[8,32,8,256]{3,2,1,0:T(8,128)}), f32[8,32,8,256]{3,2,1,0:T(8,128)}, u32[]{:S(2)}, u32[]{:S(2)}) async-start(f32[8,32,8,256]{3,2,1,0:T(8,128)} %local_terms.4), calls=%async_computation.4 | async-start | bytes 4194304 | tf_op jit(solution)/shard_map/all_to_all | solution.py:240
  174.8 13.7 %collective-permute-start.11 = (f32[3,32,8,256]{3,2,1,0:T(8,128)S(1)}, f32[3,32,8,256]{3,2,1,0:T(8,128)S(1)}, u32[]{:S(2)}, u32[]{:S(2)}) collective-permute-start(f32[3,32,8,256]{3,2,1,0:T(8,128)S(1)} %get-tuple-element.61), channel_id=1, source_target_pairs={{1,16},{3,18},{5,20},{7,22},{9,24},{11,26},{13,28},{15,30},{16,1},... | collective-permute-start | bytes 2359304 | tf_op jit(solution)/shard_map/ppermute | solution.py:228
  176.7 20.2 %collective-permute-start.12 = (f32[3,32,8,256]{3,2,1,0:T(8,128)S(1)}, f32[3,32,8,256]{3,2,1,0:T(8,128)S(1)}, u32[]{:S(2)}, u32[]{:S(2)}) collective-permute-start(f32[3,32,8,256]{3,2,1,0:T(8,128)S(1)} %get-tuple-element.60), channel_id=1, source_target_pairs={{1,16},{3,18},{5,20},{7,22},{9,24},{11,26},{13,28},{15,30},{16,1},... | collective-permute-start | bytes 2359304 | tf_op jit(solution)/shard_map/ppermute | solution.py:228
  199.6 21.7 %collective-permute-start.13 = (f32[8,32,8,256]{3,2,1,0:T(8,128)S(1)}, f32[8,32,8,256]{3,2,1,0:T(8,128)}, u32[]{:S(2)}, u32[]{:S(2)}) collective-permute-start(f32[8,32,8,256]{3,2,1,0:T(8,128)S(1)} %add.31.cur.own), channel_id=1, source_target_pairs={{0,1},{1,0},{2,3},{3,2},{4,5},{5,4},{6,7},{7,6},{8,9},{9,8},{10,11... | collective-permute-start | bytes 6291464 | tf_op jit(solution)/shard_map/ppermute | solution.py:218
  204.9 30.8 %all-to-all-start.5 = ((f32[8,32,8,256]{3,2,1,0:T(8,128)}), f32[8,32,8,256]{3,2,1,0:T(8,128)}, u32[]{:S(2)}, u32[]{:S(2)}) async-start(f32[8,32,8,256]{3,2,1,0:T(8,128)} %bitcast.14), calls=%async_computation.5 | async-start | bytes 4194304 | tf_op jit(solution)/shard_map/all_to_all | solution.py:240
  209.2 1.0 copy-start.26
  209.2 3.1 %copy-start.23 = (s32[2]{0:T(128)S(1)}, s32[2]{0:T(128)}, u32[]{:S(2)}) copy-start(s32[2]{0:T(128)} %copy-done.20) | copy-start | bytes 28
  209.3 11.9 %copy-start.3 = (f32[8,32,8,256]{3,2,1,0:T(8,128)S(1)}, f32[8,32,8,256]{3,2,1,0:T(8,128)}, u32[]{:S(2)}) copy-start(f32[8,32,8,256]{3,2,1,0:T(8,128)} %copy-done.1) | copy-start | bytes 6291460
  209.4 11.9 %copy-start.6 = (f32[32,64,256]{2,1,0:T(8,128)S(1)}, f32[32,64,256]{2,1,0:T(8,128)}, u32[]{:S(2)}) copy-start(f32[32,64,256]{2,1,0:T(8,128)} %constant_dynamic-update-slice_fusion.pot) | copy-start | bytes 6291460
  209.4 11.9 %copy-start.13 = (f32[3,32,8,256]{3,2,1,0:T(8,128)S(1)}, f32[3,32,8,256]{3,2,1,0:T(8,128)}, u32[]{:S(2)}) copy-start(f32[3,32,8,256]{3,2,1,0:T(8,128)} %copy-done.12) | copy-start | bytes 2359300
  209.4 2.9 %collective-permute-start.15 = (f32[8,16,8,256]{3,2,1,0:T(8,128)S(1)}, f32[8,16,8,256]{3,2,1,0:T(8,128)S(1)}, u32[]{:S(2)}, u32[]{:S(2)}) collective-permute-start(f32[8,16,8,256]{3,2,1,0:T(8,128)S(1)} %slice.57), channel_id=1, source_target_pairs={{0,1},{1,0},{2,3},{3,2},{4,5},{5,4},{6,7},{7,6},{8,9},{9,8},{10,11... | collective-permute-start | bytes 3145736 | tf_op jit(solution)/shard_map/ppermute | solution.py:218
  210.3 11.0 %collective-permute-start.14 = (f32[2,32,8,256]{3,2,1,0:T(8,128)S(1)}, f32[2,32,8,256]{3,2,1,0:T(8,128)S(1)}, u32[]{:S(2)}, u32[]{:S(2)}) collective-permute-start(f32[2,32,8,256]{3,2,1,0:T(8,128)S(1)} %copy-done.26), channel_id=1, source_target_pairs={{1,16},{3,18},{5,20},{7,22},{9,24},{11,26},{13,28},{15,30},{16,1},... | collective-permute-start | bytes 1572872 | tf_op jit(solution)/shard_map/ppermute | solution.py:228
  227.3 1.3 copy-start.7
  235.6 5.2 %copy-start.8 = (f32[8,32,8,256]{3,2,1,0:T(8,128)S(1)}, f32[8,32,8,256]{3,2,1,0:T(8,128)}, u32[]{:S(2)}) copy-start(f32[8,32,8,256]{3,2,1,0:T(8,128)} %copy-done.7) | copy-start | bytes 6291460
  237.5 3.3 %collective-permute-start.16 = (f32[8,16,8,256]{3,2,1,0:T(8,128)S(1)}, f32[8,16,8,256]{3,2,1,0:T(8,128)S(1)}, u32[]{:S(2)}, u32[]{:S(2)}) collective-permute-start(f32[8,16,8,256]{3,2,1,0:T(8,128)S(1)} %slice_add_fusion), channel_id=1, source_target_pairs={{0,1},{1,0},{2,3},{3,2},{4,5},{5,4},{6,7},{7,6},{8,9},{9,8},{10,11... | collective-permute-start | bytes 3145736 | tf_op jit(solution)/shard_map/ppermute | solution.py:218
  (3 other events, 2.2 us)
